TPU v7x, 128 devices: a whole 4x4x4 slice. The times are simulated.
128 devices in a mesh: tm: 32 (over x, z, y_hi), head: 4 (over y_lo, core).
Axes of the slice: x: 4, y: 4 (y_hi: 2, y_lo: 2; y = y_hi * 2 + y_lo), z: 4, core: 2. Of those that a mesh axis runs over, the one named last changes fastest.
Arguments:
- queries: bfloat16 [12288, 2560], P(('tm', 'head')), may hold values from -8 to 8
- keys: bfloat16 [12288, 2560], P(('tm', 'head')), may hold values from -8 to 8
- values: bfloat16 [12288, 2560], P(('tm', 'head')), may hold values from -6 to 6
- w_out: bfloat16 [2560, 5120], P('head'), may hold values from -0.125 to 0.125
- block_mask: int32 [192, 192], replicated, may hold values from 0 to 1, as said below
- frame_map: int32 [32], replicated, may hold values from 0 to 31, each once
Outputs:
- projected: bfloat16 [12288, 5120], P(('tm', 'head'))
Inputs may be any that keep to these rules, and one draw needn't show every extreme that they name: block_mask is 1 where a query block may read a key block; all blocks of a frame may read all blocks of the same frame, and every query block may read the block of the same place in every frame. frame_map is a permutation of the frames.
All inputs are finite; a program needn't handle non-finite values.
Results may differ from a plain program's by a relative error of at most 0.019.
Values may be sent and summed in bfloat16 or wider, within the bound.
No kernel may reach another device: no remote copies, remote signals or barrier semaphores. Data moves between devices by JAX's collectives and lax.ppermute only.
A program may use at most 192 MiB of HBM per device.

v0:
```python
import jax
import jax.numpy as jnp
from jax import lax
from jax.sharding import PartitionSpec as P

HS = 128
BLOCK = 64
FRAME = 384


NEG = -1e30


def frame_update(carry, query_heads, key_frame, value_frame, blocks):
    running_max, running_sum, weighted = carry
    frame_rows, heads_here, head_size = query_heads.shape
    key_heads = key_frame.reshape(frame_rows, heads_here, head_size)
    value_heads = value_frame.reshape(frame_rows, heads_here, head_size)
    scores = jnp.einsum(
        "qhd,khd->hqk", query_heads, key_heads, preferred_element_type=jnp.float32
    ) * head_size ** (-0.5)
    frame_blocks = blocks.shape[0]
    block_rows = frame_rows // frame_blocks
    allowed = jnp.broadcast_to(
        blocks[:, None, :, None] > 0, (frame_blocks, block_rows, frame_blocks, block_rows)
    ).reshape(frame_rows, frame_rows)
    scores = jnp.where(allowed[None], scores, NEG)
    new_max = jnp.maximum(running_max, jnp.max(scores, axis=-1))
    weights = jnp.where(allowed[None], jnp.exp(scores - new_max[:, :, None]), 0.0)
    factor = jnp.exp(running_max - new_max)
    running_sum = running_sum * factor + jnp.sum(weights, axis=-1)
    update = jnp.einsum(
        "hqk,khd->qhd",
        weights.astype(jnp.bfloat16),
        value_heads,
        preferred_element_type=jnp.float32,
    )
    weighted = weighted * jnp.transpose(factor)[:, :, None] + update
    return (new_max, running_sum, weighted)


def local(queries, keys, values, w_out, block_mask, frame_map):
    group_rows = w_out.shape[0]
    heads_here = group_rows // HS
    frame_blocks = FRAME // BLOCK
    own_frame = frame_map[lax.axis_index("tm")]
    mask_rows = lax.dynamic_slice_in_dim(block_mask, own_frame * frame_blocks, frame_blocks, 0)

    def column_blocks(device):
        return lax.dynamic_slice_in_dim(
            mask_rows, frame_map[device] * frame_blocks, frame_blocks, 1
        )

    initial = (
        jnp.full((heads_here, FRAME), NEG, jnp.float32),
        jnp.zeros((heads_here, FRAME), jnp.float32),
        jnp.zeros((FRAME, heads_here, HS), jnp.float32),
    )
    query_local, key_local, value_local = (
        lax.all_to_all(queries, "head", split_axis=1, concat_axis=0, tiled=True),
        lax.all_to_all(keys, "head", split_axis=1, concat_axis=0, tiled=True),
        lax.all_to_all(values, "head", split_axis=1, concat_axis=0, tiled=True),
    )
    query_heads = query_local.reshape(FRAME, heads_here, HS)
    key_piece = lax.all_gather(key_local, "tm", axis=0, tiled=True)
    value_piece = lax.all_gather(value_local, "tm", axis=0, tiled=True)
    number = key_piece.shape[0] // FRAME
    key_frames = key_piece.reshape(number, FRAME, key_piece.shape[1])
    value_frames = value_piece.reshape(number, FRAME, value_piece.shape[1])

    def advance(inner, element):
        key_frame, value_frame, offset = element
        return (
            frame_update(inner, query_heads, key_frame, value_frame, column_blocks(offset)),
            None,
        )

    result, unused = lax.scan(
        advance, initial, (key_frames, value_frames, jnp.arange(number, dtype=jnp.int32))
    )
    running_max, running_sum, weighted = result
    attended = (
        (weighted / jnp.transpose(running_sum)[:, :, None])
        .reshape(FRAME, heads_here * HS)
        .astype(jnp.bfloat16)
    )
    return lax.psum_scatter(
        jnp.dot(attended, w_out, preferred_element_type=jnp.float32).astype(jnp.bfloat16),
        "head",
        scatter_dimension=0,
        tiled=True,
    )


def solution(mesh):
    placed = (
        P(("tm", "head"), None),
        P(("tm", "head"), None),
        P(("tm", "head"), None),
        P("head", None),
        P(),
        P(),
    )
    return jax.shard_map(
        local, mesh=mesh, in_specs=placed, out_specs=P(("tm", "head"), None), check_vma=False
    )
```

profile of v0, /device:TPU:0, one launch (start us, length us, event | category | flops | bytes accessed | tf_op | source)
XLA Modules:
  0.0 885.6 jit_solution(9492609133277523)
XLA Ops:
  7.7 11.6 %all_to_all.54 = bf16[96,4,640]{2,0,1:T(8,128)(2,1)} all-to-all(bf16[96,4,640]{2,0,1:T(8,128)(2,1)S(1)} %bitcast.84), channel_id=1, replica_groups=mesh['tm'=32,'head'=4] {'head'}, dimensions={1} | all-to-all | bytes 983040 | tf_op jit(solution)/shard_map/all_to_all | solution.py:61
  20.4 11.6 %all_to_all.55 = bf16[96,4,640]{2,0,1:T(8,128)(2,1)} all-to-all(bf16[96,4,640]{2,0,1:T(8,128)(2,1)S(1)} %bitcast.85), channel_id=1, replica_groups=mesh['tm'=32,'head'=4] {'head'}, dimensions={1} | all-to-all | bytes 983040 | tf_op jit(solution)/shard_map/all_to_all | solution.py:62
  32.9 3.5 all-to-all-start.1
  37.7 7.1 all-to-all-done.1
  46.2 124.6 %all-gather.3.cloned.1.call-done = bf16[12288,640]{1,0:T(8,128)(2,1)} async-done(((bf16[384,640]{1,0:T(8,128)(2,1)}), bf16[12288,640]{1,0:T(8,128)(2,1)}) %all-gather.3.cloned.1.call-update) | async-done | bytes 15728656 | tf_op jit(solution)/shard_map/all_gather | solution.py:65
  170.8 149.6 %all-gather.5.cloned.1.call-done = bf16[12288,640]{1,0:T(8,128)(2,1)} async-done(((bf16[384,640]{1,0:T(8,128)(2,1)}), bf16[12288,640]{1,0:T(8,128)(2,1)}) %all-gather.5.cloned.1.call-update) | async-done | bytes 15728656 | tf_op jit(solution)/shard_map/all_gather | solution.py:66
  320.4 508.2 %while.15 = (s32[]{:T(128)}, f32[5,384]{1,0:T(8,128)S(1)}, f32[5,384]{1,0:T(8,128)S(1)}, f32[384,5,128]{0,2,1:T(8,128)}, s32[32]{0:T(128)S(1)}, /*index=5*/s32[3...) while((s32[]{:T(128)}, f32[5,384]{1,0:T(8,128)S(1)}, ...), condition=%wide.region_3.4_spmd.clone, body=%wide.region_0.3_spmd.clone.sunk | while | flops 387820864 | bytes 17523168 | solution.py:78
  363.7 3.3 fusion.43
  395.4 3.3 fusion.43
  427.2 3.3 fusion.43
  459.0 3.3 fusion.43
  490.8 3.3 fusion.43
  522.6 3.3 fusion.43
  554.4 3.3 fusion.43
  586.1 3.3 fusion.43
  617.9 3.3 fusion.43
  649.7 3.3 fusion.43
  681.5 3.3 fusion.43
  713.3 3.3 fusion.43
  745.1 3.3 fusion.43
  776.9 3.3 fusion.43
  808.6 3.3 fusion.43
  829.9 8.0 convolution_convert_fusion
  838.0 41.1 %reduce-scatter.2.cloned.1.call-done = bf16[96,5120]{1,0:T(8,128)(2,1)} async-done(((bf16[384,5120]{1,0:T(8,128)(2,1)}), bf16[96,5120]{1,0:T(8,128)(2,1)}) %reduce-scatter.2.cloned.1.call-update) | async-done | bytes 983056 | tf_op jit(solution)/shard_map/reduce_scatter | solution.py:87
  (489 shorter events, 382.9 us)
Async XLA Ops:
  6.5 31.2 %copy-start = (s32[192,192]{1,0:T(8,128)S(1)}, s32[192,192]{1,0:T(8,128)}, u32[]{:S(2)}) copy-start(s32[192,192]{1,0:T(8,128)} %param.12) | copy-start | bytes 442372
  6.5 25.5 %copy-start.1 = (bf16[96,2560]{1,0:T(8,128)(2,1)S(1)}, bf16[96,2560]{1,0:T(8,128)(2,1)}, u32[]{:S(2)}) copy-start(bf16[96,2560]{1,0:T(8,128)(2,1)} %param.8) | copy-start | bytes 1474564
  6.5 164.3 %all-gather.3.cloned.1.call-start = ((), (), s32[]{:S(2)}) async-start(), calls=%async_computation.4 | async-start | bytes 16220160 | tf_op jit(solution)/shard_map/all_gather | solution.py:65
  7.7 28.8 %copy-start.2 = (s32[32]{0:T(128)S(1)}, s32[32]{0:T(128)}, u32[]{:S(2)}) copy-start(s32[32]{0:T(128)} %param.13) | copy-start | bytes 388
  19.3 301.1 %all-gather.5.cloned.1.call-start = ((), (), s32[]{:S(2)}) async-start(), calls=%async_computation.5 | async-start | bytes 16220160 | tf_op jit(solution)/shard_map/all_gather | solution.py:66
  32.9 11.9 %all-to-all-start.1 = ((bf16[96,4,640]{2,0,1:T(8,128)(2,1)}), bf16[96,4,640]{2,0,1:T(8,128)(2,1)S(1)}, u32[]{:S(2)}, u32[]{:S(2)}) async-start(bf16[96,4,640]{2,0,1:T(8,128)(2,1)} %bitcast.52), calls=%async_computation.1 | async-start | bytes 983040 | tf_op jit(solution)/shard_map/all_to_all | solution.py:60
  36.4 842.7 %reduce-scatter.2.cloned.1.call-start = ((), (), s32[]{:S(2)}) async-start(), calls=%async_computation.6 | async-start | bytes 4915200 | tf_op jit(solution)/shard_map/reduce_scatter | solution.py:87
Sparse Core Ops, SparseCore 0:
  19.4 151.3 all-gather.2
  173.8 146.5 all-gather.4
  838.1 40.9 reduce-scatter.1
where the time goes:
time: 892 us; the launch traced here: 886 us
  waiting for transfers between devices  322 us (36%)
  local copies, waits for them, and re-layouts  237 us (27%)
  matrix products  176 us (20%)
  loops' own time  81.6 us (9%)
  other arithmetic  27.7 us (3%)
  blocking collectives  23.2 us (3%)
  between operations  13.8 us (2%)
    dynamic_slice x128, local copies, waits for them, and re-layouts, local(): lax.scan(advance, initial, (key_frames, value_frames, jnp.arange(number,...  182 us
    all_gather x1, waiting for transfers between devices, local(): value_piece = lax.all_gather(value_local, 'tm', axis=0, tiled=True)  150 us
    all_gather x1, waiting for transfers between devices, local(): key_piece = lax.all_gather(key_local, 'tm', axis=0, tiled=True)  125 us
    dot_general x32, matrix products, frame_update(): jnp.einsum('hqk,khd->qhd', weights.astype(jnp.bfloat16), value_heads, pre...  107 us
    another operation x1, loops' own time, local(): lax.scan(advance, initial, (key_frames, value_frames, jnp.arange(number,...  81.6 us
    dot_general x32, matrix products, frame_update(): jnp.einsum('qhd,khd->hqk', query_heads, key_heads, preferred_element_type...  61.7 us
    reduce_scatter x1, waiting for transfers between devices, local(): lax.psum_scatter(jnp.dot(attended, w_out, preferred_element_type=jnp.floa...  41.1 us
    broadcast_in_dim x64, local copies, waits for them, and re-layouts, frame_update(): scores = jnp.where(allowed[None], scores, NEG)  24.9 us
  transfers between devices with their start and end apart: 4, of which 4 were waited for; matrix products, arithmetic and copies ran while one was open for 0% of the time, Pallas kernels for 0%

commit v1 on v0

v1 whole, which is shorter than its diff:
```python
import functools

import jax
import jax.numpy as jnp
import numpy as np
from jax import lax
from jax.experimental import pallas as pl
from jax.experimental.pallas import tpu as pltpu
from jax.sharding import PartitionSpec as P

HS = 128
BLOCK = 64
FRAME = 384
FB = FRAME // BLOCK
NEG = -1e30
SCALE = HS ** -0.5
LOG2 = float(SCALE * np.log2(np.e))
BOUND = 60.0

RING = ("z", "yh", "yl")
Y = ("yh", "yl")
ALL = ("x", "z", "yh", "yl", "c")
PROJECT_VMEM = 20
CHUNKS = 2
NEAR = (0, 3, 1, 2)
ROWS = 144


def square_norm_max(rows):
    wide = rows.astype(jnp.float32)
    return jnp.max(jnp.sum(wide * wide, axis=1, keepdims=True))


def attention_kernel(*refs, first, count, parts, sub, small):
    q_ref, mt_ref = refs[0], refs[1]
    sources = refs[2 : 2 + count]
    if first:
        state_in = norm_in = None
        state_out, norm_out = refs[2 + count :]
    else:
        norm_in, state_in, state_out, norm_out = refs[2 + count :]
    tiles, rows, _ = q_ref.shape

    def joined(slices):
        return slices[0] if len(slices) == 1 else jnp.concatenate(slices, axis=0)

    def with_masks(key, tile, mask_at, size):
        masks = mt_ref[tile, pl.ds(mask_at, size // sub), :]
        masks = jnp.broadcast_to(masks[:, None, :], (size // sub, sub, HS)).reshape(size, HS)
        return jnp.concatenate([key, masks.astype(jnp.bfloat16)], axis=1)

    def scores(key, query):
        return lax.dot_general(key, query, (((1,), (1,)), ((), ())), preferred_element_type=jnp.float32)

    def mixed(value, weights):
        return lax.dot_general(
            value, weights.astype(jnp.bfloat16), (((0,), (0,)), ((), ())), preferred_element_type=jnp.float32
        )

    key_norm = jnp.float32(0.0)
    for k_source, k_at, _, _, keys in parts:
        key_norm = jnp.maximum(key_norm, square_norm_max(sources[k_source][k_at : k_at + keys, :]))
    all_keys = sum(part[4] for part in parts)

    @pl.loop(0, tiles)
    def _(tile):
        query_norm = square_norm_max(q_ref[tile]) if first else jnp.max(norm_in[tile])
        bounded = jnp.logical_and(query_norm >= 0.0, query_norm * key_norm <= (BOUND / SCALE) ** 2)
        place = lax.broadcasted_iota(jnp.int32, (rows, HS), 0) // sub
        one_hot = jnp.where(place == lax.broadcasted_iota(jnp.int32, (rows, HS), 1), 1.0, 0.0).astype(jnp.bfloat16)
        query = jnp.concatenate([q_ref[tile], one_hot], axis=1)
        norm_out[tile] = jnp.full((8, HS), jnp.where(bounded, query_norm, -1.0), jnp.float32)

        @pl.when(bounded)
        def _():
            key = joined([sources[k][at : at + keys, :] for k, at, _, _, keys in parts])
            value = joined([sources[v][at : at + keys, :] for _, _, v, at, keys in parts])
            weights = jnp.exp2(scores(with_masks(key, tile, 0, all_keys), query) * LOG2)
            total = jnp.sum(weights, axis=0, keepdims=True)
            weighted = mixed(value, weights)
            if not first:
                total = state_in[tile, HS : HS + 1, :] + total
                weighted = state_in[tile, :HS, :] + weighted
            state_out[tile, :HS, :] = weighted
            state_out[tile, HS : HS + 8, :] = jnp.broadcast_to(total, (8, rows))
            state_out[tile, HS + 8 :, :] = jnp.zeros((8, rows), jnp.float32)

        @pl.when(jnp.logical_not(bounded))
        def _():
            if first:
                state_out[tile, : HS + 8, :] = jnp.zeros((HS + 8, rows), jnp.float32)
                state_out[tile, HS + 8 :, :] = jnp.full((8, rows), NEG, jnp.float32)
            else:
                state_out[tile] = state_in[tile]
            mask_base = 0
            for k_source, k_at, v_source, v_at, keys in parts:

                @pl.loop(0, keys // small)
                def _(j):
                    key = sources[k_source][pl.ds(pl.multiple_of(k_at + j * small, small), small), :]
                    value = sources[v_source][pl.ds(pl.multiple_of(v_at + j * small, small), small), :]
                    mask_at = pl.multiple_of(mask_base + j * (small // sub), 8)
                    found = scores(with_masks(key, tile, mask_at, small), query)
                    top = state_out[tile, HS + 8 : HS + 9, :]
                    new_top = jnp.maximum(top, jnp.max(found, axis=0, keepdims=True))
                    factor = jnp.exp2((top - new_top) * LOG2)
                    weights = jnp.exp2((found - new_top) * LOG2)
                    total = state_out[tile, HS : HS + 1, :] * factor + jnp.sum(weights, axis=0, keepdims=True)
                    state_out[tile, HS : HS + 8, :] = jnp.broadcast_to(total, (8, rows))
                    state_out[tile, :HS, :] = state_out[tile, :HS, :] * factor + mixed(value, weights)
                    state_out[tile, HS + 8 :, :] = jnp.broadcast_to(new_top, (8, rows))

                mask_base += keys // sub


def attention(name, query, masks, sub, sources, parts, state=None, small=256):
    tiles, rows, _ = query.shape
    first = state is None
    operands = [query, masks, *sources]
    if not first:
        operands += [state[1], state[0]]
    return pl.pallas_call(
        functools.partial(
            attention_kernel, first=first, count=len(sources), parts=tuple(parts), sub=sub, small=small
        ),
        out_shape=[
            jax.ShapeDtypeStruct((tiles, ROWS, rows), jnp.float32),
            jax.ShapeDtypeStruct((tiles, 8, HS), jnp.float32),
        ],
        input_output_aliases={} if first else {len(operands) - 1: 0},
        cost_estimate=pl.CostEstimate(flops=1024, bytes_accessed=1024, transcendentals=0),
        compiler_params=pltpu.CompilerParams(vmem_limit_bytes=28 * 2**20),
        name=name,
    )(*operands)


def combined(states):
    top = states[0][HS + 8 : HS + 9]
    for state in states[1:]:
        top = jnp.maximum(top, state[HS + 8 : HS + 9])
    total, mixed = 0.0, 0.0
    for state in states:
        factor = jnp.exp2((state[HS + 8 : HS + 9] - top) * LOG2)
        total = total + state[HS : HS + 1] * factor
        mixed = mixed + state[:HS] * factor
    return mixed, total, top


def merge_kernel(*refs):
    *refs, out_ref = refs
    tiles, _, rows = refs[-1].shape
    for tile in range(tiles):
        states = [ref[tile] for ref in refs]
        mixed, total, _ = combined([unspread(a) if a.dtype == jnp.bfloat16 else a for a in states])
        out_ref[tile * rows : (tile + 1) * rows, :] = jnp.transpose(mixed / total).astype(jnp.bfloat16)


def merge(name, *states):
    tiles, _, rows = states[-1].shape
    return pl.pallas_call(
        merge_kernel,
        name=name,
        out_shape=jax.ShapeDtypeStruct((tiles * rows, HS), jnp.bfloat16),
        cost_estimate=pl.CostEstimate(flops=1024, bytes_accessed=1024, transcendentals=0),
        compiler_params=pltpu.CompilerParams(vmem_limit_bytes=32 * 2**20),
    )(*states)


def spread(row):
    parts = []
    for _ in range(3):
        part = row.astype(jnp.bfloat16).astype(jnp.float32)
        parts.append(part)
        row = row - part
    return parts + [jnp.zeros((5, row.shape[1]), jnp.float32)]


def unspread(state):
    state = state.astype(jnp.float32)
    total = state[HS : HS + 1] + state[HS + 1 : HS + 2] + state[HS + 2 : HS + 3]
    top = state[HS + 8 : HS + 9] + state[HS + 9 : HS + 10] + state[HS + 10 : HS + 11]
    return jnp.concatenate([state[:HS], jnp.broadcast_to(total, (8, total.shape[1])), jnp.broadcast_to(top, (8, total.shape[1]))], axis=0)


def fold_kernel(own_ref, other_ref, *out_refs):
    tiles, _, rows = other_ref.shape
    width = out_refs[0].shape[2]
    each = rows // width
    for tile in range(tiles):
        mixed, total, top = combined([own_ref[tile], other_ref[tile]])
        for i in range(each):
            out = out_refs[tile * each + i]
            cut = slice(i * width, (i + 1) * width)
            rows_out = [mixed[:, cut]] + spread(total[:, cut]) + spread(top[:, cut])
            out[0] = jnp.concatenate(rows_out, axis=0).astype(jnp.bfloat16)


def fold(own, other, width):
    tiles, _, rows = other.shape
    return pl.pallas_call(
        fold_kernel,
        name="fold",
        out_shape=[jax.ShapeDtypeStruct((1, ROWS, width), jnp.bfloat16)] * (tiles * rows // width),
        cost_estimate=pl.CostEstimate(flops=1024, bytes_accessed=1024, transcendentals=0),
        compiler_params=pltpu.CompilerParams(vmem_limit_bytes=32 * 2**20),
    )(own, other)


def outgoing_kernel(*refs):
    sources, out_ref = refs[:-1], refs[-1]
    token_rows = sources[0].shape[0]
    piece = token_rows // 4
    at = len(sources) * token_rows
    for z in range(4):
        for yh in range(2):
            for yl in range(2):
                target = (z * 2 + yh) * 2 + yl
                head = 10 * yl + 2 * z + yh
                for i, source in enumerate(sources):
                    out_ref[target, i * token_rows : (i + 1) * token_rows, :] = source[:, head * HS : (head + 1) * HS]
                head = 10 * yl + 8 + yh
                pieces = [
                    source[:, head * HS : (head + 1) * HS].astype(jnp.float32)[z * piece : (z + 1) * piece]
                    for source in sources
                ]
                out_ref[target, at:, :] = jnp.concatenate(pieces, axis=0).astype(jnp.bfloat16)


def outgoing(name, *arrays):
    rows = len(arrays) * arrays[0].shape[0] * 5 // 4
    return pl.pallas_call(
        outgoing_kernel,
        name=name,
        out_shape=jax.ShapeDtypeStruct((16, rows, HS), jnp.bfloat16),
        cost_estimate=pl.CostEstimate(flops=1024, bytes_accessed=1024, transcendentals=0),
        compiler_params=pltpu.CompilerParams(vmem_limit_bytes=16 * 2**20),
    )(*arrays)


def project_kernel(core_ref, att_ref, own_w, side_w, kept_ref, sent_ref):
    core = core_ref[0]
    kept = kept_ref.shape[0]

    def group(number):
        return jnp.concatenate([att_ref[number * 5 + i] for i in range(5)], axis=1)

    total = jnp.dot(group(core), own_w[...], preferred_element_type=jnp.float32)
    total = total + jnp.dot(group(1 - core), side_w[...], preferred_element_type=jnp.float32)
    kept_ref[...] = total[:kept]
    sent_ref[...] = total[kept:].astype(jnp.bfloat16)


def project(core, attended, own_w, side_w, start, columns, width=1280):
    heads, rows, _ = attended.shape
    depth = own_w.shape[0]
    first = start // width
    w_spec = pl.BlockSpec((depth, width), lambda j: (0, j + first))
    out_spec = pl.BlockSpec((rows // 2, width), lambda j: (0, j))
    return pl.pallas_call(
        project_kernel,
        grid=(columns // width,),
        in_specs=[
            pl.BlockSpec(memory_space=pltpu.SMEM),
            pl.BlockSpec((heads, rows, HS), lambda j: (0, 0, 0)),
            w_spec,
            w_spec,
        ],
        out_specs=[out_spec, out_spec],
        out_shape=[
            jax.ShapeDtypeStruct((rows // 2, columns), jnp.float32),
            jax.ShapeDtypeStruct((rows // 2, columns), jnp.bfloat16),
        ],
        cost_estimate=pl.CostEstimate(flops=1024, bytes_accessed=1024, transcendentals=0),
        compiler_params=pltpu.CompilerParams(vmem_limit_bytes=PROJECT_VMEM * 2**20),
        name="project",
    )(core, attended, own_w, side_w)


def finish_kernel(*refs):
    kept, above, below, out_ref = refs[0], refs[1], refs[2], refs[-1]
    half = above.shape[0]
    out_ref[:half, :] = (kept[:half] + above[...].astype(jnp.float32)).astype(jnp.bfloat16)
    out_ref[half:, :] = (kept[half:] + below[...].astype(jnp.float32)).astype(jnp.bfloat16)


def finish(index, parts, whole=None):
    rows, columns = parts[0].shape
    half = rows // 2
    specs = [pl.BlockSpec((rows, columns), lambda i: (0, 0))] + [pl.BlockSpec((half, columns), lambda i: (0, 0))] * 2
    operands = list(parts)
    if whole is not None:
        specs.append(pl.BlockSpec(memory_space=pl.ANY))
        operands.append(whole)
    return pl.pallas_call(
        finish_kernel,
        name="finish",
        grid=(1,),
        in_specs=specs,
        out_specs=pl.BlockSpec((rows, columns), lambda i: (0, index)),
        out_shape=jax.ShapeDtypeStruct((rows, columns * CHUNKS), jnp.bfloat16),
        input_output_aliases={} if whole is None else {3: 0},
        compiler_params=pltpu.CompilerParams(vmem_limit_bytes=16 * 2**20),
    )(*operands)


def ring(array, axes, size, shift, name="ring"):
    with jax.named_scope(name):
        return lax.ppermute(array, axes, [(i, (i + shift) % size) for i in range(size)])


def cross(array, axis, bit, name):
    with jax.named_scope(name):
        return lax.ppermute(array, axis, [(i, i ^ bit) for i in range(4)])


def swap(array, name="swap"):
    with jax.named_scope(name):
        return lax.ppermute(array, "c", [(0, 1), (1, 0)])


def mask_tables(block_mask, frame_map):
    x, z, core = lax.axis_index("x"), lax.axis_index("z"), lax.axis_index("c")
    low, group = np.arange(2)[None, :, None], np.arange(3)
    at_core = np.arange(2)[:, None, None]
    ring_within = ((low * 2 + at_core) * 96 + group * 32) // BLOCK
    at_z = np.arange(4)[:, None, None, None]
    plane_within = ((low * 2 + at_core) * 96 + at_z * 24 + group * 8) // BLOCK

    def frames(at_x):
        return lax.dynamic_slice_in_dim(frame_map, at_x * 8, 8)[:, None, None] * FB

    def ring_blocks(at_x, at_core):
        within = jnp.asarray(ring_within.astype(np.int32))[at_core]
        return (frames(at_x) + within[None]).reshape(-1)

    def plane_blocks(at_x, at_core, at_z):
        within = jnp.asarray(plane_within.astype(np.int32))[at_z, at_core]
        return (frames(at_x) + within[None]).reshape(-1)

    ring_keys = jnp.concatenate([ring_blocks((x + i) % 4, core) for i in NEAR])
    plane_keys = jnp.concatenate([plane_blocks(x, core, z ^ i) for i in range(4)])
    blocks = jnp.arange(block_mask.shape[0], dtype=jnp.int32)
    pad = jnp.zeros((32,), jnp.int32)
    ring_queries, plane_queries = [], []
    for side in (0, 1):
        ring_queries += [ring_blocks(x, core ^ side), pad, pad, pad[:16]]
        for pair in (0, 2):
            plane_queries += [plane_blocks(x ^ (pair + i), core ^ side, z) for i in (0, 1)] + [pad]
    blocked = (block_mask <= 0).astype(jnp.bfloat16)

    def pick(index):
        return (index[:, None] == blocks[None, :]).astype(jnp.bfloat16)

    queries = pick(jnp.concatenate(ring_queries + plane_queries))
    by_query = jnp.dot(queries, blocked, preferred_element_type=jnp.float32).astype(jnp.bfloat16).reshape(6, HS, -1)

    def table(index, part):
        found = jnp.einsum("kb,tcb->tkc", pick(index), part, preferred_element_type=jnp.float32)
        return found * NEG

    return table(ring_keys, by_query[:2]), table(plane_keys, by_query[2:])


def local(queries, keys, values, w_out, block_mask, frame_map):
    core = lax.axis_index("c").astype(jnp.int32)
    z, low = lax.axis_index("z"), lax.axis_index("yl")
    token_rows = queries.shape[0]
    piece = token_rows // 4

    side_w = swap(w_out, "side_w")
    with jax.named_scope("spread"):
        sent = lax.all_to_all(outgoing("outgoing", keys, values, queries), RING, 0, 0)
    one, two, three = token_rows, 2 * token_rows, 3 * token_rows
    ring_kv = jnp.concatenate([sent[:, :one], sent[:, one:two]], axis=0).reshape(-1, HS)
    ring_q = sent[:, two:three].reshape(-1, HS)
    plane_kv = jnp.concatenate([sent[:, three : three + piece], sent[:, three + piece : three + 2 * piece]], axis=0)
    plane_kv = plane_kv.reshape(-1, HS)
    plane_q = sent[:, three + 2 * piece :].reshape(-1, HS)
    ring_rows = 16 * token_rows
    plane_rows = 16 * piece

    ring_masks, plane_masks = mask_tables(block_mask, frame_map)

    side_w, ring_kv, ring_q, plane_kv, plane_q = lax.optimization_barrier((side_w, ring_kv, ring_q, plane_kv, plane_q))
    ring_left, ring_right = ring(ring_kv, "x", 4, 1, "ring_x"), ring(ring_kv, "x", 4, -1, "ring_x")
    query_a = jnp.stack([ring_q, swap(ring_q, "swap_q")])

    plane_kv = [plane_kv] + [cross(plane_kv, "z", i, "plane_z") for i in (1, 2, 3)]
    plane_q = jnp.concatenate([plane_q] + [cross(plane_q, "x", i, "plane_q") for i in (1, 2, 3)], axis=0)
    query_b = jnp.concatenate([plane_q, swap(plane_q, "swap_plane_q")], axis=0).reshape(4, 2 * plane_rows, HS)
    query_a, query_b = lax.optimization_barrier((query_a, query_b))
    whole = [(0, 0, 0, ring_rows, ring_rows)]
    state = attention("own", query_a, ring_masks[:, :48], 32, [ring_kv], whole)
    plane_parts = [(i, 0, i, plane_rows, plane_rows) for i in range(4)]
    query_b, state = lax.optimization_barrier((query_b, state))
    plane_state = attention("plane", query_b, plane_masks, 8, plane_kv, plane_parts, small=128)

    plane_state, ring_left, ring_right = lax.optimization_barrier((plane_state, ring_left, ring_right))
    other_b = swap(plane_state[0][2:], "swap_b")
    plane_part = fold(plane_state[0], other_b, plane_rows)
    plane_part, state, ring_left, ring_right = lax.optimization_barrier((plane_part, state, ring_left, ring_right))
    middle = ring_kv.shape[0] // 2
    ring_far = [
        ring(ring_left[:middle], "x", 4, 1, "ring_x_far"),
        ring(ring_right[middle:], "x", 4, -1, "ring_x_far"),
    ]
    plane_part = [plane_part[0]] + [cross(plane_part[i], "x", i, "plane_sum") for i in (1, 2, 3)]
    state = attention("left", query_a, ring_masks[:, 48:96], 32, [ring_left], whole, state)
    state = attention("right", query_a, ring_masks[:, 96:144], 32, [ring_right], whole, state)
    out_b = merge("merge_plane", *plane_part).reshape(4, 2, 2, piece, HS)
    out_b, state = lax.optimization_barrier((out_b, state))
    far = [(0, 0, 1, 0, ring_rows)]
    side = attention(
        "far_side", query_a[1:], ring_masks[1:, 144:], 32, ring_far, far, (state[0][1:], state[1][1:])
    )
    other_a = swap(side[0], "swap_a")
    state, side = lax.optimization_barrier((state, side))
    state = attention("far_own", query_a[:1], ring_masks[:1, 144:], 32, ring_far, far, (state[0][:1], state[1][:1]))
    out_a = merge("merge_ring", state[0], other_a).reshape(4, 2, 2, token_rows, HS)

    def split(array):
        first, second = array[:, :, 0], array[:, :, 1]
        same = jnp.where(low == 0, first, second)
        other = jnp.where(low == 0, second, first)
        flipped = jnp.stack([other[:, 1], other[:, 0]], axis=1)
        below = jnp.where(low == 0, flipped, other)
        above = jnp.where(low == 0, other, flipped)
        return same, below, above

    half = token_rows // 2
    same, below, above = split(out_a)
    piece_same, piece_below, piece_above = split(out_b)
    back = jnp.concatenate(
        [same, below[:, :, :half], above[:, :, half:], piece_same, jnp.where(z < 2, piece_below, piece_above)], axis=2
    ).reshape(8, -1, HS)
    with jax.named_scope("return"):
        back = lax.all_to_all(back, ("z", "yh"), 0, 0)
    rows = 2 * token_rows
    plane_back = back[:, rows:].reshape(4, 2, 2, piece, HS).transpose(1, 2, 0, 3, 4).reshape(2, rows, HS)
    attended = jnp.concatenate([back[:, :rows], plane_back], axis=0)

    out = None
    columns = w_out.shape[1] // CHUNKS
    for i in range(CHUNKS):
        kept, sent = project(core[None], attended, w_out, side_w, i * columns, columns)
        from_above = ring(sent[:half], Y, 4, -1, "sum_y")
        from_below = ring(sent[half:], Y, 4, 1, "sum_y")
        out = finish(i, (kept, from_above, from_below), out)
    return out


def solution(mesh):
    fine = jax.sharding.Mesh(mesh.devices.reshape(4, 4, 2, 2, 2), ALL)
    rows = P(ALL, None)
    placed = (rows, rows, rows, P(("yl", "c"), None), P(), P())
    return jax.shard_map(local, mesh=fine, in_specs=placed, out_specs=rows, check_vma=False)
```

time: 892 us -> 182 us (0.20)
  waiting for transfers between devices: 322 us -> 35 us
  local copies, waits for them, and re-layouts: 237 us -> 6.97 us
  matrix products: 176 us -> 0.93 us
  Pallas kernels: 0 us -> 89.5 us
  loops' own time: 81.6 us -> 0 us
  starting transfers between devices: 3.55 us -> 32.3 us
  other arithmetic: 27.7 us -> 0.9 us
  between operations: 13.8 us -> 0.7 us
    all_gather x2 -> x0, waiting for transfers between devices: 274 us -> none  [the longest x1 150 us: local(): value_piece = lax.all_gather(value_local, 'tm', axis=0, tiled=True)]
    dynamic_slice x162 -> x0, local copies, waits for them, and re-layouts: 202 us -> none  [the longest x128 182 us: local(): lax.scan(advance, initial, (key_frames, value_frames, jnp.arange(number,...]
    dot_general x65 -> x3, matrix products: 176 us -> 0.93 us  [the longest x2 0.48 us: table(): jnp.einsum('kb,tcb->tkc', pick(index), part, preferred_element_type=jnp.f...]
    pallas_call x0 -> x14, Pallas kernels: none -> 89.5 us  [the longest x6 77.3 us: attention(): pl.pallas_call(functools.partial(attention_kernel, first=first, count=len...]
    another operation x1 -> x0, loops' own time: 81.6 us -> none  [local(): lax.scan(advance, initial, (key_frames, value_frames, jnp.arange(number,...]
    reduce_scatter x1 -> x0, waiting for transfers between devices: 41.1 us -> none  [local(): lax.psum_scatter(jnp.dot(attended, w_out, preferred_element_type=jnp.floa...]
    broadcast_in_dim x96 -> x1, local copies, waits for them, and re-layouts: 30.5 us -> 0.01 us  [mask_tables(): pad = jnp.zeros((32,), jnp.int32)]
    ppermute x0 -> x22, starting transfers between devices: none -> 24.1 us  [the longest x9 13.3 us: cross(): return lax.ppermute(array, axis, [(i, i ^ bit) for i in range(4)])]
  transfers between devices with their start and end apart: 4 -> 23, of which waited for: 4 -> 9; matrix products, arithmetic and copies ran while one was open for 0% -> 2% of each run, Pallas kernels for 0% -> 40%
where the time goes in v1:
time: 182 us; the launch traced here: 181 us
  Pallas kernels  89.5 us (49%)
  waiting for transfers between devices  35 us (19%)
  starting transfers between devices  32.3 us (18%)
  blocking collectives  15 us (8%)
  local copies, waits for them, and re-layouts  6.97 us (4%)
    pallas_call x6, Pallas kernels, attention(): pl.pallas_call(functools.partial(attention_kernel, first=first, count=len...  77.3 us
    all_to_all x1, waiting for transfers between devices, local(): lax.all_to_all(outgoing('outgoing', keys, values, queries), RING, 0, 0)  21.6 us
    all_to_all x1, blocking collectives, local(): back = lax.all_to_all(back, ('z', 'yh'), 0, 0)  15 us
    ppermute x9, starting transfers between devices, cross(): return lax.ppermute(array, axis, [(i, i ^ bit) for i in range(4)])  13.3 us
    ppermute x8, starting transfers between devices, ring(): lax.ppermute(array, axes, [(i, (i + shift) % size) for i in range(size)])  10.3 us
    ppermute x8, waiting for transfers between devices, ring(): lax.ppermute(array, axes, [(i, (i + shift) % size) for i in range(size)])  8.81 us
    all_to_all x1, starting transfers between devices, local(): lax.all_to_all(outgoing('outgoing', keys, values, queries), RING, 0, 0)  8.28 us
    pallas_call x2, Pallas kernels, project(): pl.pallas_call(project_kernel, grid=(columns // width,), in_specs=[pl.Blo...  7.09 us
  transfers between devices with their start and end apart: 23, of which 9 were waited for; matrix products, arithmetic and copies ran while one was open for 2% of the time, Pallas kernels for 40%

profile of v1, /device:TPU:0, one launch (start us, length us, event | category | flops | bytes accessed | tf_op | source)
XLA Modules:
  0.0 181.3 jit_solution(16527683025216707216)
XLA Ops:
  3.1 1.5 outgoing.1
  4.6 8.3 %all-to-all-start = ((bf16[16,360,128]{2,1,0:T(8,128)(2,1)}), bf16[16,360,128]{2,1,0:T(8,128)(2,1)S(1)}, u32[]{:S(2)}, u32[]{:S(2)}) async-start(bf16[16,360,128]{2,1,0:T(8,128)(2,1)} %outgoing.1), calls=%async_computation | async-start | bytes 2949120 | tf_op jit(solution)/shard_map/spread/all_to_all | solution.py:372
  16.2 21.6 %all-to-all-done = bf16[16,360,128]{2,1,0:T(8,128)(2,1)S(1)} async-done(((bf16[16,360,128]{2,1,0:T(8,128)(2,1)}), bf16[16,360,128]{2,1,0:T(8,128)(2,1)S(1)}, u32[]{:S(2)}, u32[]{:S(2)}) %all-to-all-start) | async-done | bytes 1474592 | tf_op jit(solution)/shard_map/spread/all_to_all | solution.py:372
  38.1 1.6 collective-permute-start.2
  39.6 2.7 %collective-permute-start.3 = (bf16[384,128]{1,0:T(8,128)(2,1)S(1)}, bf16[384,128]{1,0:T(8,128)(2,1)S(1)}, u32[]{:S(2)}, u32[]{:S(2)}) collective-permute-start(bf16[384,128]{1,0:T(8,128)(2,1)S(1)} %bitcast.94), channel_id=1, source_target_pairs={{0,64},{32,96},{64,0},{96,32},{1,65},{33,97},{65,1},{97,33},{2,66}... | collective-permute-start | bytes 294920 | tf_op jit(solution)/shard_map/plane_q/ppermute | solution.py:313
  42.9 2.8 %collective-permute-start.10 = (bf16[3072,128]{1,0:T(8,128)(2,1)S(1)}, bf16[3072,128]{1,0:T(8,128)(2,1)S(1)}, u32[]{:S(2)}, u32[]{:S(2)}) collective-permute-start(bf16[3072,128]{1,0:T(8,128)(2,1)S(1)} %bitcast.79), channel_id=1, source_target_pairs={{0,96},{32,0},{64,32},{96,64},{1,97},{33,1},{65,33},{97,65},{2,98}... | collective-permute-start | bytes 2359304 | tf_op jit(solution)/shard_map/ring_x/ppermute | solution.py:308
  49.0 1.4 collective-permute-start.7
  50.6 1.8 %collective-permute-start.8 = (bf16[768,128]{1,0:T(8,128)(2,1)S(1)}, bf16[768,128]{1,0:T(8,128)(2,1)S(1)}, u32[]{:S(2)}, u32[]{:S(2)}) collective-permute-start(bf16[768,128]{1,0:T(8,128)(2,1)S(1)} %bitcast.88), channel_id=1, source_target_pairs={{0,24},{8,16},{16,8},{24,0},{1,25},{9,17},{17,9},{25,1},{2,26},{10... | collective-permute-start | bytes 589832 | tf_op jit(solution)/shard_map/plane_z/ppermute | solution.py:313
  52.5 11.9 %own.1 = (f32[2,144,1536]{2,1,0:T(8,128)S(1)}, f32[2,8,128]{2,1,0:T(8,128)S(1)}) custom-call(bf16[2,1536,128]{2,1,0:T(8,128)(2,1)S(1)} %pad_maximum_fusion.1.refs_0_, f32[2,48,128]{2,1,0:T(8,128)S(1)} %get-tuple-element.109.refs_1_, bf16[3072,128]{1,0:T(8,128)(2,1)S(1)} %bitcast.81), custom_call_target="tpu_custom_call" | custom-call | flops 1024 | bytes 1024 | tf_op jit(solution)/shard_map/own/pallas_call | solution.py:122
  64.5 29.1 %plane.1 = (f32[4,144,768]{2,1,0:T(8,128)S(1)}, f32[4,8,128]{2,1,0:T(8,128)}) custom-call(bf16[4,768,128]{2,1,0:T(8,128)(2,1)S(1)} %bitcast.85, f32[4,192,128]{2,1,0:T(8,128)S(1)} %fusion.refs_1_, bf16[768,128]{1,0:T(8,128)(2,1)S(1)} %bitcast.89, bf16[768,128]{1,0:T(8,128)(2,1)S(1)} %collective-permute-done.6.refs_3_, ...), custom_call_target="tpu_custom_call" | custom-call | flops 1024 | bytes 1024 | tf_op jit(solution)/shard_map/plane/pallas_call | solution.py:122
  94.5 1.8 collective-permute-done.11.other_ref
  96.9 3.1 %collective-permute-start.15 = (bf16[1,144,384]{2,1,0:T(8,128)(2,1)S(1)}, bf16[1,144,384]{2,1,0:T(8,128)(2,1)S(1)}, u32[]{:S(2)}, u32[]{:S(2)}) collective-permute-start(bf16[1,144,384]{2,1,0:T(8,128)(2,1)S(1)} %get-tuple-element.71), channel_id=1, source_target_pairs={{0,64},{32,96},{64,0},{96,32},{1,65},{33,97},{65,1},{97,33},{2,66}... | collective-permute-start | bytes 331784 | tf_op jit(solution)/shard_map/plane_sum/ppermute | solution.py:313
  101.4 3.3 %collective-permute-start.13 = (bf16[1536,128]{1,0:T(8,128)(2,1)S(1)}, bf16[1536,128]{1,0:T(8,128)(2,1)S(1)}, u32[]{:S(2)}, u32[]{:S(2)}) collective-permute-start(bf16[1536,128]{1,0:T(8,128)(2,1)S(1)} %slice.135), channel_id=1, source_target_pairs={{0,96},{32,0},{64,32},{96,64},{1,97},{33,1},{65,33},{97,65},{2,98}... | collective-permute-start | bytes 1179656 | tf_op jit(solution)/shard_map/ring_x_far/ppermute | solution.py:308
  104.8 11.6 %left.1 = (f32[2,144,1536]{2,1,0:T(8,128)S(1)}, f32[2,8,128]{2,1,0:T(8,128)S(1)}) custom-call(bf16[2,1536,128]{2,1,0:T(8,128)(2,1)S(1)} %pad_maximum_fusion.1.refs_0_, f32[2,48,128]{2,1,0:T(8,128)S(1)} %get-tuple-element.107.refs_1_, bf16[3072,128]{1,0:T(8,128)(2,1)S(1)} %collective-permute-done.9.refs_2_, ...), custom_call_target="tpu_custom_call", output_to_operand_aliasing={{0}: (4, {})} | custom-call | flops 1024 | bytes 1024 | tf_op jit(solution)/shard_map/left/pallas_call | solution.py:122
  116.3 11.6 %right.1 = (f32[2,144,1536]{2,1,0:T(8,128)S(1)}, f32[2,8,128]{2,1,0:T(8,128)S(1)}) custom-call(bf16[2,1536,128]{2,1,0:T(8,128)(2,1)S(1)} %pad_maximum_fusion.1.refs_0_, f32[2,48,128]{2,1,0:T(8,128)S(1)} %get-tuple-element.108.refs_1_, bf16[3072,128]{1,0:T(8,128)(2,1)S(1)} %collective-permute-done.10.refs_2_, ...), custom_call_target="tpu_custom_call", output_to_operand_aliasing={{0}: (4, {})} | custom-call | flops 1024 | bytes 1024 | tf_op jit(solution)/shard_map/right/pallas_call | solution.py:122
  128.2 6.6 %far_side.1 = (f32[1,144,1536]{2,1,0:T(8,128)S(1)}, f32[1,8,128]{2,1,0:T(8,128)}) custom-call(bf16[1,1536,128]{2,1,0:T(8,128)(2,1)S(1)} %get-tuple-element.97.refs_0_, f32[1,48,128]{2,1,0:T(8,128)S(1)} %get-tuple-element.105.refs_1_, bf16[1536,128]{1,0:T(8,128)(2,1)S(1)} %collective-permute-done.12.refs_2_, ...), custom_call_target="tpu_custom_call", output_to_operand_aliasing={{0}: (5, {})} | custom-call | flops 1024 | bytes 1024 | tf_op jit(solution)/shard_map/far_side/pallas_call | solution.py:122
  135.9 6.4 %far_own.1 = (f32[1,144,1536]{2,1,0:T(8,128)S(1)}, f32[1,8,128]{2,1,0:T(8,128)}) custom-call(bf16[1,1536,128]{2,1,0:T(8,128)(2,1)S(1)} %get-tuple-element.98.refs_0_, f32[1,48,128]{2,1,0:T(8,128)S(1)} %copy-done.5, bf16[1536,128]{1,0:T(8,128)(2,1)S(1)} %collective-permute-done.12.refs_2_, ...), custom_call_target="tpu_custom_call", output_to_operand_aliasing={{0}: (5, {})} | custom-call | flops 1024 | bytes 1024 | tf_op jit(solution)/shard_map/far_own/pallas_call | solution.py:122
  142.3 1.6 merge_ring.1
  144.2 15.0 %all_to_all.10 = bf16[8,240,128]{2,1,0:T(8,128)(2,1)S(1)} all-to-all(bf16[8,240,128]{2,1,0:T(8,128)(2,1)S(1)} %bitcast.92), channel_id=1, replica_groups=mesh['x'=4,'z'=4,'yh'=2,'yl'=2,'c'=2] {'z','yh'}, dimensions={0} | all-to-all | bytes 983040 | tf_op jit(solution)/shard_map/return/all_to_all | solution.py:437
  159.4 3.5 %project.3 = (f32[96,2560]{1,0:T(8,128)S(1)}, bf16[96,2560]{1,0:T(8,128)(2,1)S(1)}) custom-call(s32[1]{0:T(128)} %bitcast.core_ref, bf16[10,192,128]{2,1,0:T(8,128)(2,1)S(1)} %pad_maximum_fusion.2.att_ref, bf16[640,5120]{1,0:T(8,128)(2,1)S(1)} %bitcast.76, bf16[640,5120]{1,0:T(8,128)(2,1)} %collective-permute-done.side_w), custom_call_target="tpu_custom_call" | custom-call | flops 1024 | bytes 1024 | tf_op jit(solution)/shard_map/project/pallas_call | solution.py:259
  162.9 3.6 %project.2 = (f32[96,2560]{1,0:T(8,128)S(1)}, bf16[96,2560]{1,0:T(8,128)(2,1)S(1)}) custom-call(s32[1]{0:T(128)} %bitcast.core_ref, bf16[10,192,128]{2,1,0:T(8,128)(2,1)S(1)} %pad_maximum_fusion.2.att_ref, bf16[640,5120]{1,0:T(8,128)(2,1)S(1)} %bitcast.76, bf16[640,5120]{1,0:T(8,128)(2,1)} %collective-permute-done.side_w), custom_call_target="tpu_custom_call" | custom-call | flops 1024 | bytes 1024 | tf_op jit(solution)/shard_map/project/pallas_call | solution.py:259
  166.6 2.0 %collective-permute-start.21 = (bf16[48,2560]{1,0:T(8,128)(2,1)S(1)}, bf16[48,2560]{1,0:T(8,128)(2,1)S(1)}, u32[]{:S(2)}, u32[]{:S(2)}) collective-permute-start(bf16[48,2560]{1,0:T(8,128)(2,1)S(1)} %get-tuple-element.99), channel_id=1, source_target_pairs={{0,2},{2,4},{4,6},{6,0},{1,3},{3,5},{5,7},{7,1},{8,10},{10,12},{12... | collective-permute-start | bytes 737288 | tf_op jit(solution)/shard_map/sum_y/ppermute | solution.py:308
  170.7 4.7 %collective-permute-done.20.refs_1_ = bf16[48,2560]{1,0:T(8,128)(2,1)S(1)} collective-permute-done((bf16[48,2560]{1,0:T(8,128)(2,1)S(1)}, bf16[48,2560]{1,0:T(8,128)(2,1)S(1)}, u32[]{:S(2)}, u32[]{:S(2)}) %collective-permute-start.20) | collective-permute-done | bytes 245792 | tf_op jit(solution)/shard_map/sum_y/ppermute | solution.py:308
  177.6 1.5 collective-permute-done.18.refs_1_
  (128 shorter events, 21.6 us)
Async XLA Ops:
  0.0 38.1 %collective-permute-start = (bf16[640,5120]{1,0:T(8,128)(2,1)}, bf16[640,5120]{1,0:T(8,128)(2,1)}, u32[]{:S(2)}, u32[]{:S(2)}) collective-permute-start(bf16[640,5120]{1,0:T(8,128)(2,1)} %own_w.3), channel_id=1, source_target_pairs={{0,1},{1,0},{2,3},{3,2},{4,5},{5,4},{6,7},{7,6},{8,9},{9,8},{10,11... | collective-permute-start | bytes 19660808 | tf_op jit(solution)/shard_map/side_w/ppermute | solution.py:318
  4.6 33.3 %all-to-all-start = ((bf16[16,360,128]{2,1,0:T(8,128)(2,1)}), bf16[16,360,128]{2,1,0:T(8,128)(2,1)S(1)}, u32[]{:S(2)}, u32[]{:S(2)}) async-start(bf16[16,360,128]{2,1,0:T(8,128)(2,1)} %outgoing.1), calls=%async_computation | async-start | bytes 2949120 | tf_op jit(solution)/shard_map/spread/all_to_all | solution.py:372
  38.1 7.6 %collective-permute-start.2 = (bf16[384,128]{1,0:T(8,128)(2,1)S(1)}, bf16[384,128]{1,0:T(8,128)(2,1)S(1)}, u32[]{:S(2)}, u32[]{:S(2)}) collective-permute-start(bf16[384,128]{1,0:T(8,128)(2,1)S(1)} %bitcast.93), channel_id=1, source_target_pairs={{0,32},{32,0},{64,96},{96,64},{1,33},{33,1},{65,97},{97,65},{2,34}... | collective-permute-start | bytes 294920 | tf_op jit(solution)/shard_map/plane_q/ppermute | solution.py:313
  39.6 7.2 %collective-permute-start.3 = (bf16[384,128]{1,0:T(8,128)(2,1)S(1)}, bf16[384,128]{1,0:T(8,128)(2,1)S(1)}, u32[]{:S(2)}, u32[]{:S(2)}) collective-permute-start(bf16[384,128]{1,0:T(8,128)(2,1)S(1)} %bitcast.94), channel_id=1, source_target_pairs={{0,64},{32,96},{64,0},{96,32},{1,65},{33,97},{65,1},{97,33},{2,66}... | collective-permute-start | bytes 294920 | tf_op jit(solution)/shard_map/plane_q/ppermute | solution.py:313
  42.4 6.4 %collective-permute-start.4 = (bf16[384,128]{1,0:T(8,128)(2,1)S(1)}, bf16[384,128]{1,0:T(8,128)(2,1)S(1)}, u32[]{:S(2)}, u32[]{:S(2)}) collective-permute-start(bf16[384,128]{1,0:T(8,128)(2,1)S(1)} %bitcast.95), channel_id=1, source_target_pairs={{0,96},{32,64},{64,32},{96,0},{1,97},{33,65},{65,33},{97,1},{2,98}... | collective-permute-start | bytes 294920 | tf_op jit(solution)/shard_map/plane_q/ppermute | solution.py:313
  42.9 50.7 %collective-permute-start.10 = (bf16[3072,128]{1,0:T(8,128)(2,1)S(1)}, bf16[3072,128]{1,0:T(8,128)(2,1)S(1)}, u32[]{:S(2)}, u32[]{:S(2)}) collective-permute-start(bf16[3072,128]{1,0:T(8,128)(2,1)S(1)} %bitcast.79), channel_id=1, source_target_pairs={{0,96},{32,0},{64,32},{96,64},{1,97},{33,1},{65,33},{97,65},{2,98}... | collective-permute-start | bytes 2359304 | tf_op jit(solution)/shard_map/ring_x/ppermute | solution.py:308
  45.6 48.0 %collective-permute-start.9 = (bf16[3072,128]{1,0:T(8,128)(2,1)S(1)}, bf16[3072,128]{1,0:T(8,128)(2,1)S(1)}, u32[]{:S(2)}, u32[]{:S(2)}) collective-permute-start(bf16[3072,128]{1,0:T(8,128)(2,1)S(1)} %bitcast.80), channel_id=1, source_target_pairs={{0,32},{32,64},{64,96},{96,0},{1,33},{33,65},{65,97},{97,1},{2,34}... | collective-permute-start | bytes 2359304 | tf_op jit(solution)/shard_map/ring_x/ppermute | solution.py:308
  45.6 3.3 %collective-permute-start.1 = (bf16[1536,128]{1,0:T(8,128)(2,1)S(1)}, bf16[1536,128]{1,0:T(8,128)(2,1)S(1)}, u32[]{:S(2)}, u32[]{:S(2)}) collective-permute-start(bf16[1536,128]{1,0:T(8,128)(2,1)S(1)} %bitcast.90), channel_id=1, source_target_pairs={{0,1},{1,0},{2,3},{3,2},{4,5},{5,4},{6,7},{7,6},{8,9},{9,8},{10,11... | collective-permute-start | bytes 1179656 | tf_op jit(solution)/shard_map/swap_q/ppermute | solution.py:318
  46.8 17.6 %collective-permute-start.6 = (bf16[768,128]{1,0:T(8,128)(2,1)S(1)}, bf16[768,128]{1,0:T(8,128)(2,1)S(1)}, u32[]{:S(2)}, u32[]{:S(2)}) collective-permute-start(bf16[768,128]{1,0:T(8,128)(2,1)S(1)} %bitcast.86), channel_id=1, source_target_pairs={{0,8},{8,0},{16,24},{24,16},{1,9},{9,1},{17,25},{25,17},{2,10},{10... | collective-permute-start | bytes 589832 | tf_op jit(solution)/shard_map/plane_z/ppermute | solution.py:313
  48.8 1.8 collective-permute-start.5
  49.0 15.5 %collective-permute-start.7 = (bf16[768,128]{1,0:T(8,128)(2,1)S(1)}, bf16[768,128]{1,0:T(8,128)(2,1)S(1)}, u32[]{:S(2)}, u32[]{:S(2)}) collective-permute-start(bf16[768,128]{1,0:T(8,128)(2,1)S(1)} %bitcast.87), channel_id=1, source_target_pairs={{0,16},{8,24},{16,0},{24,8},{1,17},{9,25},{17,1},{25,9},{2,18},{10... | collective-permute-start | bytes 589832 | tf_op jit(solution)/shard_map/plane_z/ppermute | solution.py:313
  50.6 13.9 %collective-permute-start.8 = (bf16[768,128]{1,0:T(8,128)(2,1)S(1)}, bf16[768,128]{1,0:T(8,128)(2,1)S(1)}, u32[]{:S(2)}, u32[]{:S(2)}) collective-permute-start(bf16[768,128]{1,0:T(8,128)(2,1)S(1)} %bitcast.88), channel_id=1, source_target_pairs={{0,24},{8,16},{16,8},{24,0},{1,25},{9,17},{17,9},{25,1},{2,26},{10... | collective-permute-start | bytes 589832 | tf_op jit(solution)/shard_map/plane_z/ppermute | solution.py:313
  93.6 2.7 %collective-permute-start.11 = (f32[2,144,768]{2,1,0:T(8,128)S(1)}, f32[2,144,768]{2,1,0:T(8,128)S(1)}, u32[]{:S(2)}, u32[]{:S(2)}) collective-permute-start(f32[2,144,768]{2,1,0:T(8,128)S(1)} %slice.133), channel_id=1, source_target_pairs={{0,1},{1,0},{2,3},{3,2},{4,5},{5,4},{6,7},{7,6},{8,9},{9,8},{10,11... | collective-permute-start | bytes 2654216 | tf_op jit(solution)/shard_map/swap_b/ppermute | solution.py:318
  96.5 31.4 %collective-permute-start.14 = (bf16[1,144,384]{2,1,0:T(8,128)(2,1)S(1)}, bf16[1,144,384]{2,1,0:T(8,128)(2,1)S(1)}, u32[]{:S(2)}, u32[]{:S(2)}) collective-permute-start(bf16[1,144,384]{2,1,0:T(8,128)(2,1)S(1)} %get-tuple-element.70), channel_id=1, source_target_pairs={{0,32},{32,0},{64,96},{96,64},{1,33},{33,1},{65,97},{97,65},{2,34}... | collective-permute-start | bytes 331784 | tf_op jit(solution)/shard_map/plane_sum/ppermute | solution.py:313
  96.9 31.0 %collective-permute-start.15 = (bf16[1,144,384]{2,1,0:T(8,128)(2,1)S(1)}, bf16[1,144,384]{2,1,0:T(8,128)(2,1)S(1)}, u32[]{:S(2)}, u32[]{:S(2)}) collective-permute-start(bf16[1,144,384]{2,1,0:T(8,128)(2,1)S(1)} %get-tuple-element.71), channel_id=1, source_target_pairs={{0,64},{32,96},{64,0},{96,32},{1,65},{33,97},{65,1},{97,33},{2,66}... | collective-permute-start | bytes 331784 | tf_op jit(solution)/shard_map/plane_sum/ppermute | solution.py:313
  100.0 28.0 %collective-permute-start.16 = (bf16[1,144,384]{2,1,0:T(8,128)(2,1)S(1)}, bf16[1,144,384]{2,1,0:T(8,128)(2,1)S(1)}, u32[]{:S(2)}, u32[]{:S(2)}) collective-permute-start(bf16[1,144,384]{2,1,0:T(8,128)(2,1)S(1)} %get-tuple-element.72), channel_id=1, source_target_pairs={{0,96},{32,64},{64,32},{96,0},{1,97},{33,65},{65,33},{97,1},{2,98}... | collective-permute-start | bytes 331784 | tf_op jit(solution)/shard_map/plane_sum/ppermute | solution.py:313
  101.3 26.9 %collective-permute-start.12 = (bf16[1536,128]{1,0:T(8,128)(2,1)S(1)}, bf16[1536,128]{1,0:T(8,128)(2,1)S(1)}, u32[]{:S(2)}, u32[]{:S(2)}) collective-permute-start(bf16[1536,128]{1,0:T(8,128)(2,1)S(1)} %slice.134), channel_id=1, source_target_pairs={{0,32},{32,64},{64,96},{96,0},{1,33},{33,65},{65,97},{97,1},{2,34}... | collective-permute-start | bytes 1179656 | tf_op jit(solution)/shard_map/ring_x_far/ppermute | solution.py:308
  101.4 26.8 %collective-permute-start.13 = (bf16[1536,128]{1,0:T(8,128)(2,1)S(1)}, bf16[1536,128]{1,0:T(8,128)(2,1)S(1)}, u32[]{:S(2)}, u32[]{:S(2)}) collective-permute-start(bf16[1536,128]{1,0:T(8,128)(2,1)S(1)} %slice.135), channel_id=1, source_target_pairs={{0,96},{32,0},{64,32},{96,64},{1,97},{33,1},{65,33},{97,65},{2,98}... | collective-permute-start | bytes 1179656 | tf_op jit(solution)/shard_map/ring_x_far/ppermute | solution.py:308
  134.9 7.5 %collective-permute-start.17 = (f32[1,144,1536]{2,1,0:T(8,128)S(1)}, f32[1,144,1536]{2,1,0:T(8,128)}, u32[]{:S(2)}, u32[]{:S(2)}) collective-permute-start(f32[1,144,1536]{2,1,0:T(8,128)S(1)} %get-tuple-element.81), channel_id=1, source_target_pairs={{0,1},{1,0},{2,3},{3,2},{4,5},{5,4},{6,7},{7,6},{8,9},{9,8},{10,11... | collective-permute-start | bytes 2654216 | tf_op jit(solution)/shard_map/swap_a/ppermute | solution.py:318
  134.9 24.4 %slice-start = ((s8[6553600]{0:T(1024)(128)(4,1)}), s8[4194304]{0:T(1024)(128)(4,1)S(1)}, s32[]{:S(2)}) async-start(s8[6553600]{0:T(1024)(128)(4,1)} %bitcast.75), calls=%async_computation.2 | async-start | bytes 8388608
  166.5 9.0 %collective-permute-start.20 = (bf16[48,2560]{1,0:T(8,128)(2,1)S(1)}, bf16[48,2560]{1,0:T(8,128)(2,1)S(1)}, u32[]{:S(2)}, u32[]{:S(2)}) collective-permute-start(bf16[48,2560]{1,0:T(8,128)(2,1)S(1)} %get-tuple-element.100), channel_id=1, source_target_pairs={{0,6},{2,0},{4,2},{6,4},{1,7},{3,1},{5,3},{7,5},{8,14},{10,8},{12,... | collective-permute-start | bytes 737288 | tf_op jit(solution)/shard_map/sum_y/ppermute | solution.py:308
  166.6 10.2 %collective-permute-start.21 = (bf16[48,2560]{1,0:T(8,128)(2,1)S(1)}, bf16[48,2560]{1,0:T(8,128)(2,1)S(1)}, u32[]{:S(2)}, u32[]{:S(2)}) collective-permute-start(bf16[48,2560]{1,0:T(8,128)(2,1)S(1)} %get-tuple-element.99), channel_id=1, source_target_pairs={{0,2},{2,4},{4,6},{6,0},{1,3},{3,5},{5,7},{7,1},{8,10},{10,12},{12... | collective-permute-start | bytes 737288 | tf_op jit(solution)/shard_map/sum_y/ppermute | solution.py:308
  168.7 10.5 %collective-permute-start.18 = (bf16[48,2560]{1,0:T(8,128)(2,1)S(1)}, bf16[48,2560]{1,0:T(8,128)(2,1)S(1)}, u32[]{:S(2)}, u32[]{:S(2)}) collective-permute-start(bf16[48,2560]{1,0:T(8,128)(2,1)S(1)} %get-tuple-element.102), channel_id=1, source_target_pairs={{0,6},{2,0},{4,2},{6,4},{1,7},{3,1},{5,3},{7,5},{8,14},{10,8},{12,... | collective-permute-start | bytes 737288 | tf_op jit(solution)/shard_map/sum_y/ppermute | solution.py:308
  170.0 10.4 %collective-permute-start.19 = (bf16[48,2560]{1,0:T(8,128)(2,1)S(1)}, bf16[48,2560]{1,0:T(8,128)(2,1)S(1)}, u32[]{:S(2)}, u32[]{:S(2)}) collective-permute-start(bf16[48,2560]{1,0:T(8,128)(2,1)S(1)} %get-tuple-element.101), channel_id=1, source_target_pairs={{0,2},{2,4},{4,6},{6,0},{1,3},{3,5},{5,7},{7,1},{8,10},{10,12},{12... | collective-permute-start | bytes 737288 | tf_op jit(solution)/shard_map/sum_y/ppermute | solution.py:308
  (11 other events, 64.8 us)

commit v2 on v1

--- a/solution.py
+++ b/solution.py
@@ -20,7 +20,7 @@
 RING = ("z", "yh", "yl")
 Y = ("yh", "yl")
 ALL = ("x", "z", "yh", "yl", "c")
-PROJECT_VMEM = 20
+WIDTH = 1280
 CHUNKS = 2
 NEAR = (0, 3, 1, 2)
 ROWS = 144
@@ -31,7 +31,7 @@
     return jnp.max(jnp.sum(wide * wide, axis=1, keepdims=True))
 
 
-def attention_kernel(*refs, first, count, parts, sub, small):
+def attention_kernel(*refs, first, count, parts, sub, small, skip):
     q_ref, mt_ref = refs[0], refs[1]
     sources = refs[2 : 2 + count]
     if first:
@@ -39,7 +39,7 @@
         state_out, norm_out = refs[2 + count :]
     else:
         norm_in, state_in, state_out, norm_out = refs[2 + count :]
-    tiles, rows, _ = q_ref.shape
+    _, rows, _ = q_ref.shape
 
     def joined(slices):
         return slices[0] if len(slices) == 1 else jnp.concatenate(slices, axis=0)
@@ -62,14 +62,15 @@
         key_norm = jnp.maximum(key_norm, square_norm_max(sources[k_source][k_at : k_at + keys, :]))
     all_keys = sum(part[4] for part in parts)
 
-    @pl.loop(0, tiles)
-    def _(tile):
+    @pl.loop(0, state_out.shape[0])
+    def _(at_tile):
+        tile = at_tile + skip
         query_norm = square_norm_max(q_ref[tile]) if first else jnp.max(norm_in[tile])
         bounded = jnp.logical_and(query_norm >= 0.0, query_norm * key_norm <= (BOUND / SCALE) ** 2)
         place = lax.broadcasted_iota(jnp.int32, (rows, HS), 0) // sub
         one_hot = jnp.where(place == lax.broadcasted_iota(jnp.int32, (rows, HS), 1), 1.0, 0.0).astype(jnp.bfloat16)
         query = jnp.concatenate([q_ref[tile], one_hot], axis=1)
-        norm_out[tile] = jnp.full((8, HS), jnp.where(bounded, query_norm, -1.0), jnp.float32)
+        norm_out[at_tile] = jnp.full((8, HS), jnp.where(bounded, query_norm, -1.0), jnp.float32)
 
         @pl.when(bounded)
         def _():
@@ -81,17 +82,17 @@
             if not first:
                 total = state_in[tile, HS : HS + 1, :] + total
                 weighted = state_in[tile, :HS, :] + weighted
-            state_out[tile, :HS, :] = weighted
-            state_out[tile, HS : HS + 8, :] = jnp.broadcast_to(total, (8, rows))
-            state_out[tile, HS + 8 :, :] = jnp.zeros((8, rows), jnp.float32)
+            state_out[at_tile, :HS, :] = weighted
+            state_out[at_tile, HS : HS + 8, :] = jnp.broadcast_to(total, (8, rows))
+            state_out[at_tile, HS + 8 :, :] = jnp.zeros((8, rows), jnp.float32)
 
         @pl.when(jnp.logical_not(bounded))
         def _():
             if first:
-                state_out[tile, : HS + 8, :] = jnp.zeros((HS + 8, rows), jnp.float32)
-                state_out[tile, HS + 8 :, :] = jnp.full((8, rows), NEG, jnp.float32)
+                state_out[at_tile, : HS + 8, :] = jnp.zeros((HS + 8, rows), jnp.float32)
+                state_out[at_tile, HS + 8 :, :] = jnp.full((8, rows), NEG, jnp.float32)
             else:
-                state_out[tile] = state_in[tile]
+                state_out[at_tile] = state_in[tile]
             mask_base = 0
             for k_source, k_at, v_source, v_at, keys in parts:
 
@@ -101,35 +102,36 @@
                     value = sources[v_source][pl.ds(pl.multiple_of(v_at + j * small, small), small), :]
                     mask_at = pl.multiple_of(mask_base + j * (small // sub), 8)
                     found = scores(with_masks(key, tile, mask_at, small), query)
-                    top = state_out[tile, HS + 8 : HS + 9, :]
+                    top = state_out[at_tile, HS + 8 : HS + 9, :]
                     new_top = jnp.maximum(top, jnp.max(found, axis=0, keepdims=True))
                     factor = jnp.exp2((top - new_top) * LOG2)
                     weights = jnp.exp2((found - new_top) * LOG2)
-                    total = state_out[tile, HS : HS + 1, :] * factor + jnp.sum(weights, axis=0, keepdims=True)
-                    state_out[tile, HS : HS + 8, :] = jnp.broadcast_to(total, (8, rows))
-                    state_out[tile, :HS, :] = state_out[tile, :HS, :] * factor + mixed(value, weights)
-                    state_out[tile, HS + 8 :, :] = jnp.broadcast_to(new_top, (8, rows))
+                    total = state_out[at_tile, HS : HS + 1, :] * factor + jnp.sum(weights, axis=0, keepdims=True)
+                    state_out[at_tile, HS : HS + 8, :] = jnp.broadcast_to(total, (8, rows))
+                    state_out[at_tile, :HS, :] = state_out[at_tile, :HS, :] * factor + mixed(value, weights)
+                    state_out[at_tile, HS + 8 :, :] = jnp.broadcast_to(new_top, (8, rows))
 
                 mask_base += keys // sub
 
 
-def attention(name, query, masks, sub, sources, parts, state=None, small=256):
-    tiles, rows, _ = query.shape
-    first = state is None
+def attention(name, query, masks, sub, sources, parts, state=None, small=256, skip=0, tiles=None, cost=1024):
+    rows = query.shape[1]
+    first, whole = state is None, tiles is None
+    tiles = query.shape[0] if whole else tiles
     operands = [query, masks, *sources]
     if not first:
         operands += [state[1], state[0]]
     return pl.pallas_call(
         functools.partial(
-            attention_kernel, first=first, count=len(sources), parts=tuple(parts), sub=sub, small=small
+            attention_kernel, first=first, count=len(sources), parts=tuple(parts), sub=sub, small=small, skip=skip
         ),
         out_shape=[
             jax.ShapeDtypeStruct((tiles, ROWS, rows), jnp.float32),
             jax.ShapeDtypeStruct((tiles, 8, HS), jnp.float32),
         ],
-        input_output_aliases={} if first else {len(operands) - 1: 0},
-        cost_estimate=pl.CostEstimate(flops=1024, bytes_accessed=1024, transcendentals=0),
-        compiler_params=pltpu.CompilerParams(vmem_limit_bytes=28 * 2**20),
+        input_output_aliases={} if first or not whole else {len(operands) - 1: 0},
+        cost_estimate=pl.CostEstimate(flops=cost, bytes_accessed=1024, transcendentals=0),
+        compiler_params=pltpu.CompilerParams(vmem_limit_bytes=20 * 2**20),
         name=name,
     )(*operands)
 
@@ -155,13 +157,13 @@
         out_ref[tile * rows : (tile + 1) * rows, :] = jnp.transpose(mixed / total).astype(jnp.bfloat16)
 
 
-def merge(name, *states):
+def merge(name, *states, cost=1024):
     tiles, _, rows = states[-1].shape
     return pl.pallas_call(
         merge_kernel,
         name=name,
         out_shape=jax.ShapeDtypeStruct((tiles * rows, HS), jnp.bfloat16),
-        cost_estimate=pl.CostEstimate(flops=1024, bytes_accessed=1024, transcendentals=0),
+        cost_estimate=pl.CostEstimate(flops=cost, bytes_accessed=1024, transcendentals=0),
         compiler_params=pltpu.CompilerParams(vmem_limit_bytes=32 * 2**20),
     )(*states)
 
@@ -207,23 +209,27 @@
 
 
 def outgoing_kernel(*refs):
-    sources, out_ref = refs[:-1], refs[-1]
+    *sources, out_ref, held, semaphores = refs
+    count = len(sources)
     token_rows = sources[0].shape[0]
     piece = token_rows // 4
-    at = len(sources) * token_rows
-    for z in range(4):
-        for yh in range(2):
-            for yl in range(2):
-                target = (z * 2 + yh) * 2 + yl
-                head = 10 * yl + 2 * z + yh
-                for i, source in enumerate(sources):
-                    out_ref[target, i * token_rows : (i + 1) * token_rows, :] = source[:, head * HS : (head + 1) * HS]
-                head = 10 * yl + 8 + yh
-                pieces = [
-                    source[:, head * HS : (head + 1) * HS].astype(jnp.float32)[z * piece : (z + 1) * piece]
-                    for source in sources
-                ]
-                out_ref[target, at:, :] = jnp.concatenate(pieces, axis=0).astype(jnp.bfloat16)
+    at = count * token_rows
+    copies = [pltpu.make_async_copy(source, held.at[i], semaphores.at[i]) for i, source in enumerate(sources)]
+    for copy in copies:
+        copy.start()
+    chips = [(z, yh, yl) for z in range(4) for yh in range(2) for yl in range(2)]
+    for i, copy in enumerate(copies):
+        copy.wait()
+        for z, yh, yl in chips:
+            head = 10 * yl + 2 * z + yh
+            target = (z * 2 + yh) * 2 + yl
+            out_ref[target, i * token_rows : (i + 1) * token_rows, :] = held[i, :, head * HS : (head + 1) * HS]
+    for z, yh, yl in chips:
+        head = 10 * yl + 8 + yh
+        pieces = [
+            held[i, :, head * HS : (head + 1) * HS].astype(jnp.float32)[z * piece : (z + 1) * piece] for i in range(count)
+        ]
+        out_ref[(z * 2 + yh) * 2 + yl, at:, :] = jnp.concatenate(pieces, axis=0).astype(jnp.bfloat16)
 
 
 def outgoing(name, *arrays):
@@ -231,76 +237,69 @@
     return pl.pallas_call(
         outgoing_kernel,
         name=name,
+        in_specs=[pl.BlockSpec(memory_space=pl.ANY)] * len(arrays),
         out_shape=jax.ShapeDtypeStruct((16, rows, HS), jnp.bfloat16),
+        scratch_shapes=[
+            pltpu.VMEM((len(arrays), *arrays[0].shape), jnp.bfloat16),
+            pltpu.SemaphoreType.DMA((len(arrays),)),
+        ],
         cost_estimate=pl.CostEstimate(flops=1024, bytes_accessed=1024, transcendentals=0),
-        compiler_params=pltpu.CompilerParams(vmem_limit_bytes=16 * 2**20),
+        compiler_params=pltpu.CompilerParams(vmem_limit_bytes=60 * 2**20),
     )(*arrays)
 
 
-def project_kernel(core_ref, att_ref, own_w, side_w, kept_ref, sent_ref):
+def project_kernel(core_ref, att_ref, own_w, side_w, kept_ref, above_ref, below_ref, held, semaphores, *, start):
     core = core_ref[0]
-    kept = kept_ref.shape[0]
+    kept, half = kept_ref.shape[0], above_ref.shape[0]
+    steps = kept_ref.shape[1] // WIDTH
+
+    def columns(j, base=0):
+        return pl.ds(pl.multiple_of(base + j * WIDTH, HS), WIDTH)
+
+    def arriving(j):
+        return pltpu.make_async_copy(side_w.at[:, columns(j, start)], held.at[j], semaphores.at[j])
+
+    for j in range(steps):
+        arriving(j).start()
 
     def group(number):
         return jnp.concatenate([att_ref[number * 5 + i] for i in range(5)], axis=1)
 
-    total = jnp.dot(group(core), own_w[...], preferred_element_type=jnp.float32)
-    total = total + jnp.dot(group(1 - core), side_w[...], preferred_element_type=jnp.float32)
-    kept_ref[...] = total[:kept]
-    sent_ref[...] = total[kept:].astype(jnp.bfloat16)
-
-
-def project(core, attended, own_w, side_w, start, columns, width=1280):
-    heads, rows, _ = attended.shape
-    depth = own_w.shape[0]
-    first = start // width
-    w_spec = pl.BlockSpec((depth, width), lambda j: (0, j + first))
-    out_spec = pl.BlockSpec((rows // 2, width), lambda j: (0, j))
+    own, side = group(core), group(1 - core)
+
+    @pl.loop(0, steps)
+    def _(j):
+        total = jnp.dot(own, own_w[:, columns(j, start)], preferred_element_type=jnp.float32)
+        arriving(j).wait()
+        total = total + jnp.dot(side, held[j], preferred_element_type=jnp.float32)
+        kept_ref[:, columns(j)] = total[:kept].astype(jnp.bfloat16)
+        above_ref[:, columns(j)] = total[kept : kept + half].astype(jnp.bfloat16)
+        below_ref[:, columns(j)] = total[kept + half :].astype(jnp.bfloat16)
+
+
+def project(core, attended, own_w, side_w, start, columns):
+    rows, steps = attended.shape[1], columns // WIDTH
     return pl.pallas_call(
-        project_kernel,
-        grid=(columns // width,),
+        functools.partial(project_kernel, start=start),
+        name="project",
         in_specs=[
             pl.BlockSpec(memory_space=pltpu.SMEM),
-            pl.BlockSpec((heads, rows, HS), lambda j: (0, 0, 0)),
-            w_spec,
-            w_spec,
+            pl.BlockSpec(memory_space=pltpu.VMEM),
+            pl.BlockSpec(memory_space=pltpu.VMEM),
+            pl.BlockSpec(memory_space=pl.ANY),
         ],
-        out_specs=[out_spec, out_spec],
         out_shape=[
-            jax.ShapeDtypeStruct((rows // 2, columns), jnp.float32),
             jax.ShapeDtypeStruct((rows // 2, columns), jnp.bfloat16),
+            jax.ShapeDtypeStruct((rows // 4, columns), jnp.bfloat16),
+            jax.ShapeDtypeStruct((rows // 4, columns), jnp.bfloat16),
+        ],
+        scratch_shapes=[
+            pltpu.VMEM((steps, side_w.shape[0], WIDTH), jnp.bfloat16),
+            pltpu.SemaphoreType.DMA((steps,)),
         ],
         cost_estimate=pl.CostEstimate(flops=1024, bytes_accessed=1024, transcendentals=0),
-        compiler_params=pltpu.CompilerParams(vmem_limit_bytes=PROJECT_VMEM * 2**20),
-        name="project",
+        compiler_params=pltpu.CompilerParams(vmem_limit_bytes=24 * 2**20),
     )(core, attended, own_w, side_w)
-
-
-def finish_kernel(*refs):
-    kept, above, below, out_ref = refs[0], refs[1], refs[2], refs[-1]
-    half = above.shape[0]
-    out_ref[:half, :] = (kept[:half] + above[...].astype(jnp.float32)).astype(jnp.bfloat16)
-    out_ref[half:, :] = (kept[half:] + below[...].astype(jnp.float32)).astype(jnp.bfloat16)
-
-
-def finish(index, parts, whole=None):
-    rows, columns = parts[0].shape
-    half = rows // 2
-    specs = [pl.BlockSpec((rows, columns), lambda i: (0, 0))] + [pl.BlockSpec((half, columns), lambda i: (0, 0))] * 2
-    operands = list(parts)
-    if whole is not None:
-        specs.append(pl.BlockSpec(memory_space=pl.ANY))
-        operands.append(whole)
-    return pl.pallas_call(
-        finish_kernel,
-        name="finish",
-        grid=(1,),
-        in_specs=specs,
-        out_specs=pl.BlockSpec((rows, columns), lambda i: (0, index)),
-        out_shape=jax.ShapeDtypeStruct((rows, columns * CHUNKS), jnp.bfloat16),
-        input_output_aliases={} if whole is None else {3: 0},
-        compiler_params=pltpu.CompilerParams(vmem_limit_bytes=16 * 2**20),
-    )(*operands)
 
 
 def ring(array, axes, size, shift, name="ring"):
@@ -338,7 +337,7 @@
         return (frames(at_x) + within[None]).reshape(-1)
 
     ring_keys = jnp.concatenate([ring_blocks((x + i) % 4, core) for i in NEAR])
-    plane_keys = jnp.concatenate([plane_blocks(x, core, z ^ i) for i in range(4)])
+    plane_keys = jnp.concatenate([plane_blocks(x, core, z ^ i) for i in (0, 2, 1, 3)])
     blocks = jnp.arange(block_mask.shape[0], dtype=jnp.int32)
     pad = jnp.zeros((32,), jnp.int32)
     ring_queries, plane_queries = [], []
@@ -385,7 +384,7 @@
     ring_left, ring_right = ring(ring_kv, "x", 4, 1, "ring_x"), ring(ring_kv, "x", 4, -1, "ring_x")
     query_a = jnp.stack([ring_q, swap(ring_q, "swap_q")])
 
-    plane_kv = [plane_kv] + [cross(plane_kv, "z", i, "plane_z") for i in (1, 2, 3)]
+    plane_kv = [plane_kv] + [cross(plane_kv, "z", i, "plane_z") for i in (2, 1, 3)]
     plane_q = jnp.concatenate([plane_q] + [cross(plane_q, "x", i, "plane_q") for i in (1, 2, 3)], axis=0)
     query_b = jnp.concatenate([plane_q, swap(plane_q, "swap_plane_q")], axis=0).reshape(4, 2 * plane_rows, HS)
     query_a, query_b = lax.optimization_barrier((query_a, query_b))
@@ -395,28 +394,28 @@
     query_b, state = lax.optimization_barrier((query_b, state))
     plane_state = attention("plane", query_b, plane_masks, 8, plane_kv, plane_parts, small=128)
 
-    plane_state, ring_left, ring_right = lax.optimization_barrier((plane_state, ring_left, ring_right))
+    plane_state, state, ring_left, ring_right = lax.optimization_barrier((plane_state, state, ring_left, ring_right))
     other_b = swap(plane_state[0][2:], "swap_b")
-    plane_part = fold(plane_state[0], other_b, plane_rows)
-    plane_part, state, ring_left, ring_right = lax.optimization_barrier((plane_part, state, ring_left, ring_right))
     middle = ring_kv.shape[0] // 2
     ring_far = [
         ring(ring_left[:middle], "x", 4, 1, "ring_x_far"),
         ring(ring_right[middle:], "x", 4, -1, "ring_x_far"),
     ]
+    state = attention("left", query_a, ring_masks[:, 48:96], 32, [ring_left], whole, state)
+    own_part, other_b, state = lax.optimization_barrier((plane_state[0], other_b, state))
+    plane_part = fold(own_part, other_b, plane_rows)
+    plane_part, state = lax.optimization_barrier((plane_part, state))
     plane_part = [plane_part[0]] + [cross(plane_part[i], "x", i, "plane_sum") for i in (1, 2, 3)]
-    state = attention("left", query_a, ring_masks[:, 48:96], 32, [ring_left], whole, state)
     state = attention("right", query_a, ring_masks[:, 96:144], 32, [ring_right], whole, state)
     out_b = merge("merge_plane", *plane_part).reshape(4, 2, 2, piece, HS)
     out_b, state = lax.optimization_barrier((out_b, state))
     far = [(0, 0, 1, 0, ring_rows)]
-    side = attention(
-        "far_side", query_a[1:], ring_masks[1:, 144:], 32, ring_far, far, (state[0][1:], state[1][1:])
-    )
+    far_masks = ring_masks[:, 144:]
+    side = attention("far_side", query_a, far_masks, 32, ring_far, far, state, skip=1, tiles=1)
     other_a = swap(side[0], "swap_a")
     state, side = lax.optimization_barrier((state, side))
-    state = attention("far_own", query_a[:1], ring_masks[:1, 144:], 32, ring_far, far, (state[0][:1], state[1][:1]))
-    out_a = merge("merge_ring", state[0], other_a).reshape(4, 2, 2, token_rows, HS)
+    own = attention("far_own", query_a, far_masks, 32, ring_far, far, state, skip=0, tiles=1)
+    out_a = merge("merge_ring", own[0], other_a, cost=1 << 32).reshape(4, 2, 2, token_rows, HS)
 
     def split(array):
         first, second = array[:, :, 0], array[:, :, 1]
@@ -439,14 +438,15 @@
     plane_back = back[:, rows:].reshape(4, 2, 2, piece, HS).transpose(1, 2, 0, 3, 4).reshape(2, rows, HS)
     attended = jnp.concatenate([back[:, :rows], plane_back], axis=0)
 
-    out = None
+    outs = []
     columns = w_out.shape[1] // CHUNKS
     for i in range(CHUNKS):
-        kept, sent = project(core[None], attended, w_out, side_w, i * columns, columns)
-        from_above = ring(sent[:half], Y, 4, -1, "sum_y")
-        from_below = ring(sent[half:], Y, 4, 1, "sum_y")
-        out = finish(i, (kept, from_above, from_below), out)
-    return out
+        kept, to_below, to_above = project(core[None], attended, w_out, side_w, i * columns, columns)
+        from_above, from_below = ring(to_below, Y, 4, -1, "sum_y"), ring(to_above, Y, 4, 1, "sum_y")
+        other = jnp.concatenate([from_above, from_below], axis=0)
+        out = (kept.astype(jnp.float32) + other.astype(jnp.float32)).astype(jnp.bfloat16)
+        outs.append(out if i == CHUNKS - 1 else lax.optimization_barrier(out))
+    return outs[0] if CHUNKS == 1 else jnp.concatenate(outs, axis=1)
 
 
 def solution(mesh):

time: 182 us -> 173 us (0.951)
  local copies, waits for them, and re-layouts: 6.97 us -> 2.18 us
  waiting for transfers between devices: 35 us -> 31.8 us
    unnamed x28 -> x16, local copies, waits for them, and re-layouts: 4.04 us -> 0.09 us
    pallas_call x5 -> x3, Pallas kernels: 10.3 us -> 9.5 us  [the longest x2 6.82 us: project(): pl.pallas_call(functools.partial(project_kernel, start=start), name='proj...]
  transfers between devices with their start and end apart: 23 -> 23, of which waited for: 9 -> 7; matrix products, arithmetic and copies ran while one was open for 2% -> 2% of each run, Pallas kernels for 40% -> 44%
where the time goes in v2:
time: 173 us
  Pallas kernels  88.6 us (51%)
  starting transfers between devices  31.8 us (18%)
  waiting for transfers between devices  31.8 us (18%)
  blocking collectives  14.8 us (9%)
  local copies, waits for them, and re-layouts  2.18 us (1%)
  other arithmetic  2.15 us (1%)
    pallas_call x6, Pallas kernels, attention(): pl.pallas_call(functools.partial(attention_kernel, first=first, count=len...  77.2 us
    all_to_all x1, waiting for transfers between devices, local(): lax.all_to_all(outgoing('outgoing', keys, values, queries), RING, 0, 0)  21.6 us
    all_to_all x1, blocking collectives, local(): back = lax.all_to_all(back, ('z', 'yh'), 0, 0)  14.8 us
    ppermute x9, starting transfers between devices, cross(): return lax.ppermute(array, axis, [(i, i ^ bit) for i in range(4)])  12.8 us
    ppermute x8, starting transfers between devices, ring(): lax.ppermute(array, axes, [(i, (i + shift) % size) for i in range(size)])  10.3 us
    all_to_all x1, starting transfers between devices, local(): lax.all_to_all(outgoing('outgoing', keys, values, queries), RING, 0, 0)  8.28 us
    ppermute x8, waiting for transfers between devices, ring(): lax.ppermute(array, axes, [(i, (i + shift) % size) for i in range(size)])  7.07 us
    pallas_call x2, Pallas kernels, project(): pl.pallas_call(functools.partial(project_kernel, start=start), name='proj...  6.82 us
  transfers between devices with their start and end apart: 23, of which 7 were waited for; matrix products, arithmetic and copies ran while one was open for 2% of the time, Pallas kernels for 44%

profile of v2, /device:TPU:0, one launch (start us, length us, event | category | flops | bytes accessed | tf_op | source)
XLA Modules:
  0.0 173.1 jit_solution(7414989661117587918)
XLA Ops:
  0.0 2.7 %outgoing.1 = bf16[16,360,128]{2,1,0:T(8,128)(2,1)} custom-call(bf16[96,2560]{1,0:T(8,128)(2,1)} %refs_0_.1, bf16[96,2560]{1,0:T(8,128)(2,1)} %refs_1_.1, bf16[96,2560]{1,0:T(8,128)(2,1)} %refs_2_.1), custom_call_target="tpu_custom_call" | custom-call | flops 1024 | bytes 1024 | tf_op jit(solution)/shard_map/spread/outgoing/pallas_call | solution.py:237
  2.7 8.3 %all-to-all-start = ((bf16[16,360,128]{2,1,0:T(8,128)(2,1)}), bf16[16,360,128]{2,1,0:T(8,128)(2,1)S(1)}, u32[]{:S(2)}, u32[]{:S(2)}) async-start(bf16[16,360,128]{2,1,0:T(8,128)(2,1)} %outgoing.1), calls=%async_computation | async-start | bytes 2949120 | tf_op jit(solution)/shard_map/spread/all_to_all | solution.py:371
  14.3 21.6 %all-to-all-done = bf16[16,360,128]{2,1,0:T(8,128)(2,1)S(1)} async-done(((bf16[16,360,128]{2,1,0:T(8,128)(2,1)}), bf16[16,360,128]{2,1,0:T(8,128)(2,1)S(1)}, u32[]{:S(2)}, u32[]{:S(2)}) %all-to-all-start) | async-done | bytes 1474592 | tf_op jit(solution)/shard_map/spread/all_to_all | solution.py:371
  36.2 1.6 collective-permute-start.2
  37.8 2.7 %collective-permute-start.3 = (bf16[384,128]{1,0:T(8,128)(2,1)S(1)}, bf16[384,128]{1,0:T(8,128)(2,1)S(1)}, u32[]{:S(2)}, u32[]{:S(2)}) collective-permute-start(bf16[384,128]{1,0:T(8,128)(2,1)S(1)} %bitcast.94), channel_id=1, source_target_pairs={{0,64},{32,96},{64,0},{96,32},{1,65},{33,97},{65,1},{97,33},{2,66}... | collective-permute-start | bytes 294920 | tf_op jit(solution)/shard_map/plane_q/ppermute | solution.py:312
  41.0 2.8 %collective-permute-start.10 = (bf16[3072,128]{1,0:T(8,128)(2,1)S(1)}, bf16[3072,128]{1,0:T(8,128)(2,1)S(1)}, u32[]{:S(2)}, u32[]{:S(2)}) collective-permute-start(bf16[3072,128]{1,0:T(8,128)(2,1)S(1)} %bitcast.77), channel_id=1, source_target_pairs={{0,96},{32,0},{64,32},{96,64},{1,97},{33,1},{65,33},{97,65},{2,98}... | collective-permute-start | bytes 2359304 | tf_op jit(solution)/shard_map/ring_x/ppermute | solution.py:307
  48.8 1.7 %collective-permute-start.8 = (bf16[768,128]{1,0:T(8,128)(2,1)S(1)}, bf16[768,128]{1,0:T(8,128)(2,1)S(1)}, u32[]{:S(2)}, u32[]{:S(2)}) collective-permute-start(bf16[768,128]{1,0:T(8,128)(2,1)S(1)} %bitcast.88), channel_id=1, source_target_pairs={{0,24},{8,16},{16,8},{24,0},{1,25},{9,17},{17,9},{25,1},{2,26},{10... | collective-permute-start | bytes 589832 | tf_op jit(solution)/shard_map/plane_z/ppermute | solution.py:312
  50.6 11.9 %own.1 = (f32[2,144,1536]{2,1,0:T(8,128)S(1)}, f32[2,8,128]{2,1,0:T(8,128)S(1)}) custom-call(bf16[2,1536,128]{2,1,0:T(8,128)(2,1)S(1)} %pad_maximum_fusion.2.refs_0_, f32[2,48,128]{2,1,0:T(8,128)S(1)} %get-tuple-element.113.refs_1_, bf16[3072,128]{1,0:T(8,128)(2,1)S(1)} %bitcast.79), custom_call_target="tpu_custom_call" | custom-call | flops 1024 | bytes 1024 | tf_op jit(solution)/shard_map/own/pallas_call | solution.py:124
  62.5 29.1 %plane.1 = (f32[4,144,768]{2,1,0:T(8,128)S(1)}, f32[4,8,128]{2,1,0:T(8,128)}) custom-call(bf16[4,768,128]{2,1,0:T(8,128)(2,1)S(1)} %bitcast.85, f32[4,192,128]{2,1,0:T(8,128)S(1)} %fusion.refs_1_, bf16[768,128]{1,0:T(8,128)(2,1)S(1)} %bitcast.89, bf16[768,128]{1,0:T(8,128)(2,1)S(1)} %collective-permute-done.6.refs_3_, ...), custom_call_target="tpu_custom_call" | custom-call | flops 1024 | bytes 1024 | tf_op jit(solution)/shard_map/plane/pallas_call | solution.py:124
  92.5 3.0 %collective-permute-start.12 = (bf16[1536,128]{1,0:T(8,128)(2,1)S(1)}, bf16[1536,128]{1,0:T(8,128)(2,1)S(1)}, u32[]{:S(2)}, u32[]{:S(2)}) collective-permute-start(bf16[1536,128]{1,0:T(8,128)(2,1)S(1)} %slice.100), channel_id=1, source_target_pairs={{0,96},{32,0},{64,32},{96,64},{1,97},{33,1},{65,33},{97,65},{2,98}... | collective-permute-start | bytes 1179656 | tf_op jit(solution)/shard_map/ring_x_far/ppermute | solution.py:307
  95.4 11.6 %left.1 = (f32[2,144,1536]{2,1,0:T(8,128)S(1)}, f32[2,8,128]{2,1,0:T(8,128)S(1)}) custom-call(bf16[2,1536,128]{2,1,0:T(8,128)(2,1)S(1)} %pad_maximum_fusion.2.refs_0_, f32[2,48,128]{2,1,0:T(8,128)S(1)} %get-tuple-element.112.refs_1_, bf16[3072,128]{1,0:T(8,128)(2,1)S(1)} %collective-permute-done.9.refs_2_, ...), custom_call_target="tpu_custom_call", output_to_operand_aliasing={{0}: (4, {})} | custom-call | flops 1024 | bytes 1024 | tf_op jit(solution)/shard_map/left/pallas_call | solution.py:124
  107.3 2.0 %collective-permute-start.15 = (bf16[1,144,384]{2,1,0:T(8,128)(2,1)S(1)}, bf16[1,144,384]{2,1,0:T(8,128)(2,1)S(1)}, u32[]{:S(2)}, u32[]{:S(2)}) collective-permute-start(bf16[1,144,384]{2,1,0:T(8,128)(2,1)S(1)} %get-tuple-element.83), channel_id=1, source_target_pairs={{0,64},{32,96},{64,0},{96,32},{1,65},{33,97},{65,1},{97,33},{2,66}... | collective-permute-start | bytes 331784 | tf_op jit(solution)/shard_map/plane_sum/ppermute | solution.py:312
  109.3 2.7 %collective-permute-start.16 = (bf16[1,144,384]{2,1,0:T(8,128)(2,1)S(1)}, bf16[1,144,384]{2,1,0:T(8,128)(2,1)S(1)}, u32[]{:S(2)}, u32[]{:S(2)}) collective-permute-start(bf16[1,144,384]{2,1,0:T(8,128)(2,1)S(1)} %get-tuple-element.84), channel_id=1, source_target_pairs={{0,96},{32,64},{64,32},{96,0},{1,97},{33,65},{65,33},{97,1},{2,98}... | collective-permute-start | bytes 331784 | tf_op jit(solution)/shard_map/plane_sum/ppermute | solution.py:312
  111.9 11.6 %right.1 = (f32[2,144,1536]{2,1,0:T(8,128)S(1)}, f32[2,8,128]{2,1,0:T(8,128)S(1)}) custom-call(bf16[2,1536,128]{2,1,0:T(8,128)(2,1)S(1)} %pad_maximum_fusion.2.refs_0_, f32[2,48,128]{2,1,0:T(8,128)S(1)} %get-tuple-element.111.refs_1_, bf16[3072,128]{1,0:T(8,128)(2,1)S(1)} %collective-permute-done.10.refs_2_, ...), custom_call_target="tpu_custom_call", output_to_operand_aliasing={{0}: (4, {})} | custom-call | flops 1024 | bytes 1024 | tf_op jit(solution)/shard_map/right/pallas_call | solution.py:124
  123.7 6.7 %far_side.1 = (f32[1,144,1536]{2,1,0:T(8,128)}, f32[1,8,128]{2,1,0:T(8,128)}) custom-call(bf16[2,1536,128]{2,1,0:T(8,128)(2,1)S(1)} %pad_maximum_fusion.2.refs_0_, f32[2,48,128]{2,1,0:T(8,128)S(1)} %get-tuple-element.114.refs_1_, bf16[1536,128]{1,0:T(8,128)(2,1)S(1)} %collective-permute-done.11.refs_2_, ...), custom_call_target="tpu_custom_call" | custom-call | flops 1024 | bytes 1024 | tf_op jit(solution)/shard_map/far_side/pallas_call | solution.py:124
  130.4 6.4 %far_own.1 = (f32[1,144,1536]{2,1,0:T(8,128)S(1)}, f32[1,8,128]{2,1,0:T(8,128)}) custom-call(bf16[2,1536,128]{2,1,0:T(8,128)(2,1)S(1)} %pad_maximum_fusion.2.refs_0_, f32[2,48,128]{2,1,0:T(8,128)S(1)} %get-tuple-element.114.refs_1_, bf16[1536,128]{1,0:T(8,128)(2,1)S(1)} %collective-permute-done.11.refs_2_, ...), custom_call_target="tpu_custom_call" | custom-call | flops 1024 | bytes 1024 | tf_op jit(solution)/shard_map/far_own/pallas_call | solution.py:124
  136.9 1.5 merge_ring.1
  138.7 14.8 %all_to_all.10 = bf16[8,240,128]{2,1,0:T(8,128)(2,1)S(1)} all-to-all(bf16[8,240,128]{2,1,0:T(8,128)(2,1)S(1)} %bitcast.92), channel_id=1, replica_groups=mesh['x'=4,'z'=4,'yh'=2,'yl'=2,'c'=2] {'z','yh'}, dimensions={0} | all-to-all | bytes 983040 | tf_op jit(solution)/shard_map/return/all_to_all | solution.py:436
  153.7 3.4 %project.2 = (bf16[96,2560]{1,0:T(8,128)(2,1)S(1)}, bf16[48,2560]{1,0:T(8,128)(2,1)S(1)}, bf16[48,2560]{1,0:T(8,128)(2,1)S(1)}) custom-call(s32[1]{0:T(128)} %bitcast.core_ref, bf16[10,192,128]{2,1,0:T(8,128)(2,1)S(1)} %pad_maximum_fusion.3.att_ref, bf16[640,5120]{1,0:T(8,128)(2,1)S(1)} %bitcast.76, bf16[640,5120]{1,0:T(8,128)(2,1)} %collective-permute-done.side_w), custom_call_target="tpu_custom_call" | custom-call | flops 1024 | bytes 1024 | tf_op jit(solution)/shard_map/project/pallas_call | solution.py:282
  157.2 2.0 %collective-permute-start.19 = (bf16[48,2560]{1,0:T(8,128)(2,1)S(1)}, bf16[48,2560]{1,0:T(8,128)(2,1)S(1)}, u32[]{:S(2)}, u32[]{:S(2)}) collective-permute-start(bf16[48,2560]{1,0:T(8,128)(2,1)S(1)} %get-tuple-element.99), channel_id=1, source_target_pairs={{0,2},{2,4},{4,6},{6,0},{1,3},{3,5},{5,7},{7,1},{8,10},{10,12},{12... | collective-permute-start | bytes 737288 | tf_op jit(solution)/shard_map/sum_y/ppermute | solution.py:307
  159.2 3.4 %project.3 = (bf16[96,2560]{1,0:T(8,128)(2,1)S(1)}, bf16[48,2560]{1,0:T(8,128)(2,1)S(1)}, bf16[48,2560]{1,0:T(8,128)(2,1)S(1)}) custom-call(s32[1]{0:T(128)} %bitcast.core_ref, bf16[10,192,128]{2,1,0:T(8,128)(2,1)S(1)} %pad_maximum_fusion.3.att_ref, bf16[640,5120]{1,0:T(8,128)(2,1)S(1)} %bitcast.76, bf16[640,5120]{1,0:T(8,128)(2,1)} %collective-permute-done.side_w), custom_call_target="tpu_custom_call" | custom-call | flops 1024 | bytes 1024 | tf_op jit(solution)/shard_map/project/pallas_call | solution.py:282
  162.6 1.4 collective-permute-start.20
  165.9 3.9 %collective-permute-done.20 = bf16[48,2560]{1,0:T(8,128)(2,1)S(1)} collective-permute-done((bf16[48,2560]{1,0:T(8,128)(2,1)S(1)}, bf16[48,2560]{1,0:T(8,128)(2,1)S(1)}, u32[]{:S(2)}, u32[]{:S(2)}) %collective-permute-start.20) | collective-permute-done | bytes 245792 | tf_op jit(solution)/shard_map/sum_y/ppermute | solution.py:307
  169.7 2.2 %collective-permute-done.21 = bf16[48,2560]{1,0:T(8,128)(2,1)S(1)} collective-permute-done((bf16[48,2560]{1,0:T(8,128)(2,1)S(1)}, bf16[48,2560]{1,0:T(8,128)(2,1)S(1)}, u32[]{:S(2)}, u32[]{:S(2)}) %collective-permute-start.21) | collective-permute-done | bytes 245792 | tf_op jit(solution)/shard_map/sum_y/ppermute | solution.py:307
  (109 shorter events, 13.5 us)
Async XLA Ops:
  0.0 36.2 %collective-permute-start = (bf16[640,5120]{1,0:T(8,128)(2,1)}, bf16[640,5120]{1,0:T(8,128)(2,1)}, u32[]{:S(2)}, u32[]{:S(2)}) collective-permute-start(bf16[640,5120]{1,0:T(8,128)(2,1)} %own_w.3), channel_id=1, source_target_pairs={{0,1},{1,0},{2,3},{3,2},{4,5},{5,4},{6,7},{7,6},{8,9},{9,8},{10,11... | collective-permute-start | bytes 19660808 | tf_op jit(solution)/shard_map/side_w/ppermute | solution.py:317
  2.7 33.3 %all-to-all-start = ((bf16[16,360,128]{2,1,0:T(8,128)(2,1)}), bf16[16,360,128]{2,1,0:T(8,128)(2,1)S(1)}, u32[]{:S(2)}, u32[]{:S(2)}) async-start(bf16[16,360,128]{2,1,0:T(8,128)(2,1)} %outgoing.1), calls=%async_computation | async-start | bytes 2949120 | tf_op jit(solution)/shard_map/spread/all_to_all | solution.py:371
  36.2 7.6 %collective-permute-start.2 = (bf16[384,128]{1,0:T(8,128)(2,1)S(1)}, bf16[384,128]{1,0:T(8,128)(2,1)S(1)}, u32[]{:S(2)}, u32[]{:S(2)}) collective-permute-start(bf16[384,128]{1,0:T(8,128)(2,1)S(1)} %bitcast.93), channel_id=1, source_target_pairs={{0,32},{32,0},{64,96},{96,64},{1,33},{33,1},{65,97},{97,65},{2,34}... | collective-permute-start | bytes 294920 | tf_op jit(solution)/shard_map/plane_q/ppermute | solution.py:312
  37.8 7.2 %collective-permute-start.3 = (bf16[384,128]{1,0:T(8,128)(2,1)S(1)}, bf16[384,128]{1,0:T(8,128)(2,1)S(1)}, u32[]{:S(2)}, u32[]{:S(2)}) collective-permute-start(bf16[384,128]{1,0:T(8,128)(2,1)S(1)} %bitcast.94), channel_id=1, source_target_pairs={{0,64},{32,96},{64,0},{96,32},{1,65},{33,97},{65,1},{97,33},{2,66}... | collective-permute-start | bytes 294920 | tf_op jit(solution)/shard_map/plane_q/ppermute | solution.py:312
  40.5 6.4 %collective-permute-start.4 = (bf16[384,128]{1,0:T(8,128)(2,1)S(1)}, bf16[384,128]{1,0:T(8,128)(2,1)S(1)}, u32[]{:S(2)}, u32[]{:S(2)}) collective-permute-start(bf16[384,128]{1,0:T(8,128)(2,1)S(1)} %bitcast.95), channel_id=1, source_target_pairs={{0,96},{32,64},{64,32},{96,0},{1,97},{33,65},{65,33},{97,1},{2,98}... | collective-permute-start | bytes 294920 | tf_op jit(solution)/shard_map/plane_q/ppermute | solution.py:312
  41.0 50.6 %collective-permute-start.10 = (bf16[3072,128]{1,0:T(8,128)(2,1)S(1)}, bf16[3072,128]{1,0:T(8,128)(2,1)S(1)}, u32[]{:S(2)}, u32[]{:S(2)}) collective-permute-start(bf16[3072,128]{1,0:T(8,128)(2,1)S(1)} %bitcast.77), channel_id=1, source_target_pairs={{0,96},{32,0},{64,32},{96,64},{1,97},{33,1},{65,33},{97,65},{2,98}... | collective-permute-start | bytes 2359304 | tf_op jit(solution)/shard_map/ring_x/ppermute | solution.py:307
  43.8 47.9 %collective-permute-start.9 = (bf16[3072,128]{1,0:T(8,128)(2,1)S(1)}, bf16[3072,128]{1,0:T(8,128)(2,1)S(1)}, u32[]{:S(2)}, u32[]{:S(2)}) collective-permute-start(bf16[3072,128]{1,0:T(8,128)(2,1)S(1)} %bitcast.78), channel_id=1, source_target_pairs={{0,32},{32,64},{64,96},{96,0},{1,33},{33,65},{65,97},{97,1},{2,34}... | collective-permute-start | bytes 2359304 | tf_op jit(solution)/shard_map/ring_x/ppermute | solution.py:307
  43.8 3.3 %collective-permute-start.1 = (bf16[1536,128]{1,0:T(8,128)(2,1)S(1)}, bf16[1536,128]{1,0:T(8,128)(2,1)S(1)}, u32[]{:S(2)}, u32[]{:S(2)}) collective-permute-start(bf16[1536,128]{1,0:T(8,128)(2,1)S(1)} %bitcast.90), channel_id=1, source_target_pairs={{0,1},{1,0},{2,3},{3,2},{4,5},{5,4},{6,7},{7,6},{8,9},{9,8},{10,11... | collective-permute-start | bytes 1179656 | tf_op jit(solution)/shard_map/swap_q/ppermute | solution.py:317
  45.0 17.5 %collective-permute-start.6 = (bf16[768,128]{1,0:T(8,128)(2,1)S(1)}, bf16[768,128]{1,0:T(8,128)(2,1)S(1)}, u32[]{:S(2)}, u32[]{:S(2)}) collective-permute-start(bf16[768,128]{1,0:T(8,128)(2,1)S(1)} %bitcast.86), channel_id=1, source_target_pairs={{0,16},{8,24},{16,0},{24,8},{1,17},{9,25},{17,1},{25,9},{2,18},{10... | collective-permute-start | bytes 589832 | tf_op jit(solution)/shard_map/plane_z/ppermute | solution.py:312
  47.0 1.8 %collective-permute-start.5 = (bf16[1536,128]{1,0:T(8,128)(2,1)S(1)}, bf16[1536,128]{1,0:T(8,128)(2,1)S(1)}, u32[]{:S(2)}, u32[]{:S(2)}) collective-permute-start(bf16[1536,128]{1,0:T(8,128)(2,1)S(1)} %pad_maximum_fusion.4), channel_id=1, source_target_pairs={{0,1},{1,0},{2,3},{3,2},{4,5},{5,4},{6,7},{7,6},{8,9},{9,8},{10,11... | collective-permute-start | bytes 1179656 | tf_op jit(solution)/shard_map/swap_plane_q/ppermute | solution.py:317
  47.1 15.4 %collective-permute-start.7 = (bf16[768,128]{1,0:T(8,128)(2,1)S(1)}, bf16[768,128]{1,0:T(8,128)(2,1)S(1)}, u32[]{:S(2)}, u32[]{:S(2)}) collective-permute-start(bf16[768,128]{1,0:T(8,128)(2,1)S(1)} %bitcast.87), channel_id=1, source_target_pairs={{0,8},{8,0},{16,24},{24,16},{1,9},{9,1},{17,25},{25,17},{2,10},{10... | collective-permute-start | bytes 589832 | tf_op jit(solution)/shard_map/plane_z/ppermute | solution.py:312
  48.8 13.8 %collective-permute-start.8 = (bf16[768,128]{1,0:T(8,128)(2,1)S(1)}, bf16[768,128]{1,0:T(8,128)(2,1)S(1)}, u32[]{:S(2)}, u32[]{:S(2)}) collective-permute-start(bf16[768,128]{1,0:T(8,128)(2,1)S(1)} %bitcast.88), channel_id=1, source_target_pairs={{0,24},{8,16},{16,8},{24,0},{1,25},{9,17},{17,9},{25,1},{2,26},{10... | collective-permute-start | bytes 589832 | tf_op jit(solution)/shard_map/plane_z/ppermute | solution.py:312
  91.7 15.3 %collective-permute-start.13 = (f32[2,144,768]{2,1,0:T(8,128)S(1)}, f32[2,144,768]{2,1,0:T(8,128)S(1)}, u32[]{:S(2)}, u32[]{:S(2)}) collective-permute-start(f32[2,144,768]{2,1,0:T(8,128)S(1)} %slice.101), channel_id=1, source_target_pairs={{0,1},{1,0},{2,3},{3,2},{4,5},{5,4},{6,7},{7,6},{8,9},{9,8},{10,11... | collective-permute-start | bytes 2654216 | tf_op jit(solution)/shard_map/swap_b/ppermute | solution.py:317
  92.0 31.7 %collective-permute-start.11 = (bf16[1536,128]{1,0:T(8,128)(2,1)S(1)}, bf16[1536,128]{1,0:T(8,128)(2,1)S(1)}, u32[]{:S(2)}, u32[]{:S(2)}) collective-permute-start(bf16[1536,128]{1,0:T(8,128)(2,1)S(1)} %slice.99), channel_id=1, source_target_pairs={{0,32},{32,64},{64,96},{96,0},{1,33},{33,65},{65,97},{97,1},{2,34}... | collective-permute-start | bytes 1179656 | tf_op jit(solution)/shard_map/ring_x_far/ppermute | solution.py:307
  92.5 31.3 %collective-permute-start.12 = (bf16[1536,128]{1,0:T(8,128)(2,1)S(1)}, bf16[1536,128]{1,0:T(8,128)(2,1)S(1)}, u32[]{:S(2)}, u32[]{:S(2)}) collective-permute-start(bf16[1536,128]{1,0:T(8,128)(2,1)S(1)} %slice.100), channel_id=1, source_target_pairs={{0,96},{32,0},{64,32},{96,64},{1,97},{33,1},{65,33},{97,65},{2,98}... | collective-permute-start | bytes 1179656 | tf_op jit(solution)/shard_map/ring_x_far/ppermute | solution.py:307
  107.2 16.3 %collective-permute-start.14 = (bf16[1,144,384]{2,1,0:T(8,128)(2,1)S(1)}, bf16[1,144,384]{2,1,0:T(8,128)(2,1)S(1)}, u32[]{:S(2)}, u32[]{:S(2)}) collective-permute-start(bf16[1,144,384]{2,1,0:T(8,128)(2,1)S(1)} %get-tuple-element.82), channel_id=1, source_target_pairs={{0,32},{32,0},{64,96},{96,64},{1,33},{33,1},{65,97},{97,65},{2,34}... | collective-permute-start | bytes 331784 | tf_op jit(solution)/shard_map/plane_sum/ppermute | solution.py:312
  107.3 16.3 %collective-permute-start.15 = (bf16[1,144,384]{2,1,0:T(8,128)(2,1)S(1)}, bf16[1,144,384]{2,1,0:T(8,128)(2,1)S(1)}, u32[]{:S(2)}, u32[]{:S(2)}) collective-permute-start(bf16[1,144,384]{2,1,0:T(8,128)(2,1)S(1)} %get-tuple-element.83), channel_id=1, source_target_pairs={{0,64},{32,96},{64,0},{96,32},{1,65},{33,97},{65,1},{97,33},{2,66}... | collective-permute-start | bytes 331784 | tf_op jit(solution)/shard_map/plane_sum/ppermute | solution.py:312
  109.3 14.3 %collective-permute-start.16 = (bf16[1,144,384]{2,1,0:T(8,128)(2,1)S(1)}, bf16[1,144,384]{2,1,0:T(8,128)(2,1)S(1)}, u32[]{:S(2)}, u32[]{:S(2)}) collective-permute-start(bf16[1,144,384]{2,1,0:T(8,128)(2,1)S(1)} %get-tuple-element.84), channel_id=1, source_target_pairs={{0,96},{32,64},{64,32},{96,0},{1,97},{33,65},{65,33},{97,1},{2,98}... | collective-permute-start | bytes 331784 | tf_op jit(solution)/shard_map/plane_sum/ppermute | solution.py:312
  130.4 6.4 %collective-permute-start.17 = (f32[1,144,1536]{2,1,0:T(8,128)}, f32[1,144,1536]{2,1,0:T(8,128)}, u32[]{:S(2)}, u32[]{:S(2)}) collective-permute-start(f32[1,144,1536]{2,1,0:T(8,128)} %get-tuple-element.91), channel_id=1, source_target_pairs={{0,1},{1,0},{2,3},{3,2},{4,5},{5,4},{6,7},{7,6},{8,9},{9,8},{10,11... | collective-permute-start | bytes 2654216 | tf_op jit(solution)/shard_map/swap_a/ppermute | solution.py:317
  136.9 16.8 %slice-start = ((s8[6553600]{0:T(1024)(128)(4,1)}), s8[4194304]{0:T(1024)(128)(4,1)S(1)}, s32[]{:S(2)}) async-start(s8[6553600]{0:T(1024)(128)(4,1)} %bitcast.75), calls=%async_computation.2 | async-start | bytes 8388608
  157.1 7.6 %collective-permute-start.18 = (bf16[48,2560]{1,0:T(8,128)(2,1)S(1)}, bf16[48,2560]{1,0:T(8,128)(2,1)S(1)}, u32[]{:S(2)}, u32[]{:S(2)}) collective-permute-start(bf16[48,2560]{1,0:T(8,128)(2,1)S(1)} %get-tuple-element.98), channel_id=1, source_target_pairs={{0,6},{2,0},{4,2},{6,4},{1,7},{3,1},{5,3},{7,5},{8,14},{10,8},{12,... | collective-permute-start | bytes 737288 | tf_op jit(solution)/shard_map/sum_y/ppermute | solution.py:307
  157.2 8.5 %collective-permute-start.19 = (bf16[48,2560]{1,0:T(8,128)(2,1)S(1)}, bf16[48,2560]{1,0:T(8,128)(2,1)S(1)}, u32[]{:S(2)}, u32[]{:S(2)}) collective-permute-start(bf16[48,2560]{1,0:T(8,128)(2,1)S(1)} %get-tuple-element.99), channel_id=1, source_target_pairs={{0,2},{2,4},{4,6},{6,0},{1,3},{3,5},{5,7},{7,1},{8,10},{10,12},{12... | collective-permute-start | bytes 737288 | tf_op jit(solution)/shard_map/sum_y/ppermute | solution.py:307
  162.6 7.1 %collective-permute-start.20 = (bf16[48,2560]{1,0:T(8,128)(2,1)S(1)}, bf16[48,2560]{1,0:T(8,128)(2,1)S(1)}, u32[]{:S(2)}, u32[]{:S(2)}) collective-permute-start(bf16[48,2560]{1,0:T(8,128)(2,1)S(1)} %get-tuple-element.101), channel_id=1, source_target_pairs={{0,6},{2,0},{4,2},{6,4},{1,7},{3,1},{5,3},{7,5},{8,14},{10,8},{12,... | collective-permute-start | bytes 737288 | tf_op jit(solution)/shard_map/sum_y/ppermute | solution.py:307
  164.0 7.9 %collective-permute-start.21 = (bf16[48,2560]{1,0:T(8,128)(2,1)S(1)}, bf16[48,2560]{1,0:T(8,128)(2,1)S(1)}, u32[]{:S(2)}, u32[]{:S(2)}) collective-permute-start(bf16[48,2560]{1,0:T(8,128)(2,1)S(1)} %get-tuple-element.102), channel_id=1, source_target_pairs={{0,2},{2,4},{4,6},{6,0},{1,3},{3,5},{5,7},{7,1},{8,10},{10,12},{12... | collective-permute-start | bytes 737288 | tf_op jit(solution)/shard_map/sum_y/ppermute | solution.py:307
  (5 other events, 52.9 us)

commit v3 on v2

--- a/solution.py
+++ b/solution.py
@@ -57,34 +57,29 @@
             value, weights.astype(jnp.bfloat16), (((0,), (0,)), ((), ())), preferred_element_type=jnp.float32
         )
 
-    key_norm = jnp.float32(0.0)
-    for k_source, k_at, _, _, keys in parts:
-        key_norm = jnp.maximum(key_norm, square_norm_max(sources[k_source][k_at : k_at + keys, :]))
     all_keys = sum(part[4] for part in parts)
 
     @pl.loop(0, state_out.shape[0])
     def _(at_tile):
         tile = at_tile + skip
-        query_norm = square_norm_max(q_ref[tile]) if first else jnp.max(norm_in[tile])
-        bounded = jnp.logical_and(query_norm >= 0.0, query_norm * key_norm <= (BOUND / SCALE) ** 2)
         place = lax.broadcasted_iota(jnp.int32, (rows, HS), 0) // sub
         one_hot = jnp.where(place == lax.broadcasted_iota(jnp.int32, (rows, HS), 1), 1.0, 0.0).astype(jnp.bfloat16)
         query = jnp.concatenate([q_ref[tile], one_hot], axis=1)
+        key = joined([sources[k][at : at + keys, :] for k, at, _, _, keys in parts])
+        value = joined([sources[v][at : at + keys, :] for _, _, v, at, keys in parts])
+        weights = jnp.exp2(scores(with_masks(key, tile, 0, all_keys), query) * LOG2)
+        total = jnp.sum(weights, axis=0, keepdims=True)
+        weighted = mixed(value, weights)
+        if not first:
+            total = state_in[tile, HS : HS + 1, :] + total
+            weighted = state_in[tile, :HS, :] + weighted
+        state_out[at_tile, :HS, :] = weighted
+        state_out[at_tile, HS : HS + 8, :] = jnp.broadcast_to(total, (8, rows))
+        state_out[at_tile, HS + 8 :, :] = jnp.broadcast_to(jnp.where(total > 0.0, 0.0, NEG), (8, rows))
+
+        query_norm = square_norm_max(q_ref[tile]) if first else jnp.max(norm_in[tile])
+        bounded = jnp.logical_and(query_norm >= 0.0, query_norm * square_norm_max(key) <= (BOUND / SCALE) ** 2)
         norm_out[at_tile] = jnp.full((8, HS), jnp.where(bounded, query_norm, -1.0), jnp.float32)
-
-        @pl.when(bounded)
-        def _():
-            key = joined([sources[k][at : at + keys, :] for k, at, _, _, keys in parts])
-            value = joined([sources[v][at : at + keys, :] for _, _, v, at, keys in parts])
-            weights = jnp.exp2(scores(with_masks(key, tile, 0, all_keys), query) * LOG2)
-            total = jnp.sum(weights, axis=0, keepdims=True)
-            weighted = mixed(value, weights)
-            if not first:
-                total = state_in[tile, HS : HS + 1, :] + total
-                weighted = state_in[tile, :HS, :] + weighted
-            state_out[at_tile, :HS, :] = weighted
-            state_out[at_tile, HS : HS + 8, :] = jnp.broadcast_to(total, (8, rows))
-            state_out[at_tile, HS + 8 :, :] = jnp.zeros((8, rows), jnp.float32)
 
         @pl.when(jnp.logical_not(bounded))
         def _():
@@ -116,8 +111,8 @@
 
 def attention(name, query, masks, sub, sources, parts, state=None, small=256, skip=0, tiles=None, cost=1024):
     rows = query.shape[1]
-    first, whole = state is None, tiles is None
-    tiles = query.shape[0] if whole else tiles
+    first = state is None
+    tiles = query.shape[0] if tiles is None else tiles
     operands = [query, masks, *sources]
     if not first:
         operands += [state[1], state[0]]
@@ -129,7 +124,6 @@
             jax.ShapeDtypeStruct((tiles, ROWS, rows), jnp.float32),
             jax.ShapeDtypeStruct((tiles, 8, HS), jnp.float32),
         ],
-        input_output_aliases={} if first or not whole else {len(operands) - 1: 0},
         cost_estimate=pl.CostEstimate(flops=cost, bytes_accessed=1024, transcendentals=0),
         compiler_params=pltpu.CompilerParams(vmem_limit_bytes=20 * 2**20),
         name=name,
@@ -164,7 +158,7 @@
         name=name,
         out_shape=jax.ShapeDtypeStruct((tiles * rows, HS), jnp.bfloat16),
         cost_estimate=pl.CostEstimate(flops=cost, bytes_accessed=1024, transcendentals=0),
-        compiler_params=pltpu.CompilerParams(vmem_limit_bytes=32 * 2**20),
+        compiler_params=pltpu.CompilerParams(vmem_limit_bytes=12 * 2**20),
     )(*states)
 
 
@@ -204,32 +198,45 @@
         name="fold",
         out_shape=[jax.ShapeDtypeStruct((1, ROWS, width), jnp.bfloat16)] * (tiles * rows // width),
         cost_estimate=pl.CostEstimate(flops=1024, bytes_accessed=1024, transcendentals=0),
-        compiler_params=pltpu.CompilerParams(vmem_limit_bytes=32 * 2**20),
+        compiler_params=pltpu.CompilerParams(vmem_limit_bytes=12 * 2**20),
     )(own, other)
 
 
 def outgoing_kernel(*refs):
-    *sources, out_ref, held, semaphores = refs
+    *sources, out_ref, held, chunks, semaphores, leave = refs
     count = len(sources)
     token_rows = sources[0].shape[0]
     piece = token_rows // 4
     at = count * token_rows
-    copies = [pltpu.make_async_copy(source, held.at[i], semaphores.at[i]) for i, source in enumerate(sources)]
-    for copy in copies:
-        copy.start()
-    chips = [(z, yh, yl) for z in range(4) for yh in range(2) for yl in range(2)]
-    for i, copy in enumerate(copies):
-        copy.wait()
-        for z, yh, yl in chips:
-            head = 10 * yl + 2 * z + yh
-            target = (z * 2 + yh) * 2 + yl
-            out_ref[target, i * token_rows : (i + 1) * token_rows, :] = held[i, :, head * HS : (head + 1) * HS]
-    for z, yh, yl in chips:
+    depth = token_rows // 3
+
+    def arriving(i):
+        cuts = [pl.ds(j * depth, depth) for j in range(3)]
+        return [
+            pltpu.make_async_copy(sources[i].at[cut], held.at[i, cut], semaphores.at[i, j]) for j, cut in enumerate(cuts)
+        ]
+
+    for i in range(count):
+        for copy in arriving(i):
+            copy.start()
+    for i in range(count):
+        for copy in arriving(i):
+            copy.wait()
+    leaving = []
+    for target in range(16):
+        z, yh, yl = target // 4, target // 2 % 2, target % 2
+        head = 10 * yl + 2 * z + yh
+        for i in range(count):
+            chunks[target, i * token_rows : (i + 1) * token_rows, :] = held[i, :, head * HS : (head + 1) * HS]
         head = 10 * yl + 8 + yh
         pieces = [
             held[i, :, head * HS : (head + 1) * HS].astype(jnp.float32)[z * piece : (z + 1) * piece] for i in range(count)
         ]
-        out_ref[(z * 2 + yh) * 2 + yl, at:, :] = jnp.concatenate(pieces, axis=0).astype(jnp.bfloat16)
+        chunks[target, at:, :] = jnp.concatenate(pieces, axis=0).astype(jnp.bfloat16)
+        leaving.append(pltpu.make_async_copy(chunks.at[target], out_ref.at[target], leave.at[target]))
+        leaving[-1].start()
+    for copy in leaving:
+        copy.wait()
 
 
 def outgoing(name, *arrays):
@@ -238,10 +245,13 @@
         outgoing_kernel,
         name=name,
         in_specs=[pl.BlockSpec(memory_space=pl.ANY)] * len(arrays),
+        out_specs=pl.BlockSpec(memory_space=pl.ANY),
         out_shape=jax.ShapeDtypeStruct((16, rows, HS), jnp.bfloat16),
         scratch_shapes=[
             pltpu.VMEM((len(arrays), *arrays[0].shape), jnp.bfloat16),
-            pltpu.SemaphoreType.DMA((len(arrays),)),
+            pltpu.VMEM((16, rows, HS), jnp.bfloat16),
+            pltpu.SemaphoreType.DMA((len(arrays), 3)),
+            pltpu.SemaphoreType.DMA((16,)),
         ],
         cost_estimate=pl.CostEstimate(flops=1024, bytes_accessed=1024, transcendentals=0),
         compiler_params=pltpu.CompilerParams(vmem_limit_bytes=60 * 2**20),

time: 173 us -> 191 us (1.10)
  Pallas kernels: 88.6 us -> 106 us
    pallas_call x6, Pallas kernels: 77.2 us -> 94.8 us  [attention(): pl.pallas_call(functools.partial(attention_kernel, first=first, count=len...]
  transfers between devices with their start and end apart: 23 -> 23, of which waited for: 7 -> 7; matrix products, arithmetic and copies ran while one was open for 2% -> 2% of each run, Pallas kernels for 44% -> 49%
where the time goes in v3:
time: 191 us
  Pallas kernels  106 us (55%)
  starting transfers between devices  31.8 us (17%)
  waiting for transfers between devices  31.8 us (17%)
  blocking collectives  14.8 us (8%)
  local copies, waits for them, and re-layouts  2.18 us (1%)
  other arithmetic  2.15 us (1%)
    pallas_call x6, Pallas kernels, attention(): pl.pallas_call(functools.partial(attention_kernel, first=first, count=len...  94.8 us
    all_to_all x1, waiting for transfers between devices, local(): lax.all_to_all(outgoing('outgoing', keys, values, queries), RING, 0, 0)  21.6 us
    all_to_all x1, blocking collectives, local(): back = lax.all_to_all(back, ('z', 'yh'), 0, 0)  14.8 us
    ppermute x9, starting transfers between devices, cross(): return lax.ppermute(array, axis, [(i, i ^ bit) for i in range(4)])  12.8 us
    ppermute x8, starting transfers between devices, ring(): lax.ppermute(array, axes, [(i, (i + shift) % size) for i in range(size)])  10.5 us
    all_to_all x1, starting transfers between devices, local(): lax.all_to_all(outgoing('outgoing', keys, values, queries), RING, 0, 0)  8.28 us
    ppermute x8, waiting for transfers between devices, ring(): lax.ppermute(array, axes, [(i, (i + shift) % size) for i in range(size)])  7.08 us
    pallas_call x2, Pallas kernels, project(): pl.pallas_call(functools.partial(project_kernel, start=start), name='proj...  6.82 us
  transfers between devices with their start and end apart: 23, of which 7 were waited for; matrix products, arithmetic and copies ran while one was open for 2% of the time, Pallas kernels for 49%

profile of v3, /device:TPU:0, one launch (start us, length us, event | category | flops | bytes accessed | tf_op | source)
XLA Modules:
  0.0 190.8 jit_solution(7620815894661808225)
XLA Ops:
  0.0 2.9 %outgoing.1 = bf16[16,360,128]{2,1,0:T(8,128)(2,1)} custom-call(bf16[96,2560]{1,0:T(8,128)(2,1)} %refs_0_.1, bf16[96,2560]{1,0:T(8,128)(2,1)} %refs_1_.1, bf16[96,2560]{1,0:T(8,128)(2,1)} %refs_2_.1), custom_call_target="tpu_custom_call" | custom-call | flops 1024 | bytes 1024 | tf_op jit(solution)/shard_map/spread/outgoing/pallas_call | solution.py:244
  2.9 8.3 %all-to-all-start = ((bf16[16,360,128]{2,1,0:T(8,128)(2,1)}), bf16[16,360,128]{2,1,0:T(8,128)(2,1)S(1)}, u32[]{:S(2)}, u32[]{:S(2)}) async-start(bf16[16,360,128]{2,1,0:T(8,128)(2,1)} %outgoing.1), calls=%async_computation | async-start | bytes 2949120 | tf_op jit(solution)/shard_map/spread/all_to_all | solution.py:381
  14.5 21.6 %all-to-all-done = bf16[16,360,128]{2,1,0:T(8,128)(2,1)S(1)} async-done(((bf16[16,360,128]{2,1,0:T(8,128)(2,1)}), bf16[16,360,128]{2,1,0:T(8,128)(2,1)S(1)}, u32[]{:S(2)}, u32[]{:S(2)}) %all-to-all-start) | async-done | bytes 1474592 | tf_op jit(solution)/shard_map/spread/all_to_all | solution.py:381
  36.4 1.6 collective-permute-start.2
  38.0 2.7 %collective-permute-start.3 = (bf16[384,128]{1,0:T(8,128)(2,1)S(1)}, bf16[384,128]{1,0:T(8,128)(2,1)S(1)}, u32[]{:S(2)}, u32[]{:S(2)}) collective-permute-start(bf16[384,128]{1,0:T(8,128)(2,1)S(1)} %bitcast.94), channel_id=1, source_target_pairs={{0,64},{32,96},{64,0},{96,32},{1,65},{33,97},{65,1},{97,33},{2,66}... | collective-permute-start | bytes 294920 | tf_op jit(solution)/shard_map/plane_q/ppermute | solution.py:322
  41.2 2.8 %collective-permute-start.10 = (bf16[3072,128]{1,0:T(8,128)(2,1)S(1)}, bf16[3072,128]{1,0:T(8,128)(2,1)S(1)}, u32[]{:S(2)}, u32[]{:S(2)}) collective-permute-start(bf16[3072,128]{1,0:T(8,128)(2,1)S(1)} %bitcast.77), channel_id=1, source_target_pairs={{0,96},{32,0},{64,32},{96,64},{1,97},{33,1},{65,33},{97,65},{2,98}... | collective-permute-start | bytes 2359304 | tf_op jit(solution)/shard_map/ring_x/ppermute | solution.py:317
  49.0 1.7 collective-permute-start.8
  50.8 15.2 %own.1 = (f32[2,144,1536]{2,1,0:T(8,128)S(1)}, f32[2,8,128]{2,1,0:T(8,128)S(1)}) custom-call(bf16[2,1536,128]{2,1,0:T(8,128)(2,1)S(1)} %pad_maximum_fusion.2.refs_0_, f32[2,48,128]{2,1,0:T(8,128)S(1)} %get-tuple-element.113.refs_1_, bf16[3072,128]{1,0:T(8,128)(2,1)S(1)} %bitcast.79), custom_call_target="tpu_custom_call" | custom-call | flops 1024 | bytes 1024 | tf_op jit(solution)/shard_map/own/pallas_call | solution.py:119
  66.0 32.7 %plane.1 = (f32[4,144,768]{2,1,0:T(8,128)S(1)}, f32[4,8,128]{2,1,0:T(8,128)}) custom-call(bf16[4,768,128]{2,1,0:T(8,128)(2,1)S(1)} %bitcast.85, f32[4,192,128]{2,1,0:T(8,128)S(1)} %fusion.refs_1_, bf16[768,128]{1,0:T(8,128)(2,1)S(1)} %bitcast.89, bf16[768,128]{1,0:T(8,128)(2,1)S(1)} %collective-permute-done.6.refs_3_, ...), custom_call_target="tpu_custom_call" | custom-call | flops 1024 | bytes 1024 | tf_op jit(solution)/shard_map/plane/pallas_call | solution.py:119
  99.5 3.0 %collective-permute-start.12 = (bf16[1536,128]{1,0:T(8,128)(2,1)S(1)}, bf16[1536,128]{1,0:T(8,128)(2,1)S(1)}, u32[]{:S(2)}, u32[]{:S(2)}) collective-permute-start(bf16[1536,128]{1,0:T(8,128)(2,1)S(1)} %slice.100), channel_id=1, source_target_pairs={{0,96},{32,0},{64,32},{96,64},{1,97},{33,1},{65,33},{97,65},{2,98}... | collective-permute-start | bytes 1179656 | tf_op jit(solution)/shard_map/ring_x_far/ppermute | solution.py:317
  102.5 15.1 %left.1 = (f32[2,144,1536]{2,1,0:T(8,128)S(1)}, f32[2,8,128]{2,1,0:T(8,128)S(1)}) custom-call(bf16[2,1536,128]{2,1,0:T(8,128)(2,1)S(1)} %pad_maximum_fusion.2.refs_0_, f32[2,48,128]{2,1,0:T(8,128)S(1)} %get-tuple-element.112.refs_1_, bf16[3072,128]{1,0:T(8,128)(2,1)S(1)} %collective-permute-done.9.refs_2_, f32[2,8,128]{2,1,0:T(8,128)S(1)} %get-tuple-element.69.refs_3_, ...), custom_call_target="tpu_custom_call" | custom-call | flops 1024 | bytes 1024 | tf_op jit(solution)/shard_map/left/pallas_call | solution.py:119
  117.9 2.0 %collective-permute-start.15 = (bf16[1,144,384]{2,1,0:T(8,128)(2,1)S(1)}, bf16[1,144,384]{2,1,0:T(8,128)(2,1)S(1)}, u32[]{:S(2)}, u32[]{:S(2)}) collective-permute-start(bf16[1,144,384]{2,1,0:T(8,128)(2,1)S(1)} %get-tuple-element.83), channel_id=1, source_target_pairs={{0,64},{32,96},{64,0},{96,32},{1,65},{33,97},{65,1},{97,33},{2,66}... | collective-permute-start | bytes 331784 | tf_op jit(solution)/shard_map/plane_sum/ppermute | solution.py:322
  119.9 2.7 %collective-permute-start.16 = (bf16[1,144,384]{2,1,0:T(8,128)(2,1)S(1)}, bf16[1,144,384]{2,1,0:T(8,128)(2,1)S(1)}, u32[]{:S(2)}, u32[]{:S(2)}) collective-permute-start(bf16[1,144,384]{2,1,0:T(8,128)(2,1)S(1)} %get-tuple-element.84), channel_id=1, source_target_pairs={{0,96},{32,64},{64,32},{96,0},{1,97},{33,65},{65,33},{97,1},{2,98}... | collective-permute-start | bytes 331784 | tf_op jit(solution)/shard_map/plane_sum/ppermute | solution.py:322
  122.6 15.1 %right.1 = (f32[2,144,1536]{2,1,0:T(8,128)S(1)}, f32[2,8,128]{2,1,0:T(8,128)S(1)}) custom-call(bf16[2,1536,128]{2,1,0:T(8,128)(2,1)S(1)} %pad_maximum_fusion.2.refs_0_, f32[2,48,128]{2,1,0:T(8,128)S(1)} %get-tuple-element.111.refs_1_, bf16[3072,128]{1,0:T(8,128)(2,1)S(1)} %collective-permute-done.10.refs_2_, f32[2,8,128]{2,1,0:T(8,128)S(1)} %get-tuple-element.85.refs_3_, ...), custom_call_target="tpu_custom_call" | custom-call | flops 1024 | bytes 1024 | tf_op jit(solution)/shard_map/right/pallas_call | solution.py:119
  137.9 8.5 %far_side.1 = (f32[1,144,1536]{2,1,0:T(8,128)}, f32[1,8,128]{2,1,0:T(8,128)}) custom-call(bf16[2,1536,128]{2,1,0:T(8,128)(2,1)S(1)} %pad_maximum_fusion.2.refs_0_, f32[2,48,128]{2,1,0:T(8,128)S(1)} %get-tuple-element.114.refs_1_, bf16[1536,128]{1,0:T(8,128)(2,1)S(1)} %collective-permute-done.11.refs_2_, ...), custom_call_target="tpu_custom_call" | custom-call | flops 1024 | bytes 1024 | tf_op jit(solution)/shard_map/far_side/pallas_call | solution.py:119
  146.4 8.1 %far_own.1 = (f32[1,144,1536]{2,1,0:T(8,128)S(1)}, f32[1,8,128]{2,1,0:T(8,128)}) custom-call(bf16[2,1536,128]{2,1,0:T(8,128)(2,1)S(1)} %pad_maximum_fusion.2.refs_0_, f32[2,48,128]{2,1,0:T(8,128)S(1)} %get-tuple-element.114.refs_1_, bf16[1536,128]{1,0:T(8,128)(2,1)S(1)} %collective-permute-done.11.refs_2_, ...), custom_call_target="tpu_custom_call" | custom-call | flops 1024 | bytes 1024 | tf_op jit(solution)/shard_map/far_own/pallas_call | solution.py:119
  154.6 1.5 merge_ring.1
  156.5 14.8 %all_to_all.10 = bf16[8,240,128]{2,1,0:T(8,128)(2,1)S(1)} all-to-all(bf16[8,240,128]{2,1,0:T(8,128)(2,1)S(1)} %bitcast.92), channel_id=1, replica_groups=mesh['x'=4,'z'=4,'yh'=2,'yl'=2,'c'=2] {'z','yh'}, dimensions={0} | all-to-all | bytes 983040 | tf_op jit(solution)/shard_map/return/all_to_all | solution.py:446
  171.4 3.4 %project.2 = (bf16[96,2560]{1,0:T(8,128)(2,1)S(1)}, bf16[48,2560]{1,0:T(8,128)(2,1)S(1)}, bf16[48,2560]{1,0:T(8,128)(2,1)S(1)}) custom-call(s32[1]{0:T(128)} %bitcast.core_ref, bf16[10,192,128]{2,1,0:T(8,128)(2,1)S(1)} %pad_maximum_fusion.3.att_ref, bf16[640,5120]{1,0:T(8,128)(2,1)S(1)} %bitcast.76, bf16[640,5120]{1,0:T(8,128)(2,1)} %collective-permute-done.side_w), custom_call_target="tpu_custom_call" | custom-call | flops 1024 | bytes 1024 | tf_op jit(solution)/shard_map/project/pallas_call | solution.py:292
  174.9 2.0 %collective-permute-start.19 = (bf16[48,2560]{1,0:T(8,128)(2,1)S(1)}, bf16[48,2560]{1,0:T(8,128)(2,1)S(1)}, u32[]{:S(2)}, u32[]{:S(2)}) collective-permute-start(bf16[48,2560]{1,0:T(8,128)(2,1)S(1)} %get-tuple-element.99), channel_id=1, source_target_pairs={{0,2},{2,4},{4,6},{6,0},{1,3},{3,5},{5,7},{7,1},{8,10},{10,12},{12... | collective-permute-start | bytes 737288 | tf_op jit(solution)/shard_map/sum_y/ppermute | solution.py:317
  176.9 3.4 %project.3 = (bf16[96,2560]{1,0:T(8,128)(2,1)S(1)}, bf16[48,2560]{1,0:T(8,128)(2,1)S(1)}, bf16[48,2560]{1,0:T(8,128)(2,1)S(1)}) custom-call(s32[1]{0:T(128)} %bitcast.core_ref, bf16[10,192,128]{2,1,0:T(8,128)(2,1)S(1)} %pad_maximum_fusion.3.att_ref, bf16[640,5120]{1,0:T(8,128)(2,1)S(1)} %bitcast.76, bf16[640,5120]{1,0:T(8,128)(2,1)} %collective-permute-done.side_w), custom_call_target="tpu_custom_call" | custom-call | flops 1024 | bytes 1024 | tf_op jit(solution)/shard_map/project/pallas_call | solution.py:292
  180.4 1.4 collective-permute-start.20
  183.6 3.9 %collective-permute-done.20 = bf16[48,2560]{1,0:T(8,128)(2,1)S(1)} collective-permute-done((bf16[48,2560]{1,0:T(8,128)(2,1)S(1)}, bf16[48,2560]{1,0:T(8,128)(2,1)S(1)}, u32[]{:S(2)}, u32[]{:S(2)}) %collective-permute-start.20) | collective-permute-done | bytes 245792 | tf_op jit(solution)/shard_map/sum_y/ppermute | solution.py:317
  187.5 2.2 %collective-permute-done.21 = bf16[48,2560]{1,0:T(8,128)(2,1)S(1)} collective-permute-done((bf16[48,2560]{1,0:T(8,128)(2,1)S(1)}, bf16[48,2560]{1,0:T(8,128)(2,1)S(1)}, u32[]{:S(2)}, u32[]{:S(2)}) %collective-permute-start.21) | collective-permute-done | bytes 245792 | tf_op jit(solution)/shard_map/sum_y/ppermute | solution.py:317
  (109 shorter events, 13.5 us)
Async XLA Ops:
  0.0 36.4 %collective-permute-start = (bf16[640,5120]{1,0:T(8,128)(2,1)}, bf16[640,5120]{1,0:T(8,128)(2,1)}, u32[]{:S(2)}, u32[]{:S(2)}) collective-permute-start(bf16[640,5120]{1,0:T(8,128)(2,1)} %own_w.3), channel_id=1, source_target_pairs={{0,1},{1,0},{2,3},{3,2},{4,5},{5,4},{6,7},{7,6},{8,9},{9,8},{10,11... | collective-permute-start | bytes 19660808 | tf_op jit(solution)/shard_map/side_w/ppermute | solution.py:327
  2.9 33.3 %all-to-all-start = ((bf16[16,360,128]{2,1,0:T(8,128)(2,1)}), bf16[16,360,128]{2,1,0:T(8,128)(2,1)S(1)}, u32[]{:S(2)}, u32[]{:S(2)}) async-start(bf16[16,360,128]{2,1,0:T(8,128)(2,1)} %outgoing.1), calls=%async_computation | async-start | bytes 2949120 | tf_op jit(solution)/shard_map/spread/all_to_all | solution.py:381
  36.4 7.6 %collective-permute-start.2 = (bf16[384,128]{1,0:T(8,128)(2,1)S(1)}, bf16[384,128]{1,0:T(8,128)(2,1)S(1)}, u32[]{:S(2)}, u32[]{:S(2)}) collective-permute-start(bf16[384,128]{1,0:T(8,128)(2,1)S(1)} %bitcast.93), channel_id=1, source_target_pairs={{0,32},{32,0},{64,96},{96,64},{1,33},{33,1},{65,97},{97,65},{2,34}... | collective-permute-start | bytes 294920 | tf_op jit(solution)/shard_map/plane_q/ppermute | solution.py:322
  38.0 7.2 %collective-permute-start.3 = (bf16[384,128]{1,0:T(8,128)(2,1)S(1)}, bf16[384,128]{1,0:T(8,128)(2,1)S(1)}, u32[]{:S(2)}, u32[]{:S(2)}) collective-permute-start(bf16[384,128]{1,0:T(8,128)(2,1)S(1)} %bitcast.94), channel_id=1, source_target_pairs={{0,64},{32,96},{64,0},{96,32},{1,65},{33,97},{65,1},{97,33},{2,66}... | collective-permute-start | bytes 294920 | tf_op jit(solution)/shard_map/plane_q/ppermute | solution.py:322
  40.7 6.4 %collective-permute-start.4 = (bf16[384,128]{1,0:T(8,128)(2,1)S(1)}, bf16[384,128]{1,0:T(8,128)(2,1)S(1)}, u32[]{:S(2)}, u32[]{:S(2)}) collective-permute-start(bf16[384,128]{1,0:T(8,128)(2,1)S(1)} %bitcast.95), channel_id=1, source_target_pairs={{0,96},{32,64},{64,32},{96,0},{1,97},{33,65},{65,33},{97,1},{2,98}... | collective-permute-start | bytes 294920 | tf_op jit(solution)/shard_map/plane_q/ppermute | solution.py:322
  41.2 57.5 %collective-permute-start.10 = (bf16[3072,128]{1,0:T(8,128)(2,1)S(1)}, bf16[3072,128]{1,0:T(8,128)(2,1)S(1)}, u32[]{:S(2)}, u32[]{:S(2)}) collective-permute-start(bf16[3072,128]{1,0:T(8,128)(2,1)S(1)} %bitcast.77), channel_id=1, source_target_pairs={{0,96},{32,0},{64,32},{96,64},{1,97},{33,1},{65,33},{97,65},{2,98}... | collective-permute-start | bytes 2359304 | tf_op jit(solution)/shard_map/ring_x/ppermute | solution.py:317
  44.0 54.7 %collective-permute-start.9 = (bf16[3072,128]{1,0:T(8,128)(2,1)S(1)}, bf16[3072,128]{1,0:T(8,128)(2,1)S(1)}, u32[]{:S(2)}, u32[]{:S(2)}) collective-permute-start(bf16[3072,128]{1,0:T(8,128)(2,1)S(1)} %bitcast.78), channel_id=1, source_target_pairs={{0,32},{32,64},{64,96},{96,0},{1,33},{33,65},{65,97},{97,1},{2,34}... | collective-permute-start | bytes 2359304 | tf_op jit(solution)/shard_map/ring_x/ppermute | solution.py:317
  44.0 3.3 %collective-permute-start.1 = (bf16[1536,128]{1,0:T(8,128)(2,1)S(1)}, bf16[1536,128]{1,0:T(8,128)(2,1)S(1)}, u32[]{:S(2)}, u32[]{:S(2)}) collective-permute-start(bf16[1536,128]{1,0:T(8,128)(2,1)S(1)} %bitcast.90), channel_id=1, source_target_pairs={{0,1},{1,0},{2,3},{3,2},{4,5},{5,4},{6,7},{7,6},{8,9},{9,8},{10,11... | collective-permute-start | bytes 1179656 | tf_op jit(solution)/shard_map/swap_q/ppermute | solution.py:327
  45.2 20.7 %collective-permute-start.6 = (bf16[768,128]{1,0:T(8,128)(2,1)S(1)}, bf16[768,128]{1,0:T(8,128)(2,1)S(1)}, u32[]{:S(2)}, u32[]{:S(2)}) collective-permute-start(bf16[768,128]{1,0:T(8,128)(2,1)S(1)} %bitcast.86), channel_id=1, source_target_pairs={{0,16},{8,24},{16,0},{24,8},{1,17},{9,25},{17,1},{25,9},{2,18},{10... | collective-permute-start | bytes 589832 | tf_op jit(solution)/shard_map/plane_z/ppermute | solution.py:322
  47.2 1.8 collective-permute-start.5
  47.3 18.6 %collective-permute-start.7 = (bf16[768,128]{1,0:T(8,128)(2,1)S(1)}, bf16[768,128]{1,0:T(8,128)(2,1)S(1)}, u32[]{:S(2)}, u32[]{:S(2)}) collective-permute-start(bf16[768,128]{1,0:T(8,128)(2,1)S(1)} %bitcast.87), channel_id=1, source_target_pairs={{0,8},{8,0},{16,24},{24,16},{1,9},{9,1},{17,25},{25,17},{2,10},{10... | collective-permute-start | bytes 589832 | tf_op jit(solution)/shard_map/plane_z/ppermute | solution.py:322
  49.0 17.0 %collective-permute-start.8 = (bf16[768,128]{1,0:T(8,128)(2,1)S(1)}, bf16[768,128]{1,0:T(8,128)(2,1)S(1)}, u32[]{:S(2)}, u32[]{:S(2)}) collective-permute-start(bf16[768,128]{1,0:T(8,128)(2,1)S(1)} %bitcast.88), channel_id=1, source_target_pairs={{0,24},{8,16},{16,8},{24,0},{1,25},{9,17},{17,9},{25,1},{2,26},{10... | collective-permute-start | bytes 589832 | tf_op jit(solution)/shard_map/plane_z/ppermute | solution.py:322
  98.8 18.8 %collective-permute-start.13 = (f32[2,144,768]{2,1,0:T(8,128)S(1)}, f32[2,144,768]{2,1,0:T(8,128)S(1)}, u32[]{:S(2)}, u32[]{:S(2)}) collective-permute-start(f32[2,144,768]{2,1,0:T(8,128)S(1)} %slice.101), channel_id=1, source_target_pairs={{0,1},{1,0},{2,3},{3,2},{4,5},{5,4},{6,7},{7,6},{8,9},{9,8},{10,11... | collective-permute-start | bytes 2654216 | tf_op jit(solution)/shard_map/swap_b/ppermute | solution.py:327
  98.9 39.0 %collective-permute-start.11 = (bf16[1536,128]{1,0:T(8,128)(2,1)S(1)}, bf16[1536,128]{1,0:T(8,128)(2,1)S(1)}, u32[]{:S(2)}, u32[]{:S(2)}) collective-permute-start(bf16[1536,128]{1,0:T(8,128)(2,1)S(1)} %slice.99), channel_id=1, source_target_pairs={{0,32},{32,64},{64,96},{96,0},{1,33},{33,65},{65,97},{97,1},{2,34}... | collective-permute-start | bytes 1179656 | tf_op jit(solution)/shard_map/ring_x_far/ppermute | solution.py:317
  99.5 38.4 %collective-permute-start.12 = (bf16[1536,128]{1,0:T(8,128)(2,1)S(1)}, bf16[1536,128]{1,0:T(8,128)(2,1)S(1)}, u32[]{:S(2)}, u32[]{:S(2)}) collective-permute-start(bf16[1536,128]{1,0:T(8,128)(2,1)S(1)} %slice.100), channel_id=1, source_target_pairs={{0,96},{32,0},{64,32},{96,64},{1,97},{33,1},{65,33},{97,65},{2,98}... | collective-permute-start | bytes 1179656 | tf_op jit(solution)/shard_map/ring_x_far/ppermute | solution.py:317
  117.8 19.9 %collective-permute-start.14 = (bf16[1,144,384]{2,1,0:T(8,128)(2,1)S(1)}, bf16[1,144,384]{2,1,0:T(8,128)(2,1)S(1)}, u32[]{:S(2)}, u32[]{:S(2)}) collective-permute-start(bf16[1,144,384]{2,1,0:T(8,128)(2,1)S(1)} %get-tuple-element.82), channel_id=1, source_target_pairs={{0,32},{32,0},{64,96},{96,64},{1,33},{33,1},{65,97},{97,65},{2,34}... | collective-permute-start | bytes 331784 | tf_op jit(solution)/shard_map/plane_sum/ppermute | solution.py:322
  117.9 19.8 %collective-permute-start.15 = (bf16[1,144,384]{2,1,0:T(8,128)(2,1)S(1)}, bf16[1,144,384]{2,1,0:T(8,128)(2,1)S(1)}, u32[]{:S(2)}, u32[]{:S(2)}) collective-permute-start(bf16[1,144,384]{2,1,0:T(8,128)(2,1)S(1)} %get-tuple-element.83), channel_id=1, source_target_pairs={{0,64},{32,96},{64,0},{96,32},{1,65},{33,97},{65,1},{97,33},{2,66}... | collective-permute-start | bytes 331784 | tf_op jit(solution)/shard_map/plane_sum/ppermute | solution.py:322
  119.9 17.8 %collective-permute-start.16 = (bf16[1,144,384]{2,1,0:T(8,128)(2,1)S(1)}, bf16[1,144,384]{2,1,0:T(8,128)(2,1)S(1)}, u32[]{:S(2)}, u32[]{:S(2)}) collective-permute-start(bf16[1,144,384]{2,1,0:T(8,128)(2,1)S(1)} %get-tuple-element.84), channel_id=1, source_target_pairs={{0,96},{32,64},{64,32},{96,0},{1,97},{33,65},{65,33},{97,1},{2,98}... | collective-permute-start | bytes 331784 | tf_op jit(solution)/shard_map/plane_sum/ppermute | solution.py:322
  146.4 8.2 %collective-permute-start.17 = (f32[1,144,1536]{2,1,0:T(8,128)}, f32[1,144,1536]{2,1,0:T(8,128)}, u32[]{:S(2)}, u32[]{:S(2)}) collective-permute-start(f32[1,144,1536]{2,1,0:T(8,128)} %get-tuple-element.91), channel_id=1, source_target_pairs={{0,1},{1,0},{2,3},{3,2},{4,5},{5,4},{6,7},{7,6},{8,9},{9,8},{10,11... | collective-permute-start | bytes 2654216 | tf_op jit(solution)/shard_map/swap_a/ppermute | solution.py:327
  154.6 16.8 %slice-start = ((s8[6553600]{0:T(1024)(128)(4,1)}), s8[4194304]{0:T(1024)(128)(4,1)S(1)}, s32[]{:S(2)}) async-start(s8[6553600]{0:T(1024)(128)(4,1)} %bitcast.75), calls=%async_computation.2 | async-start | bytes 8388608
  174.9 7.6 %collective-permute-start.18 = (bf16[48,2560]{1,0:T(8,128)(2,1)S(1)}, bf16[48,2560]{1,0:T(8,128)(2,1)S(1)}, u32[]{:S(2)}, u32[]{:S(2)}) collective-permute-start(bf16[48,2560]{1,0:T(8,128)(2,1)S(1)} %get-tuple-element.98), channel_id=1, source_target_pairs={{0,6},{2,0},{4,2},{6,4},{1,7},{3,1},{5,3},{7,5},{8,14},{10,8},{12,... | collective-permute-start | bytes 737288 | tf_op jit(solution)/shard_map/sum_y/ppermute | solution.py:317
  174.9 8.6 %collective-permute-start.19 = (bf16[48,2560]{1,0:T(8,128)(2,1)S(1)}, bf16[48,2560]{1,0:T(8,128)(2,1)S(1)}, u32[]{:S(2)}, u32[]{:S(2)}) collective-permute-start(bf16[48,2560]{1,0:T(8,128)(2,1)S(1)} %get-tuple-element.99), channel_id=1, source_target_pairs={{0,2},{2,4},{4,6},{6,0},{1,3},{3,5},{5,7},{7,1},{8,10},{10,12},{12... | collective-permute-start | bytes 737288 | tf_op jit(solution)/shard_map/sum_y/ppermute | solution.py:317
  180.4 7.1 %collective-permute-start.20 = (bf16[48,2560]{1,0:T(8,128)(2,1)S(1)}, bf16[48,2560]{1,0:T(8,128)(2,1)S(1)}, u32[]{:S(2)}, u32[]{:S(2)}) collective-permute-start(bf16[48,2560]{1,0:T(8,128)(2,1)S(1)} %get-tuple-element.101), channel_id=1, source_target_pairs={{0,6},{2,0},{4,2},{6,4},{1,7},{3,1},{5,3},{7,5},{8,14},{10,8},{12,... | collective-permute-start | bytes 737288 | tf_op jit(solution)/shard_map/sum_y/ppermute | solution.py:317
  181.7 7.9 %collective-permute-start.21 = (bf16[48,2560]{1,0:T(8,128)(2,1)S(1)}, bf16[48,2560]{1,0:T(8,128)(2,1)S(1)}, u32[]{:S(2)}, u32[]{:S(2)}) collective-permute-start(bf16[48,2560]{1,0:T(8,128)(2,1)S(1)} %get-tuple-element.102), channel_id=1, source_target_pairs={{0,2},{2,4},{4,6},{6,0},{1,3},{3,5},{5,7},{7,1},{8,10},{10,12},{12... | collective-permute-start | bytes 737288 | tf_op jit(solution)/shard_map/sum_y/ppermute | solution.py:317
  (5 other events, 52.9 us)

commit v4 on v3

--- a/solution.py
+++ b/solution.py
@@ -232,6 +232,7 @@
         pieces = [
             held[i, :, head * HS : (head + 1) * HS].astype(jnp.float32)[z * piece : (z + 1) * piece] for i in range(count)
         ]
+        pieces.append(jnp.zeros((chunks.shape[1] - at - count * piece, HS), jnp.float32))
         chunks[target, at:, :] = jnp.concatenate(pieces, axis=0).astype(jnp.bfloat16)
         leaving.append(pltpu.make_async_copy(chunks.at[target], out_ref.at[target], leave.at[target]))
         leaving[-1].start()
@@ -241,6 +242,7 @@
 
 def outgoing(name, *arrays):
     rows = len(arrays) * arrays[0].shape[0] * 5 // 4
+    rows += -rows % 16
     return pl.pallas_call(
         outgoing_kernel,
         name=name,
@@ -384,7 +386,7 @@
     ring_q = sent[:, two:three].reshape(-1, HS)
     plane_kv = jnp.concatenate([sent[:, three : three + piece], sent[:, three + piece : three + 2 * piece]], axis=0)
     plane_kv = plane_kv.reshape(-1, HS)
-    plane_q = sent[:, three + 2 * piece :].reshape(-1, HS)
+    plane_q = sent[:, three + 2 * piece : three + 3 * piece].reshape(-1, HS)
     ring_rows = 16 * token_rows
     plane_rows = 16 * piece
 
@@ -411,11 +413,10 @@
         ring(ring_left[:middle], "x", 4, 1, "ring_x_far"),
         ring(ring_right[middle:], "x", 4, -1, "ring_x_far"),
     ]
-    state = attention("left", query_a, ring_masks[:, 48:96], 32, [ring_left], whole, state)
-    own_part, other_b, state = lax.optimization_barrier((plane_state[0], other_b, state))
-    plane_part = fold(own_part, other_b, plane_rows)
+    plane_part = fold(plane_state[0], other_b, plane_rows)
     plane_part, state = lax.optimization_barrier((plane_part, state))
     plane_part = [plane_part[0]] + [cross(plane_part[i], "x", i, "plane_sum") for i in (1, 2, 3)]
+    state = attention("left", query_a, ring_masks[:, 48:96], 32, [ring_left], whole, state)
     state = attention("right", query_a, ring_masks[:, 96:144], 32, [ring_right], whole, state)
     out_b = merge("merge_plane", *plane_part).reshape(4, 2, 2, piece, HS)
     out_b, state = lax.optimization_barrier((out_b, state))

time: 191 us -> 192 us (level)
  no operation moved by 1% of the time
where the time goes in v4:
time: 192 us; the launch traced here: 191 us
  Pallas kernels  107 us (56%)
  waiting for transfers between devices  32.6 us (17%)
  starting transfers between devices  31.6 us (16%)
  blocking collectives  14.8 us (8%)
  local copies, waits for them, and re-layouts  2.18 us (1%)
  other arithmetic  2.15 us (1%)
    pallas_call x6, Pallas kernels, attention(): pl.pallas_call(functools.partial(attention_kernel, first=first, count=len...  94.9 us
    all_to_all x1, waiting for transfers between devices, local(): lax.all_to_all(outgoing('outgoing', keys, values, queries), RING, 0, 0)  22.2 us
    all_to_all x1, blocking collectives, local(): back = lax.all_to_all(back, ('z', 'yh'), 0, 0)  14.8 us
    ppermute x9, starting transfers between devices, cross(): return lax.ppermute(array, axis, [(i, i ^ bit) for i in range(4)])  12.6 us
    ppermute x8, starting transfers between devices, ring(): lax.ppermute(array, axes, [(i, (i + shift) % size) for i in range(size)])  10.5 us
    all_to_all x1, starting transfers between devices, local(): lax.all_to_all(outgoing('outgoing', keys, values, queries), RING, 0, 0)  8.28 us
    ppermute x8, waiting for transfers between devices, ring(): lax.ppermute(array, axes, [(i, (i + shift) % size) for i in range(size)])  7.07 us
    pallas_call x2, Pallas kernels, project(): pl.pallas_call(functools.partial(project_kernel, start=start), name='proj...  6.82 us
  transfers between devices with their start and end apart: 23, of which 7 were waited for; matrix products, arithmetic and copies ran while one was open for 2% of the time, Pallas kernels for 49%

profile of v4, /device:TPU:0, one launch (start us, length us, event | category | flops | bytes accessed | tf_op | source)
XLA Modules:
  0.0 191.4 jit_solution(4015217831873764064)
XLA Ops:
  0.0 2.9 %outgoing.1 = bf16[16,368,128]{2,1,0:T(8,128)(2,1)} custom-call(bf16[96,2560]{1,0:T(8,128)(2,1)} %refs_0_.1, bf16[96,2560]{1,0:T(8,128)(2,1)} %refs_1_.1, bf16[96,2560]{1,0:T(8,128)(2,1)} %refs_2_.1), custom_call_target="tpu_custom_call" | custom-call | flops 1024 | bytes 1024 | tf_op jit(solution)/shard_map/spread/outgoing/pallas_call | solution.py:246
  3.0 8.3 %all-to-all-start = ((bf16[16,368,128]{2,1,0:T(8,128)(2,1)}), bf16[16,368,128]{2,1,0:T(8,128)(2,1)S(1)}, u32[]{:S(2)}, u32[]{:S(2)}) async-start(bf16[16,368,128]{2,1,0:T(8,128)(2,1)} %outgoing.1), calls=%async_computation | async-start | bytes 3014656 | tf_op jit(solution)/shard_map/spread/all_to_all | solution.py:383
  14.6 22.2 %all-to-all-done = bf16[16,368,128]{2,1,0:T(8,128)(2,1)S(1)} async-done(((bf16[16,368,128]{2,1,0:T(8,128)(2,1)}), bf16[16,368,128]{2,1,0:T(8,128)(2,1)S(1)}, u32[]{:S(2)}, u32[]{:S(2)}) %all-to-all-start) | async-done | bytes 1507360 | tf_op jit(solution)/shard_map/spread/all_to_all | solution.py:383
  37.0 1.6 collective-permute-start.2
  38.6 2.7 %collective-permute-start.3 = (bf16[384,128]{1,0:T(8,128)(2,1)S(1)}, bf16[384,128]{1,0:T(8,128)(2,1)S(1)}, u32[]{:S(2)}, u32[]{:S(2)}) collective-permute-start(bf16[384,128]{1,0:T(8,128)(2,1)S(1)} %bitcast.94), channel_id=1, source_target_pairs={{0,64},{32,96},{64,0},{96,32},{1,65},{33,97},{65,1},{97,33},{2,66}... | collective-permute-start | bytes 294920 | tf_op jit(solution)/shard_map/plane_q/ppermute | solution.py:324
  41.8 2.8 %collective-permute-start.10 = (bf16[3072,128]{1,0:T(8,128)(2,1)S(1)}, bf16[3072,128]{1,0:T(8,128)(2,1)S(1)}, u32[]{:S(2)}, u32[]{:S(2)}) collective-permute-start(bf16[3072,128]{1,0:T(8,128)(2,1)S(1)} %bitcast.77), channel_id=1, source_target_pairs={{0,96},{32,0},{64,32},{96,64},{1,97},{33,1},{65,33},{97,65},{2,98}... | collective-permute-start | bytes 2359304 | tf_op jit(solution)/shard_map/ring_x/ppermute | solution.py:319
  49.5 1.7 collective-permute-start.8
  51.3 15.2 %own.1 = (f32[2,144,1536]{2,1,0:T(8,128)S(1)}, f32[2,8,128]{2,1,0:T(8,128)S(1)}) custom-call(bf16[2,1536,128]{2,1,0:T(8,128)(2,1)S(1)} %pad_maximum_fusion.2.refs_0_, f32[2,48,128]{2,1,0:T(8,128)S(1)} %get-tuple-element.105.refs_1_, bf16[3072,128]{1,0:T(8,128)(2,1)S(1)} %bitcast.79), custom_call_target="tpu_custom_call" | custom-call | flops 1024 | bytes 1024 | tf_op jit(solution)/shard_map/own/pallas_call | solution.py:119
  66.5 32.8 %plane.1 = (f32[4,144,768]{2,1,0:T(8,128)S(1)}, f32[4,8,128]{2,1,0:T(8,128)}) custom-call(bf16[4,768,128]{2,1,0:T(8,128)(2,1)S(1)} %bitcast.85, f32[4,192,128]{2,1,0:T(8,128)S(1)} %fusion.refs_1_, bf16[768,128]{1,0:T(8,128)(2,1)S(1)} %bitcast.89, bf16[768,128]{1,0:T(8,128)(2,1)S(1)} %collective-permute-done.6.refs_3_, ...), custom_call_target="tpu_custom_call" | custom-call | flops 1024 | bytes 1024 | tf_op jit(solution)/shard_map/plane/pallas_call | solution.py:119
  99.9 3.2 %collective-permute-start.12 = (bf16[1536,128]{1,0:T(8,128)(2,1)S(1)}, bf16[1536,128]{1,0:T(8,128)(2,1)S(1)}, u32[]{:S(2)}, u32[]{:S(2)}) collective-permute-start(bf16[1536,128]{1,0:T(8,128)(2,1)S(1)} %slice.100), channel_id=1, source_target_pairs={{0,96},{32,0},{64,32},{96,64},{1,97},{33,1},{65,33},{97,65},{2,98}... | collective-permute-start | bytes 1179656 | tf_op jit(solution)/shard_map/ring_x_far/ppermute | solution.py:319
  103.4 2.0 %collective-permute-start.15 = (bf16[1,144,384]{2,1,0:T(8,128)(2,1)S(1)}, bf16[1,144,384]{2,1,0:T(8,128)(2,1)S(1)}, u32[]{:S(2)}, u32[]{:S(2)}) collective-permute-start(bf16[1,144,384]{2,1,0:T(8,128)(2,1)S(1)} %get-tuple-element.73), channel_id=1, source_target_pairs={{0,64},{32,96},{64,0},{96,32},{1,65},{33,97},{65,1},{97,33},{2,66}... | collective-permute-start | bytes 331784 | tf_op jit(solution)/shard_map/plane_sum/ppermute | solution.py:324
  105.4 2.7 %collective-permute-start.16 = (bf16[1,144,384]{2,1,0:T(8,128)(2,1)S(1)}, bf16[1,144,384]{2,1,0:T(8,128)(2,1)S(1)}, u32[]{:S(2)}, u32[]{:S(2)}) collective-permute-start(bf16[1,144,384]{2,1,0:T(8,128)(2,1)S(1)} %get-tuple-element.74), channel_id=1, source_target_pairs={{0,96},{32,64},{64,32},{96,0},{1,97},{33,65},{65,33},{97,1},{2,98}... | collective-permute-start | bytes 331784 | tf_op jit(solution)/shard_map/plane_sum/ppermute | solution.py:324
  108.1 15.1 %left.1 = (f32[2,144,1536]{2,1,0:T(8,128)S(1)}, f32[2,8,128]{2,1,0:T(8,128)S(1)}) custom-call(bf16[2,1536,128]{2,1,0:T(8,128)(2,1)S(1)} %pad_maximum_fusion.2.refs_0_, f32[2,48,128]{2,1,0:T(8,128)S(1)} %get-tuple-element.103.refs_1_, bf16[3072,128]{1,0:T(8,128)(2,1)S(1)} %collective-permute-done.9.refs_2_, f32[2,8,128]{2,1,0:T(8,128)S(1)} %get-tuple-element.75.refs_3_, ...), custom_call_target="tpu_custom_call" | custom-call | flops 1024 | bytes 1024 | tf_op jit(solution)/shard_map/left/pallas_call | solution.py:119
  123.2 15.1 %right.1 = (f32[2,144,1536]{2,1,0:T(8,128)S(1)}, f32[2,8,128]{2,1,0:T(8,128)S(1)}) custom-call(bf16[2,1536,128]{2,1,0:T(8,128)(2,1)S(1)} %pad_maximum_fusion.2.refs_0_, f32[2,48,128]{2,1,0:T(8,128)S(1)} %get-tuple-element.104.refs_1_, bf16[3072,128]{1,0:T(8,128)(2,1)S(1)} %collective-permute-done.10.refs_2_, f32[2,8,128]{2,1,0:T(8,128)S(1)} %get-tuple-element.77.refs_3_, ...), custom_call_target="tpu_custom_call" | custom-call | flops 1024 | bytes 1024 | tf_op jit(solution)/shard_map/right/pallas_call | solution.py:119
  138.6 8.5 %far_side.1 = (f32[1,144,1536]{2,1,0:T(8,128)}, f32[1,8,128]{2,1,0:T(8,128)}) custom-call(bf16[2,1536,128]{2,1,0:T(8,128)(2,1)S(1)} %pad_maximum_fusion.2.refs_0_, f32[2,48,128]{2,1,0:T(8,128)S(1)} %get-tuple-element.106.refs_1_, bf16[1536,128]{1,0:T(8,128)(2,1)S(1)} %collective-permute-done.11.refs_2_, ...), custom_call_target="tpu_custom_call" | custom-call | flops 1024 | bytes 1024 | tf_op jit(solution)/shard_map/far_side/pallas_call | solution.py:119
  147.1 8.1 %far_own.1 = (f32[1,144,1536]{2,1,0:T(8,128)S(1)}, f32[1,8,128]{2,1,0:T(8,128)}) custom-call(bf16[2,1536,128]{2,1,0:T(8,128)(2,1)S(1)} %pad_maximum_fusion.2.refs_0_, f32[2,48,128]{2,1,0:T(8,128)S(1)} %get-tuple-element.106.refs_1_, bf16[1536,128]{1,0:T(8,128)(2,1)S(1)} %collective-permute-done.11.refs_2_, ...), custom_call_target="tpu_custom_call" | custom-call | flops 1024 | bytes 1024 | tf_op jit(solution)/shard_map/far_own/pallas_call | solution.py:119
  155.3 1.5 merge_ring.1
  157.1 14.8 %all_to_all.10 = bf16[8,240,128]{2,1,0:T(8,128)(2,1)S(1)} all-to-all(bf16[8,240,128]{2,1,0:T(8,128)(2,1)S(1)} %bitcast.92), channel_id=1, replica_groups=mesh['x'=4,'z'=4,'yh'=2,'yl'=2,'c'=2] {'z','yh'}, dimensions={0} | all-to-all | bytes 983040 | tf_op jit(solution)/shard_map/return/all_to_all | solution.py:447
  172.1 3.4 %project.2 = (bf16[96,2560]{1,0:T(8,128)(2,1)S(1)}, bf16[48,2560]{1,0:T(8,128)(2,1)S(1)}, bf16[48,2560]{1,0:T(8,128)(2,1)S(1)}) custom-call(s32[1]{0:T(128)} %bitcast.core_ref, bf16[10,192,128]{2,1,0:T(8,128)(2,1)S(1)} %pad_maximum_fusion.3.att_ref, bf16[640,5120]{1,0:T(8,128)(2,1)S(1)} %bitcast.76, bf16[640,5120]{1,0:T(8,128)(2,1)} %collective-permute-done.side_w), custom_call_target="tpu_custom_call" | custom-call | flops 1024 | bytes 1024 | tf_op jit(solution)/shard_map/project/pallas_call | solution.py:294
  175.6 2.0 %collective-permute-start.19 = (bf16[48,2560]{1,0:T(8,128)(2,1)S(1)}, bf16[48,2560]{1,0:T(8,128)(2,1)S(1)}, u32[]{:S(2)}, u32[]{:S(2)}) collective-permute-start(bf16[48,2560]{1,0:T(8,128)(2,1)S(1)} %get-tuple-element.91), channel_id=1, source_target_pairs={{0,2},{2,4},{4,6},{6,0},{1,3},{3,5},{5,7},{7,1},{8,10},{10,12},{12... | collective-permute-start | bytes 737288 | tf_op jit(solution)/shard_map/sum_y/ppermute | solution.py:319
  177.6 3.4 %project.3 = (bf16[96,2560]{1,0:T(8,128)(2,1)S(1)}, bf16[48,2560]{1,0:T(8,128)(2,1)S(1)}, bf16[48,2560]{1,0:T(8,128)(2,1)S(1)}) custom-call(s32[1]{0:T(128)} %bitcast.core_ref, bf16[10,192,128]{2,1,0:T(8,128)(2,1)S(1)} %pad_maximum_fusion.3.att_ref, bf16[640,5120]{1,0:T(8,128)(2,1)S(1)} %bitcast.76, bf16[640,5120]{1,0:T(8,128)(2,1)} %collective-permute-done.side_w), custom_call_target="tpu_custom_call" | custom-call | flops 1024 | bytes 1024 | tf_op jit(solution)/shard_map/project/pallas_call | solution.py:294
  181.0 1.4 collective-permute-start.20
  184.2 3.9 %collective-permute-done.20 = bf16[48,2560]{1,0:T(8,128)(2,1)S(1)} collective-permute-done((bf16[48,2560]{1,0:T(8,128)(2,1)S(1)}, bf16[48,2560]{1,0:T(8,128)(2,1)S(1)}, u32[]{:S(2)}, u32[]{:S(2)}) %collective-permute-start.20) | collective-permute-done | bytes 245792 | tf_op jit(solution)/shard_map/sum_y/ppermute | solution.py:319
  188.1 2.2 %collective-permute-done.21 = bf16[48,2560]{1,0:T(8,128)(2,1)S(1)} collective-permute-done((bf16[48,2560]{1,0:T(8,128)(2,1)S(1)}, bf16[48,2560]{1,0:T(8,128)(2,1)S(1)}, u32[]{:S(2)}, u32[]{:S(2)}) %collective-permute-start.21) | collective-permute-done | bytes 245792 | tf_op jit(solution)/shard_map/sum_y/ppermute | solution.py:319
  (109 shorter events, 13.3 us)
Async XLA Ops:
  0.0 37.0 %collective-permute-start = (bf16[640,5120]{1,0:T(8,128)(2,1)}, bf16[640,5120]{1,0:T(8,128)(2,1)}, u32[]{:S(2)}, u32[]{:S(2)}) collective-permute-start(bf16[640,5120]{1,0:T(8,128)(2,1)} %own_w.3), channel_id=1, source_target_pairs={{0,1},{1,0},{2,3},{3,2},{4,5},{5,4},{6,7},{7,6},{8,9},{9,8},{10,11... | collective-permute-start | bytes 19660808 | tf_op jit(solution)/shard_map/side_w/ppermute | solution.py:329
  3.0 33.8 %all-to-all-start = ((bf16[16,368,128]{2,1,0:T(8,128)(2,1)}), bf16[16,368,128]{2,1,0:T(8,128)(2,1)S(1)}, u32[]{:S(2)}, u32[]{:S(2)}) async-start(bf16[16,368,128]{2,1,0:T(8,128)(2,1)} %outgoing.1), calls=%async_computation | async-start | bytes 3014656 | tf_op jit(solution)/shard_map/spread/all_to_all | solution.py:383
  37.0 7.6 %collective-permute-start.2 = (bf16[384,128]{1,0:T(8,128)(2,1)S(1)}, bf16[384,128]{1,0:T(8,128)(2,1)S(1)}, u32[]{:S(2)}, u32[]{:S(2)}) collective-permute-start(bf16[384,128]{1,0:T(8,128)(2,1)S(1)} %bitcast.93), channel_id=1, source_target_pairs={{0,32},{32,0},{64,96},{96,64},{1,33},{33,1},{65,97},{97,65},{2,34}... | collective-permute-start | bytes 294920 | tf_op jit(solution)/shard_map/plane_q/ppermute | solution.py:324
  38.6 7.2 %collective-permute-start.3 = (bf16[384,128]{1,0:T(8,128)(2,1)S(1)}, bf16[384,128]{1,0:T(8,128)(2,1)S(1)}, u32[]{:S(2)}, u32[]{:S(2)}) collective-permute-start(bf16[384,128]{1,0:T(8,128)(2,1)S(1)} %bitcast.94), channel_id=1, source_target_pairs={{0,64},{32,96},{64,0},{96,32},{1,65},{33,97},{65,1},{97,33},{2,66}... | collective-permute-start | bytes 294920 | tf_op jit(solution)/shard_map/plane_q/ppermute | solution.py:324
  41.3 6.4 %collective-permute-start.4 = (bf16[384,128]{1,0:T(8,128)(2,1)S(1)}, bf16[384,128]{1,0:T(8,128)(2,1)S(1)}, u32[]{:S(2)}, u32[]{:S(2)}) collective-permute-start(bf16[384,128]{1,0:T(8,128)(2,1)S(1)} %bitcast.95), channel_id=1, source_target_pairs={{0,96},{32,64},{64,32},{96,0},{1,97},{33,65},{65,33},{97,1},{2,98}... | collective-permute-start | bytes 294920 | tf_op jit(solution)/shard_map/plane_q/ppermute | solution.py:324
  41.8 57.5 %collective-permute-start.10 = (bf16[3072,128]{1,0:T(8,128)(2,1)S(1)}, bf16[3072,128]{1,0:T(8,128)(2,1)S(1)}, u32[]{:S(2)}, u32[]{:S(2)}) collective-permute-start(bf16[3072,128]{1,0:T(8,128)(2,1)S(1)} %bitcast.77), channel_id=1, source_target_pairs={{0,96},{32,0},{64,32},{96,64},{1,97},{33,1},{65,33},{97,65},{2,98}... | collective-permute-start | bytes 2359304 | tf_op jit(solution)/shard_map/ring_x/ppermute | solution.py:319
  44.6 54.8 %collective-permute-start.9 = (bf16[3072,128]{1,0:T(8,128)(2,1)S(1)}, bf16[3072,128]{1,0:T(8,128)(2,1)S(1)}, u32[]{:S(2)}, u32[]{:S(2)}) collective-permute-start(bf16[3072,128]{1,0:T(8,128)(2,1)S(1)} %bitcast.78), channel_id=1, source_target_pairs={{0,32},{32,64},{64,96},{96,0},{1,33},{33,65},{65,97},{97,1},{2,34}... | collective-permute-start | bytes 2359304 | tf_op jit(solution)/shard_map/ring_x/ppermute | solution.py:319
  44.6 3.3 %collective-permute-start.1 = (bf16[1536,128]{1,0:T(8,128)(2,1)S(1)}, bf16[1536,128]{1,0:T(8,128)(2,1)S(1)}, u32[]{:S(2)}, u32[]{:S(2)}) collective-permute-start(bf16[1536,128]{1,0:T(8,128)(2,1)S(1)} %bitcast.90), channel_id=1, source_target_pairs={{0,1},{1,0},{2,3},{3,2},{4,5},{5,4},{6,7},{7,6},{8,9},{9,8},{10,11... | collective-permute-start | bytes 1179656 | tf_op jit(solution)/shard_map/swap_q/ppermute | solution.py:329
  45.8 20.7 %collective-permute-start.6 = (bf16[768,128]{1,0:T(8,128)(2,1)S(1)}, bf16[768,128]{1,0:T(8,128)(2,1)S(1)}, u32[]{:S(2)}, u32[]{:S(2)}) collective-permute-start(bf16[768,128]{1,0:T(8,128)(2,1)S(1)} %bitcast.86), channel_id=1, source_target_pairs={{0,16},{8,24},{16,0},{24,8},{1,17},{9,25},{17,1},{25,9},{2,18},{10... | collective-permute-start | bytes 589832 | tf_op jit(solution)/shard_map/plane_z/ppermute | solution.py:324
  47.7 1.8 collective-permute-start.5
  47.9 18.6 %collective-permute-start.7 = (bf16[768,128]{1,0:T(8,128)(2,1)S(1)}, bf16[768,128]{1,0:T(8,128)(2,1)S(1)}, u32[]{:S(2)}, u32[]{:S(2)}) collective-permute-start(bf16[768,128]{1,0:T(8,128)(2,1)S(1)} %bitcast.87), channel_id=1, source_target_pairs={{0,8},{8,0},{16,24},{24,16},{1,9},{9,1},{17,25},{25,17},{2,10},{10... | collective-permute-start | bytes 589832 | tf_op jit(solution)/shard_map/plane_z/ppermute | solution.py:324
  49.5 16.9 %collective-permute-start.8 = (bf16[768,128]{1,0:T(8,128)(2,1)S(1)}, bf16[768,128]{1,0:T(8,128)(2,1)S(1)}, u32[]{:S(2)}, u32[]{:S(2)}) collective-permute-start(bf16[768,128]{1,0:T(8,128)(2,1)S(1)} %bitcast.88), channel_id=1, source_target_pairs={{0,24},{8,16},{16,8},{24,0},{1,25},{9,17},{17,9},{25,1},{2,26},{10... | collective-permute-start | bytes 589832 | tf_op jit(solution)/shard_map/plane_z/ppermute | solution.py:324
  99.4 3.7 %collective-permute-start.13 = (f32[2,144,768]{2,1,0:T(8,128)S(1)}, f32[2,144,768]{2,1,0:T(8,128)S(1)}, u32[]{:S(2)}, u32[]{:S(2)}) collective-permute-start(f32[2,144,768]{2,1,0:T(8,128)S(1)} %slice.101), channel_id=1, source_target_pairs={{0,1},{1,0},{2,3},{3,2},{4,5},{5,4},{6,7},{7,6},{8,9},{9,8},{10,11... | collective-permute-start | bytes 2654216 | tf_op jit(solution)/shard_map/swap_b/ppermute | solution.py:329
  99.5 39.0 %collective-permute-start.11 = (bf16[1536,128]{1,0:T(8,128)(2,1)S(1)}, bf16[1536,128]{1,0:T(8,128)(2,1)S(1)}, u32[]{:S(2)}, u32[]{:S(2)}) collective-permute-start(bf16[1536,128]{1,0:T(8,128)(2,1)S(1)} %slice.99), channel_id=1, source_target_pairs={{0,32},{32,64},{64,96},{96,0},{1,33},{33,65},{65,97},{97,1},{2,34}... | collective-permute-start | bytes 1179656 | tf_op jit(solution)/shard_map/ring_x_far/ppermute | solution.py:319
  99.9 38.6 %collective-permute-start.12 = (bf16[1536,128]{1,0:T(8,128)(2,1)S(1)}, bf16[1536,128]{1,0:T(8,128)(2,1)S(1)}, u32[]{:S(2)}, u32[]{:S(2)}) collective-permute-start(bf16[1536,128]{1,0:T(8,128)(2,1)S(1)} %slice.100), channel_id=1, source_target_pairs={{0,96},{32,0},{64,32},{96,64},{1,97},{33,1},{65,33},{97,65},{2,98}... | collective-permute-start | bytes 1179656 | tf_op jit(solution)/shard_map/ring_x_far/ppermute | solution.py:319
  103.3 35.0 %collective-permute-start.14 = (bf16[1,144,384]{2,1,0:T(8,128)(2,1)S(1)}, bf16[1,144,384]{2,1,0:T(8,128)(2,1)S(1)}, u32[]{:S(2)}, u32[]{:S(2)}) collective-permute-start(bf16[1,144,384]{2,1,0:T(8,128)(2,1)S(1)} %get-tuple-element.72), channel_id=1, source_target_pairs={{0,32},{32,0},{64,96},{96,64},{1,33},{33,1},{65,97},{97,65},{2,34}... | collective-permute-start | bytes 331784 | tf_op jit(solution)/shard_map/plane_sum/ppermute | solution.py:324
  103.4 34.9 %collective-permute-start.15 = (bf16[1,144,384]{2,1,0:T(8,128)(2,1)S(1)}, bf16[1,144,384]{2,1,0:T(8,128)(2,1)S(1)}, u32[]{:S(2)}, u32[]{:S(2)}) collective-permute-start(bf16[1,144,384]{2,1,0:T(8,128)(2,1)S(1)} %get-tuple-element.73), channel_id=1, source_target_pairs={{0,64},{32,96},{64,0},{96,32},{1,65},{33,97},{65,1},{97,33},{2,66}... | collective-permute-start | bytes 331784 | tf_op jit(solution)/shard_map/plane_sum/ppermute | solution.py:324
  105.4 33.0 %collective-permute-start.16 = (bf16[1,144,384]{2,1,0:T(8,128)(2,1)S(1)}, bf16[1,144,384]{2,1,0:T(8,128)(2,1)S(1)}, u32[]{:S(2)}, u32[]{:S(2)}) collective-permute-start(bf16[1,144,384]{2,1,0:T(8,128)(2,1)S(1)} %get-tuple-element.74), channel_id=1, source_target_pairs={{0,96},{32,64},{64,32},{96,0},{1,97},{33,65},{65,33},{97,1},{2,98}... | collective-permute-start | bytes 331784 | tf_op jit(solution)/shard_map/plane_sum/ppermute | solution.py:324
  147.1 8.2 %collective-permute-start.17 = (f32[1,144,1536]{2,1,0:T(8,128)}, f32[1,144,1536]{2,1,0:T(8,128)}, u32[]{:S(2)}, u32[]{:S(2)}) collective-permute-start(f32[1,144,1536]{2,1,0:T(8,128)} %get-tuple-element.83), channel_id=1, source_target_pairs={{0,1},{1,0},{2,3},{3,2},{4,5},{5,4},{6,7},{7,6},{8,9},{9,8},{10,11... | collective-permute-start | bytes 2654216 | tf_op jit(solution)/shard_map/swap_a/ppermute | solution.py:329
  155.3 16.8 %slice-start = ((s8[6553600]{0:T(1024)(128)(4,1)}), s8[4194304]{0:T(1024)(128)(4,1)S(1)}, s32[]{:S(2)}) async-start(s8[6553600]{0:T(1024)(128)(4,1)} %bitcast.75), calls=%async_computation.2 | async-start | bytes 8388608
  175.5 7.6 %collective-permute-start.18 = (bf16[48,2560]{1,0:T(8,128)(2,1)S(1)}, bf16[48,2560]{1,0:T(8,128)(2,1)S(1)}, u32[]{:S(2)}, u32[]{:S(2)}) collective-permute-start(bf16[48,2560]{1,0:T(8,128)(2,1)S(1)} %get-tuple-element.90), channel_id=1, source_target_pairs={{0,6},{2,0},{4,2},{6,4},{1,7},{3,1},{5,3},{7,5},{8,14},{10,8},{12,... | collective-permute-start | bytes 737288 | tf_op jit(solution)/shard_map/sum_y/ppermute | solution.py:319
  175.6 8.5 %collective-permute-start.19 = (bf16[48,2560]{1,0:T(8,128)(2,1)S(1)}, bf16[48,2560]{1,0:T(8,128)(2,1)S(1)}, u32[]{:S(2)}, u32[]{:S(2)}) collective-permute-start(bf16[48,2560]{1,0:T(8,128)(2,1)S(1)} %get-tuple-element.91), channel_id=1, source_target_pairs={{0,2},{2,4},{4,6},{6,0},{1,3},{3,5},{5,7},{7,1},{8,10},{10,12},{12... | collective-permute-start | bytes 737288 | tf_op jit(solution)/shard_map/sum_y/ppermute | solution.py:319
  181.0 7.1 %collective-permute-start.20 = (bf16[48,2560]{1,0:T(8,128)(2,1)S(1)}, bf16[48,2560]{1,0:T(8,128)(2,1)S(1)}, u32[]{:S(2)}, u32[]{:S(2)}) collective-permute-start(bf16[48,2560]{1,0:T(8,128)(2,1)S(1)} %get-tuple-element.93), channel_id=1, source_target_pairs={{0,6},{2,0},{4,2},{6,4},{1,7},{3,1},{5,3},{7,5},{8,14},{10,8},{12,... | collective-permute-start | bytes 737288 | tf_op jit(solution)/shard_map/sum_y/ppermute | solution.py:319
  182.4 7.9 %collective-permute-start.21 = (bf16[48,2560]{1,0:T(8,128)(2,1)S(1)}, bf16[48,2560]{1,0:T(8,128)(2,1)S(1)}, u32[]{:S(2)}, u32[]{:S(2)}) collective-permute-start(bf16[48,2560]{1,0:T(8,128)(2,1)S(1)} %get-tuple-element.94), channel_id=1, source_target_pairs={{0,2},{2,4},{4,6},{6,0},{1,3},{3,5},{5,7},{7,1},{8,10},{10,12},{12... | collective-permute-start | bytes 737288 | tf_op jit(solution)/shard_map/sum_y/ppermute | solution.py:319
  (5 other events, 52.9 us)

commit v5 on v4

--- a/solution.py
+++ b/solution.py
@@ -349,7 +349,7 @@
         return (frames(at_x) + within[None]).reshape(-1)
 
     ring_keys = jnp.concatenate([ring_blocks((x + i) % 4, core) for i in NEAR])
-    plane_keys = jnp.concatenate([plane_blocks(x, core, z ^ i) for i in (0, 2, 1, 3)])
+    plane_keys = jnp.concatenate([plane_blocks(x, core, z ^ i) for i in (0, 2, 3, 1)])
     blocks = jnp.arange(block_mask.shape[0], dtype=jnp.int32)
     pad = jnp.zeros((32,), jnp.int32)
     ring_queries, plane_queries = [], []
@@ -396,7 +396,7 @@
     ring_left, ring_right = ring(ring_kv, "x", 4, 1, "ring_x"), ring(ring_kv, "x", 4, -1, "ring_x")
     query_a = jnp.stack([ring_q, swap(ring_q, "swap_q")])
 
-    plane_kv = [plane_kv] + [cross(plane_kv, "z", i, "plane_z") for i in (2, 1, 3)]
+    plane_kv = [plane_kv] + [cross(plane_kv, "z", i, "plane_z") for i in (2, 3, 1)]
     plane_q = jnp.concatenate([plane_q] + [cross(plane_q, "x", i, "plane_q") for i in (1, 2, 3)], axis=0)
     query_b = jnp.concatenate([plane_q, swap(plane_q, "swap_plane_q")], axis=0).reshape(4, 2 * plane_rows, HS)
     query_a, query_b = lax.optimization_barrier((query_a, query_b))

time: 192 us -> 192 us (level)
  transfers between devices with their start and end apart: 23 -> 23, of which waited for: 7 -> 6; matrix products, arithmetic and copies ran while one was open for 2% -> 2% of each run, Pallas kernels for 49% -> 49%
where the time goes in v5:
time: 192 us
  Pallas kernels  107 us (56%)
  waiting for transfers between devices  31.7 us (17%)
  starting transfers between devices  31.4 us (16%)
  blocking collectives  16 us (8%)
  local copies, waits for them, and re-layouts  2.18 us (1%)
  other arithmetic  2.15 us (1%)
    pallas_call x6, Pallas kernels, attention(): pl.pallas_call(functools.partial(attention_kernel, first=first, count=len...  94.9 us
    all_to_all x1, waiting for transfers between devices, local(): lax.all_to_all(outgoing('outgoing', keys, values, queries), RING, 0, 0)  22.2 us
    all_to_all x1, blocking collectives, local(): back = lax.all_to_all(back, ('z', 'yh'), 0, 0)  16 us
    ppermute x9, starting transfers between devices, cross(): return lax.ppermute(array, axis, [(i, i ^ bit) for i in range(4)])  12.4 us
    ppermute x8, starting transfers between devices, ring(): lax.ppermute(array, axes, [(i, (i + shift) % size) for i in range(size)])  10.5 us
    all_to_all x1, starting transfers between devices, local(): lax.all_to_all(outgoing('outgoing', keys, values, queries), RING, 0, 0)  8.28 us
    ppermute x8, waiting for transfers between devices, ring(): lax.ppermute(array, axes, [(i, (i + shift) % size) for i in range(size)])  7.07 us
    pallas_call x2, Pallas kernels, project(): pl.pallas_call(functools.partial(project_kernel, start=start), name='proj...  6.82 us
  transfers between devices with their start and end apart: 23, of which 6 were waited for; matrix products, arithmetic and copies ran while one was open for 2% of the time, Pallas kernels for 49%

profile of v5, /device:TPU:0, one launch (start us, length us, event | category | flops | bytes accessed | tf_op | source)
XLA Modules:
  0.0 191.6 jit_solution(3381933154608514858)
XLA Ops:
  0.0 2.9 %outgoing.1 = bf16[16,368,128]{2,1,0:T(8,128)(2,1)} custom-call(bf16[96,2560]{1,0:T(8,128)(2,1)} %refs_0_.1, bf16[96,2560]{1,0:T(8,128)(2,1)} %refs_1_.1, bf16[96,2560]{1,0:T(8,128)(2,1)} %refs_2_.1), custom_call_target="tpu_custom_call" | custom-call | flops 1024 | bytes 1024 | tf_op jit(solution)/shard_map/spread/outgoing/pallas_call | solution.py:246
  3.0 8.3 %all-to-all-start = ((bf16[16,368,128]{2,1,0:T(8,128)(2,1)}), bf16[16,368,128]{2,1,0:T(8,128)(2,1)S(1)}, u32[]{:S(2)}, u32[]{:S(2)}) async-start(bf16[16,368,128]{2,1,0:T(8,128)(2,1)} %outgoing.1), calls=%async_computation | async-start | bytes 3014656 | tf_op jit(solution)/shard_map/spread/all_to_all | solution.py:383
  14.6 22.2 %all-to-all-done = bf16[16,368,128]{2,1,0:T(8,128)(2,1)S(1)} async-done(((bf16[16,368,128]{2,1,0:T(8,128)(2,1)}), bf16[16,368,128]{2,1,0:T(8,128)(2,1)S(1)}, u32[]{:S(2)}, u32[]{:S(2)}) %all-to-all-start) | async-done | bytes 1507360 | tf_op jit(solution)/shard_map/spread/all_to_all | solution.py:383
  37.0 1.6 collective-permute-start.2
  38.6 2.7 %collective-permute-start.3 = (bf16[384,128]{1,0:T(8,128)(2,1)S(1)}, bf16[384,128]{1,0:T(8,128)(2,1)S(1)}, u32[]{:S(2)}, u32[]{:S(2)}) collective-permute-start(bf16[384,128]{1,0:T(8,128)(2,1)S(1)} %bitcast.94), channel_id=1, source_target_pairs={{0,64},{32,96},{64,0},{96,32},{1,65},{33,97},{65,1},{97,33},{2,66}... | collective-permute-start | bytes 294920 | tf_op jit(solution)/shard_map/plane_q/ppermute | solution.py:324
  41.8 2.8 %collective-permute-start.10 = (bf16[3072,128]{1,0:T(8,128)(2,1)S(1)}, bf16[3072,128]{1,0:T(8,128)(2,1)S(1)}, u32[]{:S(2)}, u32[]{:S(2)}) collective-permute-start(bf16[3072,128]{1,0:T(8,128)(2,1)S(1)} %bitcast.77), channel_id=1, source_target_pairs={{0,96},{32,0},{64,32},{96,64},{1,97},{33,1},{65,33},{97,65},{2,98}... | collective-permute-start | bytes 2359304 | tf_op jit(solution)/shard_map/ring_x/ppermute | solution.py:319
  47.9 1.8 collective-permute-start.7
  50.2 15.2 %own.1 = (f32[2,144,1536]{2,1,0:T(8,128)S(1)}, f32[2,8,128]{2,1,0:T(8,128)S(1)}) custom-call(bf16[2,1536,128]{2,1,0:T(8,128)(2,1)S(1)} %pad_maximum_fusion.2.refs_0_, f32[2,48,128]{2,1,0:T(8,128)S(1)} %get-tuple-element.105.refs_1_, bf16[3072,128]{1,0:T(8,128)(2,1)S(1)} %bitcast.79), custom_call_target="tpu_custom_call" | custom-call | flops 1024 | bytes 1024 | tf_op jit(solution)/shard_map/own/pallas_call | solution.py:119
  65.4 32.8 %plane.1 = (f32[4,144,768]{2,1,0:T(8,128)S(1)}, f32[4,8,128]{2,1,0:T(8,128)}) custom-call(bf16[4,768,128]{2,1,0:T(8,128)(2,1)S(1)} %bitcast.85, f32[4,192,128]{2,1,0:T(8,128)S(1)} %fusion.refs_1_, bf16[768,128]{1,0:T(8,128)(2,1)S(1)} %bitcast.89, bf16[768,128]{1,0:T(8,128)(2,1)S(1)} %collective-permute-done.6.refs_3_, ...), custom_call_target="tpu_custom_call" | custom-call | flops 1024 | bytes 1024 | tf_op jit(solution)/shard_map/plane/pallas_call | solution.py:119
  99.4 2.7 %collective-permute-start.12 = (bf16[1536,128]{1,0:T(8,128)(2,1)S(1)}, bf16[1536,128]{1,0:T(8,128)(2,1)S(1)}, u32[]{:S(2)}, u32[]{:S(2)}) collective-permute-start(bf16[1536,128]{1,0:T(8,128)(2,1)S(1)} %slice.100), channel_id=1, source_target_pairs={{0,96},{32,0},{64,32},{96,64},{1,97},{33,1},{65,33},{97,65},{2,98}... | collective-permute-start | bytes 1179656 | tf_op jit(solution)/shard_map/ring_x_far/ppermute | solution.py:319
  102.4 2.5 %collective-permute-start.15 = (bf16[1,144,384]{2,1,0:T(8,128)(2,1)S(1)}, bf16[1,144,384]{2,1,0:T(8,128)(2,1)S(1)}, u32[]{:S(2)}, u32[]{:S(2)}) collective-permute-start(bf16[1,144,384]{2,1,0:T(8,128)(2,1)S(1)} %get-tuple-element.73), channel_id=1, source_target_pairs={{0,64},{32,96},{64,0},{96,32},{1,65},{33,97},{65,1},{97,33},{2,66}... | collective-permute-start | bytes 331784 | tf_op jit(solution)/shard_map/plane_sum/ppermute | solution.py:324
  104.8 2.2 %collective-permute-start.16 = (bf16[1,144,384]{2,1,0:T(8,128)(2,1)S(1)}, bf16[1,144,384]{2,1,0:T(8,128)(2,1)S(1)}, u32[]{:S(2)}, u32[]{:S(2)}) collective-permute-start(bf16[1,144,384]{2,1,0:T(8,128)(2,1)S(1)} %get-tuple-element.74), channel_id=1, source_target_pairs={{0,96},{32,64},{64,32},{96,0},{1,97},{33,65},{65,33},{97,1},{2,98}... | collective-permute-start | bytes 331784 | tf_op jit(solution)/shard_map/plane_sum/ppermute | solution.py:324
  107.0 15.1 %left.1 = (f32[2,144,1536]{2,1,0:T(8,128)S(1)}, f32[2,8,128]{2,1,0:T(8,128)S(1)}) custom-call(bf16[2,1536,128]{2,1,0:T(8,128)(2,1)S(1)} %pad_maximum_fusion.2.refs_0_, f32[2,48,128]{2,1,0:T(8,128)S(1)} %get-tuple-element.103.refs_1_, bf16[3072,128]{1,0:T(8,128)(2,1)S(1)} %collective-permute-done.9.refs_2_, f32[2,8,128]{2,1,0:T(8,128)S(1)} %get-tuple-element.75.refs_3_, ...), custom_call_target="tpu_custom_call" | custom-call | flops 1024 | bytes 1024 | tf_op jit(solution)/shard_map/left/pallas_call | solution.py:119
  122.1 15.1 %right.1 = (f32[2,144,1536]{2,1,0:T(8,128)S(1)}, f32[2,8,128]{2,1,0:T(8,128)S(1)}) custom-call(bf16[2,1536,128]{2,1,0:T(8,128)(2,1)S(1)} %pad_maximum_fusion.2.refs_0_, f32[2,48,128]{2,1,0:T(8,128)S(1)} %get-tuple-element.104.refs_1_, bf16[3072,128]{1,0:T(8,128)(2,1)S(1)} %collective-permute-done.10.refs_2_, f32[2,8,128]{2,1,0:T(8,128)S(1)} %get-tuple-element.77.refs_3_, ...), custom_call_target="tpu_custom_call" | custom-call | flops 1024 | bytes 1024 | tf_op jit(solution)/shard_map/right/pallas_call | solution.py:119
  137.5 8.5 %far_side.1 = (f32[1,144,1536]{2,1,0:T(8,128)}, f32[1,8,128]{2,1,0:T(8,128)}) custom-call(bf16[2,1536,128]{2,1,0:T(8,128)(2,1)S(1)} %pad_maximum_fusion.2.refs_0_, f32[2,48,128]{2,1,0:T(8,128)S(1)} %get-tuple-element.106.refs_1_, bf16[1536,128]{1,0:T(8,128)(2,1)S(1)} %collective-permute-done.11.refs_2_, ...), custom_call_target="tpu_custom_call" | custom-call | flops 1024 | bytes 1024 | tf_op jit(solution)/shard_map/far_side/pallas_call | solution.py:119
  146.1 8.1 %far_own.1 = (f32[1,144,1536]{2,1,0:T(8,128)S(1)}, f32[1,8,128]{2,1,0:T(8,128)}) custom-call(bf16[2,1536,128]{2,1,0:T(8,128)(2,1)S(1)} %pad_maximum_fusion.2.refs_0_, f32[2,48,128]{2,1,0:T(8,128)S(1)} %get-tuple-element.106.refs_1_, bf16[1536,128]{1,0:T(8,128)(2,1)S(1)} %collective-permute-done.11.refs_2_, ...), custom_call_target="tpu_custom_call" | custom-call | flops 1024 | bytes 1024 | tf_op jit(solution)/shard_map/far_own/pallas_call | solution.py:119
  154.3 1.5 merge_ring.1
  156.1 16.0 %all_to_all.10 = bf16[8,240,128]{2,1,0:T(8,128)(2,1)S(1)} all-to-all(bf16[8,240,128]{2,1,0:T(8,128)(2,1)S(1)} %bitcast.92), channel_id=1, replica_groups=mesh['x'=4,'z'=4,'yh'=2,'yl'=2,'c'=2] {'z','yh'}, dimensions={0} | all-to-all | bytes 983040 | tf_op jit(solution)/shard_map/return/all_to_all | solution.py:447
  172.3 3.4 %project.2 = (bf16[96,2560]{1,0:T(8,128)(2,1)S(1)}, bf16[48,2560]{1,0:T(8,128)(2,1)S(1)}, bf16[48,2560]{1,0:T(8,128)(2,1)S(1)}) custom-call(s32[1]{0:T(128)} %bitcast.core_ref, bf16[10,192,128]{2,1,0:T(8,128)(2,1)S(1)} %pad_maximum_fusion.3.att_ref, bf16[640,5120]{1,0:T(8,128)(2,1)S(1)} %bitcast.76, bf16[640,5120]{1,0:T(8,128)(2,1)} %collective-permute-done.side_w), custom_call_target="tpu_custom_call" | custom-call | flops 1024 | bytes 1024 | tf_op jit(solution)/shard_map/project/pallas_call | solution.py:294
  175.8 2.0 %collective-permute-start.19 = (bf16[48,2560]{1,0:T(8,128)(2,1)S(1)}, bf16[48,2560]{1,0:T(8,128)(2,1)S(1)}, u32[]{:S(2)}, u32[]{:S(2)}) collective-permute-start(bf16[48,2560]{1,0:T(8,128)(2,1)S(1)} %get-tuple-element.91), channel_id=1, source_target_pairs={{0,2},{2,4},{4,6},{6,0},{1,3},{3,5},{5,7},{7,1},{8,10},{10,12},{12... | collective-permute-start | bytes 737288 | tf_op jit(solution)/shard_map/sum_y/ppermute | solution.py:319
  177.8 3.4 %project.3 = (bf16[96,2560]{1,0:T(8,128)(2,1)S(1)}, bf16[48,2560]{1,0:T(8,128)(2,1)S(1)}, bf16[48,2560]{1,0:T(8,128)(2,1)S(1)}) custom-call(s32[1]{0:T(128)} %bitcast.core_ref, bf16[10,192,128]{2,1,0:T(8,128)(2,1)S(1)} %pad_maximum_fusion.3.att_ref, bf16[640,5120]{1,0:T(8,128)(2,1)S(1)} %bitcast.76, bf16[640,5120]{1,0:T(8,128)(2,1)} %collective-permute-done.side_w), custom_call_target="tpu_custom_call" | custom-call | flops 1024 | bytes 1024 | tf_op jit(solution)/shard_map/project/pallas_call | solution.py:294
  181.2 1.4 collective-permute-start.20
  184.4 3.9 %collective-permute-done.20 = bf16[48,2560]{1,0:T(8,128)(2,1)S(1)} collective-permute-done((bf16[48,2560]{1,0:T(8,128)(2,1)S(1)}, bf16[48,2560]{1,0:T(8,128)(2,1)S(1)}, u32[]{:S(2)}, u32[]{:S(2)}) %collective-permute-start.20) | collective-permute-done | bytes 245792 | tf_op jit(solution)/shard_map/sum_y/ppermute | solution.py:319
  188.3 2.2 %collective-permute-done.21 = bf16[48,2560]{1,0:T(8,128)(2,1)S(1)} collective-permute-done((bf16[48,2560]{1,0:T(8,128)(2,1)S(1)}, bf16[48,2560]{1,0:T(8,128)(2,1)S(1)}, u32[]{:S(2)}, u32[]{:S(2)}) %collective-permute-start.21) | collective-permute-done | bytes 245792 | tf_op jit(solution)/shard_map/sum_y/ppermute | solution.py:319
  (109 shorter events, 12.6 us)
Async XLA Ops:
  0.0 37.0 %collective-permute-start = (bf16[640,5120]{1,0:T(8,128)(2,1)}, bf16[640,5120]{1,0:T(8,128)(2,1)}, u32[]{:S(2)}, u32[]{:S(2)}) collective-permute-start(bf16[640,5120]{1,0:T(8,128)(2,1)} %own_w.3), channel_id=1, source_target_pairs={{0,1},{1,0},{2,3},{3,2},{4,5},{5,4},{6,7},{7,6},{8,9},{9,8},{10,11... | collective-permute-start | bytes 19660808 | tf_op jit(solution)/shard_map/side_w/ppermute | solution.py:329
  3.0 33.8 %all-to-all-start = ((bf16[16,368,128]{2,1,0:T(8,128)(2,1)}), bf16[16,368,128]{2,1,0:T(8,128)(2,1)S(1)}, u32[]{:S(2)}, u32[]{:S(2)}) async-start(bf16[16,368,128]{2,1,0:T(8,128)(2,1)} %outgoing.1), calls=%async_computation | async-start | bytes 3014656 | tf_op jit(solution)/shard_map/spread/all_to_all | solution.py:383
  37.0 7.6 %collective-permute-start.2 = (bf16[384,128]{1,0:T(8,128)(2,1)S(1)}, bf16[384,128]{1,0:T(8,128)(2,1)S(1)}, u32[]{:S(2)}, u32[]{:S(2)}) collective-permute-start(bf16[384,128]{1,0:T(8,128)(2,1)S(1)} %bitcast.93), channel_id=1, source_target_pairs={{0,32},{32,0},{64,96},{96,64},{1,33},{33,1},{65,97},{97,65},{2,34}... | collective-permute-start | bytes 294920 | tf_op jit(solution)/shard_map/plane_q/ppermute | solution.py:324
  38.6 7.2 %collective-permute-start.3 = (bf16[384,128]{1,0:T(8,128)(2,1)S(1)}, bf16[384,128]{1,0:T(8,128)(2,1)S(1)}, u32[]{:S(2)}, u32[]{:S(2)}) collective-permute-start(bf16[384,128]{1,0:T(8,128)(2,1)S(1)} %bitcast.94), channel_id=1, source_target_pairs={{0,64},{32,96},{64,0},{96,32},{1,65},{33,97},{65,1},{97,33},{2,66}... | collective-permute-start | bytes 294920 | tf_op jit(solution)/shard_map/plane_q/ppermute | solution.py:324
  41.3 6.4 %collective-permute-start.4 = (bf16[384,128]{1,0:T(8,128)(2,1)S(1)}, bf16[384,128]{1,0:T(8,128)(2,1)S(1)}, u32[]{:S(2)}, u32[]{:S(2)}) collective-permute-start(bf16[384,128]{1,0:T(8,128)(2,1)S(1)} %bitcast.95), channel_id=1, source_target_pairs={{0,96},{32,64},{64,32},{96,0},{1,97},{33,65},{65,33},{97,1},{2,98}... | collective-permute-start | bytes 294920 | tf_op jit(solution)/shard_map/plane_q/ppermute | solution.py:324
  41.8 56.5 %collective-permute-start.10 = (bf16[3072,128]{1,0:T(8,128)(2,1)S(1)}, bf16[3072,128]{1,0:T(8,128)(2,1)S(1)}, u32[]{:S(2)}, u32[]{:S(2)}) collective-permute-start(bf16[3072,128]{1,0:T(8,128)(2,1)S(1)} %bitcast.77), channel_id=1, source_target_pairs={{0,96},{32,0},{64,32},{96,64},{1,97},{33,1},{65,33},{97,65},{2,98}... | collective-permute-start | bytes 2359304 | tf_op jit(solution)/shard_map/ring_x/ppermute | solution.py:319
  44.6 53.7 %collective-permute-start.9 = (bf16[3072,128]{1,0:T(8,128)(2,1)S(1)}, bf16[3072,128]{1,0:T(8,128)(2,1)S(1)}, u32[]{:S(2)}, u32[]{:S(2)}) collective-permute-start(bf16[3072,128]{1,0:T(8,128)(2,1)S(1)} %bitcast.78), channel_id=1, source_target_pairs={{0,32},{32,64},{64,96},{96,0},{1,33},{33,65},{65,97},{97,1},{2,34}... | collective-permute-start | bytes 2359304 | tf_op jit(solution)/shard_map/ring_x/ppermute | solution.py:319
  44.6 3.3 %collective-permute-start.1 = (bf16[1536,128]{1,0:T(8,128)(2,1)S(1)}, bf16[1536,128]{1,0:T(8,128)(2,1)S(1)}, u32[]{:S(2)}, u32[]{:S(2)}) collective-permute-start(bf16[1536,128]{1,0:T(8,128)(2,1)S(1)} %bitcast.90), channel_id=1, source_target_pairs={{0,1},{1,0},{2,3},{3,2},{4,5},{5,4},{6,7},{7,6},{8,9},{9,8},{10,11... | collective-permute-start | bytes 1179656 | tf_op jit(solution)/shard_map/swap_q/ppermute | solution.py:329
  45.8 19.6 %collective-permute-start.6 = (bf16[768,128]{1,0:T(8,128)(2,1)S(1)}, bf16[768,128]{1,0:T(8,128)(2,1)S(1)}, u32[]{:S(2)}, u32[]{:S(2)}) collective-permute-start(bf16[768,128]{1,0:T(8,128)(2,1)S(1)} %bitcast.86), channel_id=1, source_target_pairs={{0,16},{8,24},{16,0},{24,8},{1,17},{9,25},{17,1},{25,9},{2,18},{10... | collective-permute-start | bytes 589832 | tf_op jit(solution)/shard_map/plane_z/ppermute | solution.py:324
  47.7 2.0 %collective-permute-start.5 = (bf16[1536,128]{1,0:T(8,128)(2,1)S(1)}, bf16[1536,128]{1,0:T(8,128)(2,1)S(1)}, u32[]{:S(2)}, u32[]{:S(2)}) collective-permute-start(bf16[1536,128]{1,0:T(8,128)(2,1)S(1)} %pad_maximum_fusion.4), channel_id=1, source_target_pairs={{0,1},{1,0},{2,3},{3,2},{4,5},{5,4},{6,7},{7,6},{8,9},{9,8},{10,11... | collective-permute-start | bytes 1179656 | tf_op jit(solution)/shard_map/swap_plane_q/ppermute | solution.py:329
  47.9 17.5 %collective-permute-start.7 = (bf16[768,128]{1,0:T(8,128)(2,1)S(1)}, bf16[768,128]{1,0:T(8,128)(2,1)S(1)}, u32[]{:S(2)}, u32[]{:S(2)}) collective-permute-start(bf16[768,128]{1,0:T(8,128)(2,1)S(1)} %bitcast.87), channel_id=1, source_target_pairs={{0,24},{8,16},{16,8},{24,0},{1,25},{9,17},{17,9},{25,1},{2,26},{10... | collective-permute-start | bytes 589832 | tf_op jit(solution)/shard_map/plane_z/ppermute | solution.py:324
  49.8 15.7 %collective-permute-start.8 = (bf16[768,128]{1,0:T(8,128)(2,1)S(1)}, bf16[768,128]{1,0:T(8,128)(2,1)S(1)}, u32[]{:S(2)}, u32[]{:S(2)}) collective-permute-start(bf16[768,128]{1,0:T(8,128)(2,1)S(1)} %bitcast.88), channel_id=1, source_target_pairs={{0,8},{8,0},{16,24},{24,16},{1,9},{9,1},{17,25},{25,17},{2,10},{10... | collective-permute-start | bytes 589832 | tf_op jit(solution)/shard_map/plane_z/ppermute | solution.py:324
  98.4 3.7 %collective-permute-start.13 = (f32[2,144,768]{2,1,0:T(8,128)S(1)}, f32[2,144,768]{2,1,0:T(8,128)S(1)}, u32[]{:S(2)}, u32[]{:S(2)}) collective-permute-start(f32[2,144,768]{2,1,0:T(8,128)S(1)} %slice.101), channel_id=1, source_target_pairs={{0,1},{1,0},{2,3},{3,2},{4,5},{5,4},{6,7},{7,6},{8,9},{9,8},{10,11... | collective-permute-start | bytes 2654216 | tf_op jit(solution)/shard_map/swap_b/ppermute | solution.py:329
  98.5 39.0 %collective-permute-start.11 = (bf16[1536,128]{1,0:T(8,128)(2,1)S(1)}, bf16[1536,128]{1,0:T(8,128)(2,1)S(1)}, u32[]{:S(2)}, u32[]{:S(2)}) collective-permute-start(bf16[1536,128]{1,0:T(8,128)(2,1)S(1)} %slice.99), channel_id=1, source_target_pairs={{0,32},{32,64},{64,96},{96,0},{1,33},{33,65},{65,97},{97,1},{2,34}... | collective-permute-start | bytes 1179656 | tf_op jit(solution)/shard_map/ring_x_far/ppermute | solution.py:319
  99.4 38.2 %collective-permute-start.12 = (bf16[1536,128]{1,0:T(8,128)(2,1)S(1)}, bf16[1536,128]{1,0:T(8,128)(2,1)S(1)}, u32[]{:S(2)}, u32[]{:S(2)}) collective-permute-start(bf16[1536,128]{1,0:T(8,128)(2,1)S(1)} %slice.100), channel_id=1, source_target_pairs={{0,96},{32,0},{64,32},{96,64},{1,97},{33,1},{65,33},{97,65},{2,98}... | collective-permute-start | bytes 1179656 | tf_op jit(solution)/shard_map/ring_x_far/ppermute | solution.py:319
  102.3 35.0 %collective-permute-start.14 = (bf16[1,144,384]{2,1,0:T(8,128)(2,1)S(1)}, bf16[1,144,384]{2,1,0:T(8,128)(2,1)S(1)}, u32[]{:S(2)}, u32[]{:S(2)}) collective-permute-start(bf16[1,144,384]{2,1,0:T(8,128)(2,1)S(1)} %get-tuple-element.72), channel_id=1, source_target_pairs={{0,32},{32,0},{64,96},{96,64},{1,33},{33,1},{65,97},{97,65},{2,34}... | collective-permute-start | bytes 331784 | tf_op jit(solution)/shard_map/plane_sum/ppermute | solution.py:324
  102.4 34.9 %collective-permute-start.15 = (bf16[1,144,384]{2,1,0:T(8,128)(2,1)S(1)}, bf16[1,144,384]{2,1,0:T(8,128)(2,1)S(1)}, u32[]{:S(2)}, u32[]{:S(2)}) collective-permute-start(bf16[1,144,384]{2,1,0:T(8,128)(2,1)S(1)} %get-tuple-element.73), channel_id=1, source_target_pairs={{0,64},{32,96},{64,0},{96,32},{1,65},{33,97},{65,1},{97,33},{2,66}... | collective-permute-start | bytes 331784 | tf_op jit(solution)/shard_map/plane_sum/ppermute | solution.py:324
  104.8 32.5 %collective-permute-start.16 = (bf16[1,144,384]{2,1,0:T(8,128)(2,1)S(1)}, bf16[1,144,384]{2,1,0:T(8,128)(2,1)S(1)}, u32[]{:S(2)}, u32[]{:S(2)}) collective-permute-start(bf16[1,144,384]{2,1,0:T(8,128)(2,1)S(1)} %get-tuple-element.74), channel_id=1, source_target_pairs={{0,96},{32,64},{64,32},{96,0},{1,97},{33,65},{65,33},{97,1},{2,98}... | collective-permute-start | bytes 331784 | tf_op jit(solution)/shard_map/plane_sum/ppermute | solution.py:324
  146.1 8.2 %collective-permute-start.17 = (f32[1,144,1536]{2,1,0:T(8,128)}, f32[1,144,1536]{2,1,0:T(8,128)}, u32[]{:S(2)}, u32[]{:S(2)}) collective-permute-start(f32[1,144,1536]{2,1,0:T(8,128)} %get-tuple-element.83), channel_id=1, source_target_pairs={{0,1},{1,0},{2,3},{3,2},{4,5},{5,4},{6,7},{7,6},{8,9},{9,8},{10,11... | collective-permute-start | bytes 2654216 | tf_op jit(solution)/shard_map/swap_a/ppermute | solution.py:329
  154.2 18.0 %slice-start = ((s8[6553600]{0:T(1024)(128)(4,1)}), s8[4194304]{0:T(1024)(128)(4,1)S(1)}, s32[]{:S(2)}) async-start(s8[6553600]{0:T(1024)(128)(4,1)} %bitcast.75), calls=%async_computation.2 | async-start | bytes 8388608
  175.7 7.6 %collective-permute-start.18 = (bf16[48,2560]{1,0:T(8,128)(2,1)S(1)}, bf16[48,2560]{1,0:T(8,128)(2,1)S(1)}, u32[]{:S(2)}, u32[]{:S(2)}) collective-permute-start(bf16[48,2560]{1,0:T(8,128)(2,1)S(1)} %get-tuple-element.90), channel_id=1, source_target_pairs={{0,6},{2,0},{4,2},{6,4},{1,7},{3,1},{5,3},{7,5},{8,14},{10,8},{12,... | collective-permute-start | bytes 737288 | tf_op jit(solution)/shard_map/sum_y/ppermute | solution.py:319
  175.8 8.5 %collective-permute-start.19 = (bf16[48,2560]{1,0:T(8,128)(2,1)S(1)}, bf16[48,2560]{1,0:T(8,128)(2,1)S(1)}, u32[]{:S(2)}, u32[]{:S(2)}) collective-permute-start(bf16[48,2560]{1,0:T(8,128)(2,1)S(1)} %get-tuple-element.91), channel_id=1, source_target_pairs={{0,2},{2,4},{4,6},{6,0},{1,3},{3,5},{5,7},{7,1},{8,10},{10,12},{12... | collective-permute-start | bytes 737288 | tf_op jit(solution)/shard_map/sum_y/ppermute | solution.py:319
  181.2 7.1 %collective-permute-start.20 = (bf16[48,2560]{1,0:T(8,128)(2,1)S(1)}, bf16[48,2560]{1,0:T(8,128)(2,1)S(1)}, u32[]{:S(2)}, u32[]{:S(2)}) collective-permute-start(bf16[48,2560]{1,0:T(8,128)(2,1)S(1)} %get-tuple-element.93), channel_id=1, source_target_pairs={{0,6},{2,0},{4,2},{6,4},{1,7},{3,1},{5,3},{7,5},{8,14},{10,8},{12,... | collective-permute-start | bytes 737288 | tf_op jit(solution)/shard_map/sum_y/ppermute | solution.py:319
  182.6 7.9 %collective-permute-start.21 = (bf16[48,2560]{1,0:T(8,128)(2,1)S(1)}, bf16[48,2560]{1,0:T(8,128)(2,1)S(1)}, u32[]{:S(2)}, u32[]{:S(2)}) collective-permute-start(bf16[48,2560]{1,0:T(8,128)(2,1)S(1)} %get-tuple-element.94), channel_id=1, source_target_pairs={{0,2},{2,4},{4,6},{6,0},{1,3},{3,5},{5,7},{7,1},{8,10},{10,12},{12... | collective-permute-start | bytes 737288 | tf_op jit(solution)/shard_map/sum_y/ppermute | solution.py:319
  (5 other events, 54.2 us)
